TPU v7x, 128 devices: a whole 4x4x4 slice. The times are simulated.
128 devices in a mesh: tok: 4 (over y_lo, core), tp: 32 (over x, z, y_hi).
Axes of the slice: x: 4, y: 4 (y_hi: 2, y_lo: 2; y = y_hi * 2 + y_lo), z: 4, core: 2. Of those that a mesh axis runs over, the one named last changes fastest.
Arguments:
- residual: bfloat16 [1024, 16384], P('tok', 'tp')
- norm_gain: float32 [16384], replicated, may hold values from 0.5 to 1.5
- weight: bfloat16 [30720, 16384], P(('tok', 'tp')), may hold values from -6 to 6
- scale_codes: int32 [30720, 2], P(('tok', 'tp')), may hold values from 0 to 7
- zero_points: int32 [30720, 2], P(('tok', 'tp')), may hold values from 4 to 11
- panels: bfloat16 [256, 16384], P(None, ('tok', 'tp')), as said below
Outputs:
- gram: float32 [16384, 16384], P('tok', 'tp')
- quantized: bfloat16 [30720, 16384], P('tok', 'tp')
Inputs may be any that keep to these rules, and one draw needn't show every extreme that they name: Row j of panels is row j of an upper-triangular factor: entries left of column j are zero and panels[j, j] lies in [0.5, 1.5].
All inputs are finite; a program needn't handle non-finite values.
Results may differ from a plain program's by a relative error of at most 0.0085.
Values may be sent and summed in bfloat16 or wider, within the bound.
No kernel may reach another device: no remote copies, remote signals or barrier semaphores. Data moves between devices by JAX's collectives and lax.ppermute only.
A program may use at most 192 MiB of HBM per device.

v0:
```python
import math

import jax
import jax.numpy as jnp
from jax import lax
from jax.sharding import PartitionSpec as P

BLOCK = 128
BLOCKS = 2


EPS = 1e-05
SOFTNESS = 0.9
FULL_TURN = 2.0 * math.pi
HIGHEST = lax.Precision.HIGHEST


def spread(x, axis, root):
    mine = lax.axis_index(axis) == root
    return lax.psum(jnp.where(mine, x, jnp.zeros_like(x)), axis)


def dequantize(column, scale_row, zero_row):
    shifted = column / scale_row + zero_row
    softened = shifted - SOFTNESS * jnp.sin(FULL_TURN * shifted) / FULL_TURN
    return scale_row * (jnp.clip(softened, 0.0, 15.0) - zero_row)


def block_errors(block_cols, diagonal, scale_row, zero_row):
    row_count = block_cols.shape[0]
    block_width = block_cols.shape[1]
    lane_ids = lax.iota(jnp.int32, 8)
    wide_ids = lax.iota(jnp.int32, block_width)

    def sub_step(step_index, carried):
        block_now, errors = carried
        sub_first = step_index * 8
        sub_cols = lax.dynamic_slice_in_dim(block_now, sub_first, 8, 1)
        sub_panel = lax.dynamic_slice_in_dim(diagonal, sub_first, 8, 0)
        local_pivots = lax.dynamic_slice_in_dim(sub_panel, sub_first, 8, 1)
        collected = []
        for i in range(8):
            column_now = sub_cols[:, i]
            restored = dequantize(column_now, scale_row, zero_row)
            error_now = (column_now - restored) / local_pivots[i, i]
            sub_cols = (
                sub_cols
                - error_now[:, None] * jnp.where(lane_ids > i, local_pivots[i], 0.0)[None, :]
            )
            sub_cols = jnp.where((lane_ids == i)[None, :], restored[:, None], sub_cols)
            collected.append(error_now)
        sub_errors = jnp.stack(collected, axis=1)
        spill_over = jnp.dot(sub_errors, sub_panel, precision=HIGHEST)
        block_now = jnp.where(
            (wide_ids >= sub_first + 8)[None, :], block_now - spill_over, block_now
        )
        block_now = lax.dynamic_update_slice_in_dim(block_now, sub_cols, sub_first, 1)
        errors = lax.dynamic_update_slice_in_dim(errors, sub_errors, sub_first, 1)
        return (block_now, errors)

    start_state = (block_cols, jnp.zeros((row_count, block_width), jnp.float32))
    return lax.fori_loop(0, block_width // 8, sub_step, start_state)


def on_device(residual, norm_gain, weight, scale_codes, zero_points, panels):
    tok_local, feat_local = residual.shape
    tp_count = lax.axis_size("tp")
    tok_count = lax.axis_size("tok")
    feat_total = feat_local * tp_count
    tp_place = lax.axis_index("tp")
    local_rows = residual.astype(jnp.float32)
    row_sums = lax.psum(jnp.sum(local_rows * local_rows, axis=1), "tp")
    gain_own = lax.dynamic_slice_in_dim(norm_gain, tp_place * feat_local, feat_local, 0)
    x_own = (
        local_rows * lax.rsqrt(row_sums[:, None] / feat_total + EPS) * gain_own[None, :]
    ).astype(jnp.bfloat16)
    x_full = lax.all_gather(x_own, "tp", axis=1, tiled=True)
    gram_sum = lax.psum_scatter(
        lax.dot_general(
            x_full, x_own, (((0,), (0,)), ((), ())), preferred_element_type=jnp.float32
        ).astype(jnp.bfloat16),
        "tok",
        scatter_dimension=0,
        tiled=True,
    ).astype(jnp.float32)
    gram = gram_sum / (tok_local * tok_count)
    shard_cols = panels.shape[1]
    working = weight.astype(jnp.float32)
    column = lax.iota(jnp.int32, feat_total)
    for k in range(BLOCKS):
        block_start = k * BLOCK
        scale_row = jnp.exp2(scale_codes[:, k].astype(jnp.float32) * 0.5 - 3.0)
        zero_row = zero_points[:, k].astype(jnp.float32)
        root_index = block_start // shard_cols
        offset_cols = block_start - root_index * shard_cols
        own_block = panels[block_start : block_start + BLOCK, offset_cols : offset_cols + BLOCK]
        diagonal = spread(own_block, ("tok", "tp"), root_index).astype(jnp.float32)
        block_cols, errors = block_errors(
            working[:, block_start : block_start + BLOCK], diagonal, scale_row, zero_row
        )
        correction = jnp.dot(
            errors,
            lax.all_gather(
                panels[block_start : block_start + BLOCK], ("tok", "tp"), axis=1, tiled=True
            ).astype(jnp.float32),
            precision=HIGHEST,
        )
        working = jnp.where((column >= block_start + BLOCK)[None, :], working - correction, working)
        working = lax.dynamic_update_slice_in_dim(working, block_cols, block_start, 1)
    quantized = lax.all_to_all(
        working.astype(jnp.bfloat16), "tp", split_axis=1, concat_axis=0, tiled=True
    )
    return (gram, quantized)


def solution(mesh):
    in_specs = (
        P("tok", "tp"),
        P(),
        P(("tok", "tp"), None),
        P(("tok", "tp"), None),
        P(("tok", "tp"), None),
        P(None, ("tok", "tp")),
    )
    out_specs = (P("tok", "tp"), P("tok", "tp"))
    return jax.shard_map(
        on_device, mesh=mesh, in_specs=in_specs, out_specs=out_specs, check_vma=False
    )
```

profile of v0, /device:TPU:1, one launch (start us, length us, event | category | flops | bytes accessed | tf_op | source)
XLA Modules:
  0.0 1028.7 jit_solution(8658582831721151502)
XLA Ops:
  7.2 1.4 fusion.67
  10.2 1.1 fusion.62
  11.3 84.6 %psum.21 = f32[256]{0:T(256)S(1)} all-reduce(f32[256]{0:T(256)S(1)} %fusion.62), channel_id=1, replica_groups=mesh['tok'=4,'tp'=32] {'tp'}, use_global_device_ids=true, to_apply=%region_1.0 | all-reduce | flops 256 | bytes 2048 | tf_op jit(solution)/shard_map/psum | solution.py:72
  95.9 1.8 fusion.64
  100.9 54.0 %all-reduce.3.cloned.1.call-done = (bf16[128,128]{1,0:T(8,128)(2,1)}, bf16[128,128]{1,0:T(8,128)(2,1)}) async-done(((bf16[128,128]{1,0:T(8,128)(2,1)}, bf16[128,128]{1,0:T(8,128)(2,1)}), (bf16[128,128]{1,0:T(8,128)(2,1)}, bf16[128,128]{1,0:T(8,128)(2,1)})) %all-reduce.3.cloned.1.call-update) | async-done | bytes 65552 | tf_op jit(solution)/shard_map/psum | solution.py:20
  155.7 142.4 %while.40 = (s32[]{:T(128)}, f32[240,128]{0,1:T(8,128)S(1)}, f32[240,128]{0,1:T(8,128)S(1)}, f32[240]{0:T(256)S(1)}, f32[240]{0:T(256)S(1)}, /*index=5*/f32[128,...) while((s32[]{:T(128)}, f32[240,128]{0,1:T(8,128)S(1)}, ...), condition=%wide.region_5.6_spmd.clone.clone, body=%wide.region_4.5_spmd.clone.clone.sunk | while | flops 3237448 | bytes 1045935 | solution.py:62
  172.3 0.9 dynamic_update_slice.69
  181.2 0.9 dynamic_update_slice.69
  190.1 0.9 dynamic_update_slice.69
  199.0 0.9 dynamic_update_slice.69
  207.9 0.9 dynamic_update_slice.69
  216.9 0.9 dynamic_update_slice.69
  225.8 0.9 dynamic_update_slice.69
  234.7 0.9 dynamic_update_slice.69
  243.6 0.9 dynamic_update_slice.69
  252.5 0.9 dynamic_update_slice.69
  261.4 0.9 dynamic_update_slice.69
  270.4 0.9 dynamic_update_slice.69
  288.2 0.9 dynamic_update_slice.69
  298.2 116.9 %all-gather.6.cloned.1.call-done = bf16[128,16384]{1,0:T(8,128)(2,1)} async-done(((bf16[128,128]{1,0:T(8,128)(2,1)}), bf16[128,16384]{1,0:T(8,128)(2,1)}) %all-gather.6.cloned.1.call-update) | async-done | bytes 4194320 | tf_op jit(solution)/shard_map/all_gather | solution.py:103
  415.2 10.4 %subtract_select_fusion.17 = f32[240,16384]{1,0:T(8,128)S(1)} fusion(f32[240,128]{0,1:T(8,128)S(1)} %get-tuple-element.574, bf16[128,16384]{1,0:T(8,128)(2,1)} %all-gather.6.cloned.1.call-done, pred[16384]{0:T(1024)(128)(4,1)S(1)} %iota_compare_fusion.34, bf16[240,16384]{1,0:T(8,128)(2,1)} %param.12), kind=kOutput, calls=%fused_computation.148 | convolution fusion | flops 6051594240 | bytes 27926528 | tf_op jit(solution)/shard_map/dot_general | solution.py:101
  425.6 5.5 copy-done
  431.2 85.8 %all-gather.4.cloned.1.call-done = bf16[256,16384]{1,0:T(8,128)(2,1)} async-done(((bf16[256,512]{1,0:T(8,128)(2,1)}), bf16[256,16384]{1,0:T(8,128)(2,1)}) %all-gather.4.cloned.1.call-update) | async-done | bytes 8388624 | tf_op jit(solution)/shard_map/all_gather | solution.py:77
  517.0 11.7 %convolution_convert_fusion = bf16[16384,512]{1,0:T(8,128)(2,1)} fusion(bf16[256,16384]{1,0:T(8,128)(2,1)} %all-gather.4.cloned.1.call-done, bf16[256,512]{1,0:T(8,128)(2,1)S(1)} %copy-done.2), kind=kOutput, calls=%fused_computation.146 | convolution fusion | flops 4303355904 | bytes 25427968 | tf_op jit(solution)/shard_map/dot_general | solution.py:79
  528.7 141.3 %while.41 = (s32[]{:T(128)}, f32[240,128]{0,1:T(8,128)S(1)}, f32[240,128]{0,1:T(8,128)S(1)}, f32[240]{0:T(256)S(1)}, f32[240]{0:T(256)S(1)}, /*index=5*/f32[128,...) while((s32[]{:T(128)}, f32[240,128]{0,1:T(8,128)S(1)}, ...), condition=%wide.region_8.9_spmd.clone.clone, body=%wide.region_7.8_spmd.clone.clone.sunk | while | flops 3237448 | bytes 1045935 | solution.py:62
  670.1 108.6 %all-gather.8.cloned.1.call-done = bf16[128,16384]{1,0:T(8,128)(2,1)} async-done(((bf16[128,128]{1,0:T(8,128)(2,1)}), bf16[128,16384]{1,0:T(8,128)(2,1)}) %all-gather.8.cloned.1.call-update) | async-done | bytes 4194320 | tf_op jit(solution)/shard_map/all_gather | solution.py:103
  778.8 12.6 %subtract_select_fusion.16 = bf16[240,16384]{1,0:T(8,128)(2,1)S(1)} fusion(f32[240,16384]{1,0:T(8,128)} %copy-done, f32[240,128]{0,1:T(8,128)S(1)} %get-tuple-element.576, bf16[128,16384]{1,0:T(8,128)(2,1)} %all-gather.8.cloned.1.call-done, pred[16384]{0:T(1024)(128)(4,1)S(1)} %iota_compare_fusion.35), kind=kOutput, calls=%fused_computation.147 | convolution fusion | flops 6047662080 | bytes 27926528 | tf_op jit(solution)/shard_map/dot_general | solution.py:101
  791.4 4.1 copy.170
  795.5 117.0 %all_to_all.19 = bf16[240,32,512]{2,0,1:T(8,128)(2,1)} all-to-all(bf16[240,32,512]{2,0,1:T(8,128)(2,1)} %bitcast.317), channel_id=1, replica_groups=mesh['tok'=4,'tp'=32] {'tp'}, dimensions={1} | all-to-all | bytes 15728640 | tf_op jit(solution)/shard_map/all_to_all | solution.py:110
  912.5 99.5 %reduce-scatter.2.cloned.1.call-done = bf16[4096,512]{1,0:T(8,128)(2,1)} async-done(((bf16[16384,512]{1,0:T(8,128)(2,1)}), bf16[4096,512]{1,0:T(8,128)(2,1)}) %reduce-scatter.2.cloned.1.call-update) | async-done | bytes 4194320 | tf_op jit(solution)/shard_map/reduce_scatter | solution.py:78
  1012.0 6.9 convert_multiply_fusion
  1019.0 3.2 copy.210
  (1142 shorter events, 272.3 us)
Async XLA Ops:
  7.2 147.7 %all-reduce.3.cloned.1.call-start = ((), (), s32[]{:S(2)}) async-start(), calls=%async_computation.6 | async-start | bytes 131072 | tf_op jit(solution)/shard_map/psum | solution.py:20
  8.7 406.5 %all-gather.6.cloned.1.call-start = ((), (), s32[]{:S(2)}) async-start(), calls=%async_computation.4 | async-start | bytes 4227072 | tf_op jit(solution)/shard_map/all_gather | solution.py:103
  9.4 507.6 %all-gather.4.cloned.1.call-start = ((), (), s32[]{:S(2)}) async-start(), calls=%async_computation.2 | async-start | bytes 8650752 | tf_op jit(solution)/shard_map/all_gather | solution.py:77
  97.8 681.0 %all-gather.8.cloned.1.call-start = ((), (), s32[]{:S(2)}) async-start(), calls=%async_computation.5 | async-start | bytes 4227072 | tf_op jit(solution)/shard_map/all_gather | solution.py:103
  98.3 913.7 %reduce-scatter.2.cloned.1.call-start = ((), (), s32[]{:S(2)}) async-start(), calls=%async_computation.3 | async-start | bytes 20971520 | tf_op jit(solution)/shard_map/reduce_scatter | solution.py:78
  154.9 143.3 %copy-start.3 = (bf16[128,128]{1,0:T(8,128)(2,1)S(1)}, bf16[128,128]{1,0:T(8,128)(2,1)}, u32[]{:S(2)}) copy-start(bf16[128,128]{1,0:T(8,128)(2,1)} %get-tuple-element.725) | copy-start | bytes 98308
  415.2 101.9 %copy-start.2 = (bf16[256,512]{1,0:T(8,128)(2,1)S(1)}, bf16[256,512]{1,0:T(8,128)(2,1)}, u32[]{:S(2)}) copy-start(bf16[256,512]{1,0:T(8,128)(2,1)} %fusion.64) | copy-start | bytes 786436
  425.6 5.5 copy-start
  1012.0 6.9 copy-start.1
Sparse Core Ops, SparseCore 0:
  13.0 141.8 all-reduce.2
  156.6 258.5 all-gather.5
  418.9 98.0 all-gather.3
  519.2 259.5 all-gather.7
  781.2 230.7 reduce-scatter.1
where the time goes:
time: 1050 us; the launch traced here: 1030 us
  waiting for transfers between devices  466 us (44%)
  other arithmetic  216 us (21%)
  blocking collectives  202 us (19%)
  local copies, waits for them, and re-layouts  77.7 us (7%)
  matrix products  47 us (4%)
  between operations  13.9 us (1%)
    all_gather x2, waiting for transfers between devices, on_device(): lax.all_gather(panels[block_start:block_start + BLOCK], ('tok', 'tp'), ax...  226 us
    div x256, other arithmetic, sub_step(): error_now = (column_now - restored) / local_pivots[i, i]  178 us
    all_to_all x1, blocking collectives, on_device(): lax.all_to_all(working.astype(jnp.bfloat16), 'tp', split_axis=1, concat_a...  117 us
    reduce_scatter x1, waiting for transfers between devices, on_device(): lax.psum_scatter(lax.dot_general(x_full, x_own, (((0,), (0,)), ((), ())),...  99.5 us
    all_gather x1, waiting for transfers between devices, on_device(): x_full = lax.all_gather(x_own, 'tp', axis=1, tiled=True)  85.8 us
    psum x1, blocking collectives, on_device(): row_sums = lax.psum(jnp.sum(local_rows * local_rows, axis=1), 'tp')  84.6 us
    psum x1, waiting for transfers between devices, spread(): return lax.psum(jnp.where(mine, x, jnp.zeros_like(x)), axis)  54 us
    dynamic_update_slice x32, local copies, waits for them, and re-layouts, sub_step(): lax.dynamic_update_slice_in_dim(block_now, sub_cols, sub_first, 1)  27.5 us
  transfers between devices with their start and end apart: 5, of which 5 were waited for; matrix products, arithmetic and copies ran while one was open for 31% of the time, Pallas kernels for 0%

commit v1 on v0

v1 whole, which is shorter than its diff:
```python
import functools
import math

import jax
import jax.numpy as jnp
from jax import lax
from jax.experimental import pallas as pl
from jax.experimental.pallas import tpu as pltpu
from jax.sharding import PartitionSpec as P

BLOCK = 128
BLOCKS = 2
COLS = BLOCK * BLOCKS
SUB = 8

EPS = 1e-05
SOFTNESS = 0.9
ALL = ("tok", "tp")

SINE = tuple(
    c * SOFTNESS / (2.0 * math.pi)
    for c in (
        6.283182818496983,
        -41.341421393740156,
        81.59618374823393,
        -76.58009925759313,
        41.20538928368347,
        -12.271253496065944,
    )
)


def tp_index(x, z, h):
    return x * 8 + z * 2 + h


def index(t, x, z, h):
    return t * 32 + tp_index(x, z, h)


PLACES = [(t, x, z, h) for t in range(4) for x in range(4) for z in range(4) for h in range(2)]


def moves(fn):
    return [(index(*a), index(*fn(*a))) for a in PLACES]


def split3(v):
    hi = v.astype(jnp.bfloat16).astype(jnp.float32)
    rest = v - hi
    mid = rest.astype(jnp.bfloat16).astype(jnp.float32)
    return hi, mid, rest - mid


def contract_rows(a, b):
    return lax.dot_general(a, b, (((0,), (0,)), ((), ())), preferred_element_type=jnp.float32)


def errors_kernel(w_ref, codes_ref, zeros_ref, p_ref, e_ref, work, diag, panel, errs):
    rows = w_ref.shape[0]
    lanes = work.shape[1]
    w = w_ref[...].astype(jnp.float32)
    w = jnp.concatenate([w, jnp.zeros((lanes - rows, COLS), jnp.float32)], axis=0)
    work[...] = w.T
    panel[...] = p_ref[...].astype(jnp.float32)
    across = panel[...].T
    row_id = lax.broadcasted_iota(jnp.int32, (COLS, COLS), 0)
    col_id = lax.broadcasted_iota(jnp.int32, (COLS, COLS), 1)
    pivots = jnp.sum(jnp.where(row_id == col_id, across, 0.0), axis=1, keepdims=True)
    diag[:, SUB : SUB + 1] = 1.0 / pivots
    for g in range(COLS // SUB):
        diag[g * SUB : (g + 1) * SUB, :SUB] = across[g * SUB : (g + 1) * SUB, g * SUB : (g + 1) * SUB]
    sub_id = lax.broadcasted_iota(jnp.int32, (SUB, lanes), 0)
    for k in range(BLOCKS):
        first = k * BLOCK
        half = codes_ref[k : k + 1, :] * 0.5 - 3.0
        scale = jnp.broadcast_to(jnp.exp2(half), (SUB, lanes))
        inverse = jnp.broadcast_to(jnp.exp2(-half), (SUB, lanes))
        zero = jnp.broadcast_to(zeros_ref[k : k + 1, :], (SUB, lanes))

        def group(g, carry):
            base = pl.multiple_of(first + g * SUB, SUB)
            now = work[pl.ds(base, SUB), :]
            local = diag[pl.ds(base, SUB), :]
            inv_pivot = jnp.broadcast_to(local[:, SUB : SUB + 1], (SUB, lanes))
            found = jnp.zeros((SUB, lanes), jnp.float32)
            for i in range(SUB):
                u = now * inverse + zero
                r = u - jnp.round(u)
                r2 = r * r
                r4 = r2 * r2
                wave = (SINE[0] + SINE[1] * r2) + r4 * (
                    (SINE[2] + SINE[3] * r2) + r4 * (SINE[4] + SINE[5] * r2)
                )
                soft = jnp.clip(u - wave * r, 0.0, 15.0)
                error = (now - scale * (soft - zero)) * inv_pivot
                error = jnp.broadcast_to(error[i : i + 1, :], (SUB, lanes))
                now = now - jnp.broadcast_to(local[:, i : i + 1], (SUB, lanes)) * error
                found = jnp.where(sub_id == i, error, found)
            errs[pl.ds(base, SUB), :] = found
            p_rows = panel[pl.ds(base, SUB), first : first + BLOCK]
            p_rows = jnp.concatenate([p_rows] * 3, axis=0).astype(jnp.bfloat16)
            e_rows = jnp.concatenate(split3(found), axis=0).astype(jnp.bfloat16)
            work[first : first + BLOCK, :] -= contract_rows(p_rows, e_rows)
            return carry

        lax.fori_loop(0, BLOCK // SUB, group, 0)
        if k + 1 < BLOCKS:
            p_rows = panel[first : first + BLOCK, first + BLOCK :].astype(jnp.bfloat16)
            spill = 0.0
            for part in split3(errs[first : first + BLOCK, :]):
                spill = spill + contract_rows(p_rows, part.astype(jnp.bfloat16))
            work[first + BLOCK :, :] -= spill
    e_ref[...] = errs[...].T[:rows].astype(jnp.bfloat16)


def block_errors(weight, codes, zeros, first_panel):
    rows = weight.shape[0]
    lanes = -(-rows // 128) * 128
    return pl.pallas_call(
        errors_kernel,
        grid=(1,),
        out_shape=jax.ShapeDtypeStruct((rows, COLS), jnp.bfloat16),
        in_specs=[
            pl.BlockSpec((rows, COLS), lambda i: (0, 0)),
            pl.BlockSpec((BLOCKS, lanes), lambda i: (0, 0)),
            pl.BlockSpec((BLOCKS, lanes), lambda i: (0, 0)),
            pl.BlockSpec((COLS, COLS), lambda i: (0, 0)),
        ],
        out_specs=pl.BlockSpec((rows, COLS), lambda i: (0, 0)),
        scratch_shapes=[
            pltpu.VMEM((COLS, lanes), jnp.float32),
            pltpu.VMEM((COLS, 128), jnp.float32),
            pltpu.VMEM((COLS, COLS), jnp.float32),
            pltpu.VMEM((COLS, lanes), jnp.float32),
        ],
        compiler_params=pltpu.CompilerParams(vmem_limit_bytes=16 * 2**20),
        cost_estimate=pl.CostEstimate(flops=10**7, bytes_accessed=10**6, transcendentals=0),
        name="errors",
    )(weight, codes, zeros, first_panel)


def gram_kernel(total, rows_ref, own_ref, inv_ref, gain_rows_ref, gain_own_ref, out_ref, own):
    @pl.when(pl.program_id(0) == 0)
    def _():
        for g in range(own_ref.shape[0]):
            v = own_ref[g].astype(jnp.float32) * inv_ref[g] * gain_own_ref[...]
            own[g] = v.astype(jnp.bfloat16)

    acc = 0.0
    for g in range(own_ref.shape[0]):
        v = rows_ref[g, 0].astype(jnp.float32) * inv_ref[g] * gain_rows_ref[0]
        acc = acc + contract_rows(v.astype(jnp.bfloat16), own[g])
    out_ref[...] = acc * (1.0 / total)


def mean_outer(quarter, own, inv_norm, gain_rows, gain_own):
    groups, pieces, toks, feats = quarter.shape
    return pl.pallas_call(
        functools.partial(gram_kernel, groups * toks),
        grid=(pieces,),
        out_shape=jax.ShapeDtypeStruct((pieces * feats, feats), jnp.float32),
        in_specs=[
            pl.BlockSpec((groups, 1, toks, feats), lambda i: (0, i, 0, 0)),
            pl.BlockSpec((groups, toks, feats), lambda i: (0, 0, 0)),
            pl.BlockSpec((groups, toks, 1), lambda i: (0, 0, 0)),
            pl.BlockSpec((1, 1, feats), lambda i: (i, 0, 0)),
            pl.BlockSpec((1, feats), lambda i: (0, 0)),
        ],
        out_specs=pl.BlockSpec((feats, feats), lambda i: (i, 0)),
        scratch_shapes=[pltpu.VMEM((groups, toks, feats), jnp.bfloat16)],
        compiler_params=pltpu.CompilerParams(vmem_limit_bytes=32 * 2**20),
        cost_estimate=pl.CostEstimate(
            flops=2 * groups * toks * pieces * feats * feats,
            bytes_accessed=20 * 2**20,
            transcendentals=0,
        ),
        name="mean_outer",
    )(quarter, own, inv_norm, gain_rows.reshape(pieces, 1, feats), gain_own.reshape(1, feats))


def corrected_kernel(w_ref, e_ref, p_ref, out_ref):
    correction = jnp.dot(e_ref[...], p_ref[...], preferred_element_type=jnp.float32)
    out_ref[...] = (w_ref[...].astype(jnp.float32) - correction).astype(jnp.bfloat16)


def corrected(moved, errors, panel):
    rows, feats = moved.shape
    step = rows // 16
    return pl.pallas_call(
        corrected_kernel,
        grid=(rows // step,),
        out_shape=jax.ShapeDtypeStruct((rows, feats), jnp.bfloat16),
        in_specs=[
            pl.BlockSpec((step, feats), lambda i: (i, 0)),
            pl.BlockSpec((step, COLS), lambda i: (i, 0)),
            pl.BlockSpec((COLS, feats), lambda i: (0, 0)),
        ],
        out_specs=pl.BlockSpec((step, feats), lambda i: (i, 0)),
        compiler_params=pltpu.CompilerParams(vmem_limit_bytes=16 * 2**20),
        cost_estimate=pl.CostEstimate(
            flops=2 * rows * feats * COLS, bytes_accessed=20 * 2**20, transcendentals=0
        ),
        name="corrected",
    )(moved, errors, panel)


def first_columns(panels, t, p):
    nothing = jnp.zeros_like(panels)
    held = jnp.concatenate(
        [
            jnp.where((t == 0) & (p == 0), panels, nothing),
            jnp.where((t == 0) & (p == 1), panels, nothing),
        ],
        axis=1,
    )

    def step(held, perms):
        for got in [lax.ppermute(held, ALL, perm) for perm in perms]:
            held = held + got
        return held

    four = range(4)
    held = step(held, [[(index(0, 0, 0, h), index(0, 0, 0, 1 - h)) for h in range(2)]])
    held = step(
        held,
        [[(index(0, 0, 0, h), index(0, x, 0, h)) for h in range(2)] for x in (1, 2, 3)],
    )
    held = step(
        held,
        [
            [(index(0, x, 0, h), index(0, x, z, h)) for x in four for h in range(2)]
            for z in (1, 2, 3)
        ],
    )
    return step(
        held,
        [
            [(index(0, x, z, h), index(t, x, z, h)) for x in four for z in four for h in range(2)]
            for t in (1, 2, 3)
        ],
    )


def own_columns(panels, t):
    def target(k):
        def to(tt, x, z, h):
            i = (z % 2) * 2 + h
            return (i ^ k, tt, x, z // 2)

        return to

    got = jnp.stack([lax.ppermute(panels, ALL, moves(target(k))) for k in range(4)])
    order = [lax.dynamic_index_in_dim(got, t ^ i, 0, keepdims=False) for i in range(4)]
    return jnp.concatenate(order, axis=1)


def on_device(residual, norm_gain, weight, scale_codes, zero_points, panels):
    toks, feats = residual.shape
    rows, feat_total = weight.shape
    t = lax.axis_index("tok")
    p = lax.axis_index("tp")
    shards = lax.axis_size("tp")
    groups = lax.axis_size("tok")
    pieces = shards // groups

    swapped = lax.ppermute(residual, ALL, moves(lambda tt, x, z, h: (x, tt, z, h)))
    quarter = lax.all_gather(swapped, "tp").reshape(groups, pieces, toks, feats)
    own = lax.all_gather(residual, "tok")

    first_panel = first_columns(panels, t, p)
    pad = -(-rows // 128) * 128 - rows
    codes = jnp.pad(scale_codes.astype(jnp.float32).T, ((0, 0), (0, pad)))
    zeros = jnp.pad(zero_points.astype(jnp.float32).T, ((0, 0), (0, pad)))
    errors = block_errors(weight[:, :COLS], codes, zeros, first_panel)
    errors_all = lax.all_gather(errors, "tp", axis=0, tiled=True)
    own_panel = own_columns(panels, t)

    moved = lax.all_to_all(weight, "tp", split_axis=1, concat_axis=0, tiled=True)

    squares = quarter.astype(jnp.float32)
    sums = jnp.sum(squares * squares, axis=(1, 3))
    sums = sums + lax.ppermute(sums, ALL, moves(lambda tt, x, z, h: (tt ^ 1, x, z, h)))
    sums = sums + lax.ppermute(sums, ALL, moves(lambda tt, x, z, h: (tt ^ 2, x, z, h)))
    inv_norm = lax.rsqrt(sums / feat_total + EPS)[:, :, None]
    quarter_feats = feat_total // groups
    gain_rows = lax.dynamic_slice_in_dim(norm_gain, t * quarter_feats, quarter_feats, 0)
    gain_own = lax.dynamic_slice_in_dim(norm_gain, p * feats, feats, 0)
    gram = mean_outer(quarter, own, inv_norm, gain_rows, gain_own)

    return (gram, corrected(moved, errors_all, own_panel))


def solution(mesh):
    in_specs = (
        P("tok", "tp"),
        P(),
        P(("tok", "tp"), None),
        P(("tok", "tp"), None),
        P(("tok", "tp"), None),
        P(None, ("tok", "tp")),
    )
    out_specs = (P("tok", "tp"), P("tok", "tp"))
    return jax.shard_map(
        on_device, mesh=mesh, in_specs=in_specs, out_specs=out_specs, check_vma=False
    )
```

time: 1050 us -> 351 us (0.33); the launches traced: 1030 us -> 349 us
  waiting for transfers between devices: 466 us -> 225 us
  other arithmetic: 216 us -> 7.57 us
  blocking collectives: 202 us -> 0 us
  local copies, waits for them, and re-layouts: 77.7 us -> 17.9 us
  starting transfers between devices: 0.2 us -> 49.1 us
  matrix products: 47 us -> 0 us
  Pallas kernels: 0 us -> 36.3 us
    all_gather x3, waiting for transfers between devices: 311 us -> 101 us  [the longest x1 76 us: on_device(): errors_all = lax.all_gather(errors, 'tp', axis=0, tiled=True)]
    div x257 -> x0, other arithmetic: 185 us -> none  [the longest x256 178 us: sub_step(): error_now = (column_now - restored) / local_pivots[i, i]]
    ppermute x0 -> x17, waiting for transfers between devices: none -> 123 us  [the longest x4 104 us: own_columns(): lax.ppermute(panels, ALL, moves(target(k)))]
    all_to_all x1 -> x0, blocking collectives: 117 us -> none  [on_device(): lax.all_to_all(working.astype(jnp.bfloat16), 'tp', split_axis=1, concat_a...]
    reduce_scatter x1 -> x0, waiting for transfers between devices: 99.5 us -> none  [on_device(): lax.psum_scatter(lax.dot_general(x_full, x_own, (((0,), (0,)), ((), ())),...]
    psum x1 -> x0, blocking collectives: 84.6 us -> none  [on_device(): row_sums = lax.psum(jnp.sum(local_rows * local_rows, axis=1), 'tp')]
    psum x1 -> x0, waiting for transfers between devices: 54 us -> none  [spread(): return lax.psum(jnp.where(mine, x, jnp.zeros_like(x)), axis)]
    dot_general x35 -> x0, matrix products: 47 us -> none  [the longest x2 23 us: on_device(): jnp.dot(errors, lax.all_gather(panels[block_start:block_start + BLOCK], (...]
  transfers between devices with their start and end apart: 5 -> 21, of which waited for: 5 -> 8; matrix products, arithmetic and copies ran while one was open for 31% -> 5% of each run, Pallas kernels for 0% -> 8%
where the time goes in v1:
time: 351 us; the launch traced here: 349 us
  waiting for transfers between devices  225 us (64%)
  starting transfers between devices  49.1 us (14%)
  Pallas kernels  36.3 us (10%)
  local copies, waits for them, and re-layouts  17.9 us (5%)
  between operations  14 us (4%)
  other arithmetic  7.57 us (2%)
    ppermute x4, waiting for transfers between devices, own_columns(): lax.ppermute(panels, ALL, moves(target(k)))  104 us
    all_gather x1, waiting for transfers between devices, on_device(): errors_all = lax.all_gather(errors, 'tp', axis=0, tiled=True)  76 us
    all_gather x1, waiting for transfers between devices, on_device(): quarter = lax.all_gather(swapped, 'tp').reshape(groups, pieces, toks, feats)  20.2 us
    ppermute x4, starting transfers between devices, own_columns(): lax.ppermute(panels, ALL, moves(target(k)))  15.2 us
    pallas_call x1, Pallas kernels, block_errors(): pl.pallas_call(errors_kernel, grid=(1,), out_shape=jax.ShapeDtypeStruct((...  13.5 us
    pallas_call x1, Pallas kernels, corrected(): pl.pallas_call(corrected_kernel, grid=(rows // step,), out_shape=jax.Shap...  13.5 us
    ppermute x10, waiting for transfers between devices, step(): lax.ppermute(held, ALL, perm)  13.3 us
    all_to_all x1, starting transfers between devices, on_device(): lax.all_to_all(weight, 'tp', split_axis=1, concat_axis=0, tiled=True)  10.8 us
  transfers between devices with their start and end apart: 21, of which 8 were waited for; matrix products, arithmetic and copies ran while one was open for 5% of the time, Pallas kernels for 8%

profile of v1, /device:TPU:1, one launch (start us, length us, event | category | flops | bytes accessed | tf_op | source)
XLA Modules:
  0.0 349.5 jit_solution(839654674349783402)
XLA Ops:
  7.2 4.5 %collective-permute-start = (bf16[256,512]{1,0:T(8,128)(2,1)}, bf16[256,512]{1,0:T(8,128)(2,1)S(1)}, u32[]{:S(2)}, u32[]{:S(2)}) collective-permute-start(bf16[256,512]{1,0:T(8,128)(2,1)} %param.6), channel_id=1, source_target_pairs={{0,0},{1,1},{2,2},{3,3},{4,4},{5,5},{6,6},{7,7},{8,32},{9,33},{10,... | collective-permute-start | bytes 786440 | tf_op jit(solution)/shard_map/ppermute | solution.py:267
  11.7 4.3 %collective-permute-done = bf16[256,512]{1,0:T(8,128)(2,1)S(1)} collective-permute-done((bf16[256,512]{1,0:T(8,128)(2,1)}, bf16[256,512]{1,0:T(8,128)(2,1)S(1)}, u32[]{:S(2)}, u32[]{:S(2)}) %collective-permute-start) | collective-permute-done | bytes 262176 | tf_op jit(solution)/shard_map/ppermute | solution.py:267
  16.0 0.7 copy-done.3
  16.8 0.9 broadcast_select_fusion.1
  20.4 0.9 slice.3.w_ref
  23.4 0.7 convert_bitcast_fusion.1
  24.2 1.3 collective-permute-start.10
  26.8 0.7 convert_bitcast_fusion
  27.5 13.3 %collective-permute-done.10 = bf16[256,256]{1,0:T(8,128)(2,1)S(1)} collective-permute-done((bf16[256,256]{1,0:T(8,128)(2,1)S(1)}, bf16[256,256]{1,0:T(8,128)(2,1)S(1)}, u32[]{:S(2)}, u32[]{:S(2)}) %collective-permute-start.10) | collective-permute-done | bytes 131104 | tf_op jit(solution)/shard_map/ppermute | solution.py:219
  40.8 13.5 %errors.1 = bf16[240,256]{1,0:T(8,128)(2,1)} custom-call(bf16[240,256]{1,0:T(8,128)(2,1)S(1)} %slice.3.w_ref, f32[2,256]{1,0:T(2,128)S(1)} %pad.7.codes_ref, f32[2,256]{1,0:T(2,128)S(1)} %pad.8.zeros_ref, bf16[256,256]{1,0:T(8,128)(2,1)S(1)} %add_add_fusion.p_ref), custom_call_target="tpu_custom_call" | custom-call | flops 10000000 | bytes 1000000 | tf_op jit(solution)/shard_map/errors/pallas_call | solution.py:120
  54.4 7.8 %copy.15 = bf16[30,32,8,512]{3,2,0,1:T(8,128)(2,1)} copy(bf16[30,32,8,512]{3,2,1,0:T(8,128)(2,1)} %bitcast.34) | data formatting | bytes 15728640 | tf_op jit(solution)/shard_map/all_to_all | solution.py:279
  62.2 10.8 %all-to-all-start = ((bf16[240,32,512]{2,0,1:T(8,128)(2,1)}), bf16[240,32,512]{2,0,1:T(8,128)(2,1)}, u32[]{:S(2)}, u32[]{:S(2)}) async-start(bf16[240,32,512]{2,0,1:T(8,128)(2,1)} %bitcast.33), calls=%async_computation | async-start | bytes 15728640 | tf_op jit(solution)/shard_map/all_to_all | solution.py:279
  73.7 1.2 collective-permute-start.14
  74.9 4.8 %collective-permute-start.15 = (bf16[256,128]{1,0:T(8,128)(2,1)S(1)}, bf16[256,128]{1,0:T(8,128)(2,1)S(1)}, u32[]{:S(2)}, u32[]{:S(2)}) collective-permute-start(bf16[256,128]{1,0:T(8,128)(2,1)S(1)} %copy-done.4), channel_id=1, source_target_pairs={{0,64},{1,96},{2,0},{3,32},{4,65},{5,97},{6,1},{7,33},{8,66},{9,98... | collective-permute-start | bytes 196616 | tf_op jit(solution)/shard_map/ppermute | solution.py:253
  79.8 7.1 %collective-permute-start.16 = (bf16[256,128]{1,0:T(8,128)(2,1)S(1)}, bf16[256,128]{1,0:T(8,128)(2,1)S(1)}, u32[]{:S(2)}, u32[]{:S(2)}) collective-permute-start(bf16[256,128]{1,0:T(8,128)(2,1)S(1)} %copy-done.4), channel_id=1, source_target_pairs={{0,96},{1,64},{2,32},{3,0},{4,97},{5,65},{6,33},{7,1},{8,98},{9,66... | collective-permute-start | bytes 196616 | tf_op jit(solution)/shard_map/ppermute | solution.py:253
  86.9 1.9 collective-permute-start.13
  88.9 0.7 dynamic_slice.19
  89.6 0.8 dynamic_slice.20
  90.3 83.1 %collective-permute-done.14 = bf16[256,128]{1,0:T(8,128)(2,1)S(1)} collective-permute-done((bf16[256,128]{1,0:T(8,128)(2,1)S(1)}, bf16[256,128]{1,0:T(8,128)(2,1)S(1)}, u32[]{:S(2)}, u32[]{:S(2)}) %collective-permute-start.14) | collective-permute-done | bytes 65568 | tf_op jit(solution)/shard_map/ppermute | solution.py:253
  173.5 21.1 %collective-permute-done.15 = bf16[256,128]{1,0:T(8,128)(2,1)S(1)} collective-permute-done((bf16[256,128]{1,0:T(8,128)(2,1)S(1)}, bf16[256,128]{1,0:T(8,128)(2,1)S(1)}, u32[]{:S(2)}, u32[]{:S(2)}) %collective-permute-start.15) | collective-permute-done | bytes 65568 | tf_op jit(solution)/shard_map/ppermute | solution.py:253
  194.7 20.2 %all-gather.8.cloned.1.call-done = bf16[8192,512]{1,0:T(8,128)(2,1)} async-done(((bf16[256,512]{1,0:T(8,128)(2,1)}), bf16[8192,512]{1,0:T(8,128)(2,1)}) %all-gather.8.cloned.1.call-update) | async-done | bytes 8388624 | tf_op jit(solution)/shard_map/all_gather | solution.py:268
  214.9 5.1 %multiply_reduce_fusion = f32[8192]{0:T(1024)S(1)} fusion(bf16[8192,512]{1,0:T(8,128)(2,1)} %all-gather.8.cloned.1.call-done), kind=kLoop, calls=%fused_computation | loop fusion | flops 12574720 | bytes 8421376 | tf_op jit(solution)/shard_map/reduce_sum | solution.py:282
  220.0 1.0 collective-permute-start.1
  221.0 0.8 collective-permute-done.1
  221.8 10.3 %collective-permute-start.2 = (f32[4,256]{1,0:T(4,128)S(1)}, f32[4,256]{1,0:T(4,128)S(1)}, u32[]{:S(2)}, u32[]{:S(2)}) collective-permute-start(f32[4,256]{1,0:T(4,128)S(1)} %add.65), channel_id=1, source_target_pairs={{0,64},{1,65},{2,66},{3,67},{4,68},{5,69},{6,70},{7,71},{8,72},{9,... | collective-permute-start | bytes 12296 | tf_op jit(solution)/shard_map/ppermute | solution.py:284
  232.1 76.0 %all-gather.6.cloned.1.call-done.e_ref = bf16[7680,256]{1,0:T(8,128)(2,1)} async-done(((bf16[240,256]{1,0:T(8,128)(2,1)}), bf16[7680,256]{1,0:T(8,128)(2,1)}) %all-gather.6.cloned.1.call-update) | async-done | bytes 3932176 | tf_op jit(solution)/shard_map/all_gather | solution.py:276
  308.1 2.1 copy-done.1
  310.2 13.5 %corrected.1 = bf16[7680,512]{1,0:T(8,128)(2,1)} custom-call(bf16[7680,512]{1,0:T(8,128)(2,1)} %bitcast.6.w_ref, bf16[7680,256]{1,0:T(8,128)(2,1)S(1)} %copy-done.1, bf16[256,512]{1,0:T(8,128)(2,1)S(1)} %pad_maximum_fusion.1.p_ref), custom_call_target="tpu_custom_call" | custom-call | flops 2013265920 | bytes 20971520 | tf_op jit(solution)/shard_map/corrected/pallas_call | solution.py:190
  324.0 5.1 %all-gather.10.cloned.1.call-done = bf16[1024,512]{1,0:T(8,128)(2,1)} async-done(((bf16[256,512]{1,0:T(8,128)(2,1)}), bf16[1024,512]{1,0:T(8,128)(2,1)}) %all-gather.10.cloned.1.call-update) | async-done | bytes 1048592 | tf_op jit(solution)/shard_map/all_gather | solution.py:269
  329.0 3.4 copy-done
  332.4 1.2 copy-done.2
  333.6 9.3 %mean_outer.1 = f32[4096,512]{1,0:T(8,128)} custom-call(bf16[4,8,256,512]{3,2,1,0:T(8,128)(2,1)S(1)} %bitcast.29, bf16[4,256,512]{2,1,0:T(8,128)(2,1)S(1)} %bitcast.30, f32[4,256,1]{2,1,0:T(8,128)S(1)} %copy.11.inv_ref, f32[8,1,512]{2,1,0:T(1,128)S(1)} %bitcast.31, f32[1,512]{1,0:T(1,128)S(1)} %bitcast.32), custom_call_target="tpu_custom_call" | custom-call | flops 4294967296 | bytes 20971520 | tf_op jit(solution)/shard_map/mean_outer/pallas_call | solution.py:159
  (49 shorter events, 7.4 us)
Async XLA Ops:
  7.2 207.7 %all-gather.8.cloned.1.call-start = ((), (), s32[]{:S(2)}) async-start(), calls=%async_computation.2 | async-start | bytes 8650752 | tf_op jit(solution)/shard_map/all_gather | solution.py:268
  7.2 8.8 %collective-permute-start = (bf16[256,512]{1,0:T(8,128)(2,1)}, bf16[256,512]{1,0:T(8,128)(2,1)S(1)}, u32[]{:S(2)}, u32[]{:S(2)}) collective-permute-start(bf16[256,512]{1,0:T(8,128)(2,1)} %param.6), channel_id=1, source_target_pairs={{0,0},{1,1},{2,2},{3,3},{4,4},{5,5},{6,6},{7,7},{8,32},{9,33},{10,... | collective-permute-start | bytes 786440 | tf_op jit(solution)/shard_map/ppermute | solution.py:267
  16.0 0.7 copy-start.3
  16.7 291.4 %all-gather.6.cloned.1.call-start = ((), (), s32[]{:S(2)}) async-start(), calls=%async_computation.1 | async-start | bytes 4055040 | tf_op jit(solution)/shard_map/all_gather | solution.py:276
  17.7 0.7 collective-permute-start.3
  18.4 2.9 collective-permute-start.4
  19.1 2.3 collective-permute-start.5
  19.7 1.6 collective-permute-start.6
  21.4 2.7 collective-permute-start.7
  22.1 2.1 collective-permute-start.8
  22.7 1.4 collective-permute-start.9
  24.2 16.6 %collective-permute-start.10 = (bf16[256,256]{1,0:T(8,128)(2,1)S(1)}, bf16[256,256]{1,0:T(8,128)(2,1)S(1)}, u32[]{:S(2)}, u32[]{:S(2)}) collective-permute-start(bf16[256,256]{1,0:T(8,128)(2,1)S(1)} %add_add_fusion.1), channel_id=1, source_target_pairs={{0,32},{1,33},{2,34},{3,35},{4,36},{5,37},{6,38},{7,39},{8,40},{9,... | collective-permute-start | bytes 393224 | tf_op jit(solution)/shard_map/ppermute | solution.py:219
  25.5 15.3 %collective-permute-start.11 = (bf16[256,256]{1,0:T(8,128)(2,1)S(1)}, bf16[256,256]{1,0:T(8,128)(2,1)S(1)}, u32[]{:S(2)}, u32[]{:S(2)}) collective-permute-start(bf16[256,256]{1,0:T(8,128)(2,1)S(1)} %add_add_fusion.1), channel_id=1, source_target_pairs={{0,64},{1,65},{2,66},{3,67},{4,68},{5,69},{6,70},{7,71},{8,72},{9,... | collective-permute-start | bytes 393224 | tf_op jit(solution)/shard_map/ppermute | solution.py:219
  26.2 14.6 %collective-permute-start.12 = (bf16[256,256]{1,0:T(8,128)(2,1)S(1)}, bf16[256,256]{1,0:T(8,128)(2,1)S(1)}, u32[]{:S(2)}, u32[]{:S(2)}) collective-permute-start(bf16[256,256]{1,0:T(8,128)(2,1)S(1)} %add_add_fusion.1), channel_id=1, source_target_pairs={{0,96},{1,97},{2,98},{3,99},{4,100},{5,101},{6,102},{7,103},{8,104... | collective-permute-start | bytes 393224 | tf_op jit(solution)/shard_map/ppermute | solution.py:219
  62.2 11.5 %copy-start.4 = (bf16[256,128]{1,0:T(8,128)(2,1)S(1)}, bf16[256,128]{1,0:T(8,128)(2,1)}, u32[]{:S(2)}) copy-start(bf16[256,128]{1,0:T(8,128)(2,1)} %param.11) | copy-start | bytes 196612
  62.2 169.9 %all-to-all-start = ((bf16[240,32,512]{2,0,1:T(8,128)(2,1)}), bf16[240,32,512]{2,0,1:T(8,128)(2,1)}, u32[]{:S(2)}, u32[]{:S(2)}) async-start(bf16[240,32,512]{2,0,1:T(8,128)(2,1)} %bitcast.33), calls=%async_computation | async-start | bytes 15728640 | tf_op jit(solution)/shard_map/all_to_all | solution.py:279
  72.9 256.1 %all-gather.10.cloned.1.call-start = ((), (), s32[]{:S(2)}) async-start(), calls=%async_computation.3 | async-start | bytes 1310720 | tf_op jit(solution)/shard_map/all_gather | solution.py:269
  73.7 99.8 %collective-permute-start.14 = (bf16[256,128]{1,0:T(8,128)(2,1)S(1)}, bf16[256,128]{1,0:T(8,128)(2,1)S(1)}, u32[]{:S(2)}, u32[]{:S(2)}) collective-permute-start(bf16[256,128]{1,0:T(8,128)(2,1)S(1)} %copy-done.4), channel_id=1, source_target_pairs={{0,32},{1,0},{2,96},{3,64},{4,33},{5,1},{6,97},{7,65},{8,34},{9,2}... | collective-permute-start | bytes 196616 | tf_op jit(solution)/shard_map/ppermute | solution.py:253
  74.9 119.7 %collective-permute-start.15 = (bf16[256,128]{1,0:T(8,128)(2,1)S(1)}, bf16[256,128]{1,0:T(8,128)(2,1)S(1)}, u32[]{:S(2)}, u32[]{:S(2)}) collective-permute-start(bf16[256,128]{1,0:T(8,128)(2,1)S(1)} %copy-done.4), channel_id=1, source_target_pairs={{0,64},{1,96},{2,0},{3,32},{4,65},{5,97},{6,1},{7,33},{8,66},{9,98... | collective-permute-start | bytes 196616 | tf_op jit(solution)/shard_map/ppermute | solution.py:253
  79.8 114.9 %collective-permute-start.16 = (bf16[256,128]{1,0:T(8,128)(2,1)S(1)}, bf16[256,128]{1,0:T(8,128)(2,1)S(1)}, u32[]{:S(2)}, u32[]{:S(2)}) collective-permute-start(bf16[256,128]{1,0:T(8,128)(2,1)S(1)} %copy-done.4), channel_id=1, source_target_pairs={{0,96},{1,64},{2,32},{3,0},{4,97},{5,65},{6,33},{7,1},{8,98},{9,66... | collective-permute-start | bytes 196616 | tf_op jit(solution)/shard_map/ppermute | solution.py:253
  86.9 107.7 %collective-permute-start.13 = (bf16[256,128]{1,0:T(8,128)(2,1)S(1)}, bf16[256,128]{1,0:T(8,128)(2,1)S(1)}, u32[]{:S(2)}, u32[]{:S(2)}) collective-permute-start(bf16[256,128]{1,0:T(8,128)(2,1)S(1)} %copy-done.4), channel_id=1, source_target_pairs={{0,0},{1,32},{2,64},{3,96},{4,1},{5,33},{6,65},{7,97},{8,2},{9,34}... | collective-permute-start | bytes 196616 | tf_op jit(solution)/shard_map/ppermute | solution.py:253
  220.0 1.8 collective-permute-start.1
  221.8 101.9 %collective-permute-start.2 = (f32[4,256]{1,0:T(4,128)S(1)}, f32[4,256]{1,0:T(4,128)S(1)}, u32[]{:S(2)}, u32[]{:S(2)}) collective-permute-start(f32[4,256]{1,0:T(4,128)S(1)} %add.65), channel_id=1, source_target_pairs={{0,64},{1,65},{2,66},{3,67},{4,68},{5,69},{6,70},{7,71},{8,72},{9,... | collective-permute-start | bytes 12296 | tf_op jit(solution)/shard_map/ppermute | solution.py:284
  308.1 2.1 copy-start.1
  329.0 3.4 copy-start
  332.4 1.2 copy-start.2
Sparse Core Ops, SparseCore 0:
  16.8 197.9 all-gather.7
  217.8 90.2 all-gather.5
  309.8 19.2 all-gather.9

commit v2 on v1

--- a/solution.py
+++ b/solution.py
@@ -140,35 +140,47 @@
     )(weight, codes, zeros, first_panel)
 
 
-def gram_kernel(total, rows_ref, own_ref, inv_ref, gain_rows_ref, gain_own_ref, out_ref, own):
+RING = (0, 1, -1, 2)
+FIRST_PART = 128
+
+
+def gram_kernel(total, table, a_ref, d_ref, own_ref, inv_ref, gain_rows_ref, gain_own_ref, out_ref, own):
+    groups, toks = own_ref.shape[:2]
+
     @pl.when(pl.program_id(0) == 0)
     def _():
-        for g in range(own_ref.shape[0]):
-            v = own_ref[g].astype(jnp.float32) * inv_ref[g] * gain_own_ref[...]
-            own[g] = v.astype(jnp.bfloat16)
-
-    acc = 0.0
-    for g in range(own_ref.shape[0]):
-        v = rows_ref[g, 0].astype(jnp.float32) * inv_ref[g] * gain_rows_ref[0]
-        acc = acc + contract_rows(v.astype(jnp.bfloat16), own[g])
-    out_ref[...] = acc * (1.0 / total)
-
-
-def mean_outer(quarter, own, inv_norm, gain_rows, gain_own):
-    groups, pieces, toks, feats = quarter.shape
+        for g in range(groups):
+            v = own_ref[table[g]].astype(jnp.float32) * inv_ref[g] * gain_own_ref[...]
+            own[g * toks : (g + 1) * toks] = v.astype(jnp.bfloat16)
+
+    parts = []
+    for g in range(groups):
+        v = jnp.concatenate([a_ref[g, 0, 0], d_ref[0, g, 0]], axis=0).astype(jnp.float32)
+        parts.append((v * inv_ref[g] * gain_rows_ref[0]).astype(jnp.bfloat16))
+    out_ref[...] = contract_rows(jnp.concatenate(parts, axis=0), own[...]) * (1.0 / total)
+
+
+def mean_outer(part_a, part_d, own, inv_norm, gain_rows, gain_own, table):
+    groups, toks, feats = own.shape
+    pieces = 2 * groups
+    spec = pltpu.PrefetchScalarGridSpec(
+        num_scalar_prefetch=1,
+        grid=(pieces,),
+        in_specs=[
+            pl.BlockSpec((groups, 1, 1) + part_a.shape[3:], lambda i, s: (0, i // 2, i % 2, 0, 0)),
+            pl.BlockSpec((1, groups, 1) + part_d.shape[3:], lambda i, s: (i // 2, 0, i % 2, 0, 0)),
+            pl.BlockSpec((groups, toks, feats), lambda i, s: (0, 0, 0)),
+            pl.BlockSpec((groups, toks, 1), lambda i, s: (0, 0, 0)),
+            pl.BlockSpec((1, 1, feats), lambda i, s: (s[groups + i], 0, 0)),
+            pl.BlockSpec((1, feats), lambda i, s: (0, 0)),
+        ],
+        out_specs=pl.BlockSpec((feats, feats), lambda i, s: (s[groups + i], 0)),
+        scratch_shapes=[pltpu.VMEM((groups * toks, feats), jnp.bfloat16)],
+    )
     return pl.pallas_call(
         functools.partial(gram_kernel, groups * toks),
-        grid=(pieces,),
+        grid_spec=spec,
         out_shape=jax.ShapeDtypeStruct((pieces * feats, feats), jnp.float32),
-        in_specs=[
-            pl.BlockSpec((groups, 1, toks, feats), lambda i: (0, i, 0, 0)),
-            pl.BlockSpec((groups, toks, feats), lambda i: (0, 0, 0)),
-            pl.BlockSpec((groups, toks, 1), lambda i: (0, 0, 0)),
-            pl.BlockSpec((1, 1, feats), lambda i: (i, 0, 0)),
-            pl.BlockSpec((1, feats), lambda i: (0, 0)),
-        ],
-        out_specs=pl.BlockSpec((feats, feats), lambda i: (i, 0)),
-        scratch_shapes=[pltpu.VMEM((groups, toks, feats), jnp.bfloat16)],
         compiler_params=pltpu.CompilerParams(vmem_limit_bytes=32 * 2**20),
         cost_estimate=pl.CostEstimate(
             flops=2 * groups * toks * pieces * feats * feats,
@@ -176,33 +188,75 @@
             transcendentals=0,
         ),
         name="mean_outer",
-    )(quarter, own, inv_norm, gain_rows.reshape(pieces, 1, feats), gain_own.reshape(1, feats))
+    )(table, part_a, part_d, own, inv_norm, gain_rows.reshape(pieces, 1, feats), gain_own.reshape(1, feats))
 
 
 def corrected_kernel(w_ref, e_ref, p_ref, out_ref):
-    correction = jnp.dot(e_ref[...], p_ref[...], preferred_element_type=jnp.float32)
-    out_ref[...] = (w_ref[...].astype(jnp.float32) - correction).astype(jnp.bfloat16)
+    rows, feats = out_ref.shape
+    correction = jnp.dot(e_ref[...].reshape(rows, COLS), p_ref[...], preferred_element_type=jnp.float32)
+    value = w_ref[...].reshape(rows, feats).astype(jnp.float32) - correction
+    out_ref[...] = value.astype(jnp.bfloat16)
 
 
 def corrected(moved, errors, panel):
-    rows, feats = moved.shape
-    step = rows // 16
+    shards, rows, feats = moved.shape
+    step = 4
     return pl.pallas_call(
         corrected_kernel,
-        grid=(rows // step,),
-        out_shape=jax.ShapeDtypeStruct((rows, feats), jnp.bfloat16),
+        grid=(shards // step,),
+        out_shape=jax.ShapeDtypeStruct((shards * rows, feats), jnp.bfloat16),
         in_specs=[
-            pl.BlockSpec((step, feats), lambda i: (i, 0)),
-            pl.BlockSpec((step, COLS), lambda i: (i, 0)),
+            pl.BlockSpec((step, rows, feats), lambda i: (i, 0, 0)),
+            pl.BlockSpec((step, rows, COLS), lambda i: (i, 0, 0)),
             pl.BlockSpec((COLS, feats), lambda i: (0, 0)),
         ],
-        out_specs=pl.BlockSpec((step, feats), lambda i: (i, 0)),
-        compiler_params=pltpu.CompilerParams(vmem_limit_bytes=16 * 2**20),
+        out_specs=pl.BlockSpec((step * rows, feats), lambda i: (i, 0)),
+        compiler_params=pltpu.CompilerParams(vmem_limit_bytes=32 * 2**20),
         cost_estimate=pl.CostEstimate(
-            flops=2 * rows * feats * COLS, bytes_accessed=20 * 2**20, transcendentals=0
+            flops=2 * shards * rows * feats * COLS, bytes_accessed=20 * 2**20, transcendentals=0
         ),
         name="corrected",
     )(moved, errors, panel)
+
+
+def pack_kernel(w_ref, out_ref):
+    feats = out_ref.shape[2]
+    for i in range(out_ref.shape[0]):
+        out_ref[i] = w_ref[:, i * feats : (i + 1) * feats]
+
+
+def pack(weight, feats):
+    rows, total = weight.shape
+    shards = total // feats
+    return pl.pallas_call(
+        pack_kernel,
+        grid=(shards // 2,),
+        out_shape=jax.ShapeDtypeStruct((shards, rows, feats), weight.dtype),
+        in_specs=[pl.BlockSpec((rows, 2 * feats), lambda i: (0, i))],
+        out_specs=pl.BlockSpec((2, rows, feats), lambda i: (i, 0, 0)),
+        cost_estimate=pl.CostEstimate(flops=0, bytes_accessed=4 * rows * total, transcendentals=0),
+        name="pack",
+    )(weight)
+
+
+def shift(d, along_x):
+    if along_x:
+        return moves(lambda t, x, z, h: (t, (x + d) % 4, z, h))
+    return moves(lambda t, x, z, h: (t, x, (z + d) % 4, h))
+
+
+def ring(block, along_x):
+    others = [lax.ppermute(block, ALL, shift(-d, along_x)) for d in RING[1:]]
+    return [block] + others
+
+
+def exchange(block):
+    others = [lax.ppermute(block, ALL, moves(lambda t, x, z, h, k=k: (t ^ k, x, z, h))) for k in (1, 2, 3)]
+    return jnp.stack([block] + others)
+
+
+def later(value, *others):
+    return lax.optimization_barrier((value,) + others)[0]
 
 
 def first_columns(panels, t, p):
@@ -214,32 +268,23 @@
         ],
         axis=1,
     )
-
-    def step(held, perms):
-        for got in [lax.ppermute(held, ALL, perm) for perm in perms]:
-            held = held + got
-        return held
-
-    four = range(4)
-    held = step(held, [[(index(0, 0, 0, h), index(0, 0, 0, 1 - h)) for h in range(2)]])
-    held = step(
-        held,
-        [[(index(0, 0, 0, h), index(0, x, 0, h)) for h in range(2)] for x in (1, 2, 3)],
-    )
-    held = step(
-        held,
+    four, two = range(4), range(2)
+    steps = [
+        [[(index(0, 0, 0, h), index(0, 0, 0, 1 - h)) for h in two]],
+        [[(index(0, 0, 0, h), index(0, x, 0, h)) for h in two] for x in (1, 2, 3)],
+        [[(index(0, x, 0, h), index(0, x, z, h)) for x in four for h in two] for z in (1, 2, 3)],
         [
-            [(index(0, x, 0, h), index(0, x, z, h)) for x in four for h in range(2)]
-            for z in (1, 2, 3)
-        ],
-    )
-    return step(
-        held,
-        [
-            [(index(0, x, z, h), index(t, x, z, h)) for x in four for z in four for h in range(2)]
+            [(index(0, x, z, h), index(t, x, z, h)) for x in four for z in four for h in two]
             for t in (1, 2, 3)
         ],
-    )
+    ]
+    return held, steps
+
+
+def spread(held, perms):
+    for got in [lax.ppermute(held, ALL, perm) for perm in perms]:
+        held = held + got
+    return held
 
 
 def own_columns(panels, t):
@@ -260,33 +305,66 @@
     rows, feat_total = weight.shape
     t = lax.axis_index("tok")
     p = lax.axis_index("tp")
+    x, z, h = p // 8, p // 2 % 4, p % 2
     shards = lax.axis_size("tp")
     groups = lax.axis_size("tok")
-    pieces = shards // groups
-
-    swapped = lax.ppermute(residual, ALL, moves(lambda tt, x, z, h: (x, tt, z, h)))
-    quarter = lax.all_gather(swapped, "tp").reshape(groups, pieces, toks, feats)
-    own = lax.all_gather(residual, "tok")
-
-    first_panel = first_columns(panels, t, p)
+
+    held, steps = first_columns(panels, t, p)
+    held = spread(held, steps[0])
+    both = jnp.stack(
+        [
+            lax.ppermute(residual, ALL, moves(lambda tt, x, z, h: (x, tt, z, h))),
+            lax.ppermute(residual, ALL, moves(lambda tt, x, z, h: (x, tt, z, 1 - h))),
+        ]
+    )
+    both, held = lax.optimization_barrier((both, held))
+    held = spread(held, steps[1])
+    left = toks - FIRST_PART
+    part_a = jnp.concatenate(ring(both[:, :FIRST_PART], False))
+    part_d = jnp.concatenate(ring(both[:, FIRST_PART:], True))
+    held = spread(spread(held, steps[2]), steps[3])
+    part_a, part_d, first_panel, panels, residual, weight = lax.optimization_barrier(
+        (part_a, part_d, held, panels, residual, weight)
+    )
+    part_a = ring(part_a, True)
+    part_d = ring(part_d, False)
+
     pad = -(-rows // 128) * 128 - rows
     codes = jnp.pad(scale_codes.astype(jnp.float32).T, ((0, 0), (0, pad)))
     zeros = jnp.pad(zero_points.astype(jnp.float32).T, ((0, 0), (0, pad)))
     errors = block_errors(weight[:, :COLS], codes, zeros, first_panel)
-    errors_all = lax.all_gather(errors, "tp", axis=0, tiled=True)
+    packed = pack(weight, feats)
+    part_a, part_d, errors, packed, panels, residual = lax.optimization_barrier(
+        (part_a, part_d, errors, packed, panels, residual)
+    )
+
+    moved = lax.all_to_all(packed, "tp", split_axis=0, concat_axis=0)
+
+    own = exchange(residual)
     own_panel = own_columns(panels, t)
-
-    moved = lax.all_to_all(weight, "tp", split_axis=1, concat_axis=0, tiled=True)
-
-    squares = quarter.astype(jnp.float32)
-    sums = jnp.sum(squares * squares, axis=(1, 3))
+    part_a = jnp.stack(part_a).reshape(4, 4, 2, FIRST_PART, feats)
+    part_d = jnp.stack(part_d).reshape(4, 4, 2, left, feats)
+
+    sums = jnp.concatenate(
+        [
+            jnp.sum(jnp.square(part_a.astype(jnp.float32)), axis=(1, 2, 4)),
+            jnp.sum(jnp.square(part_d.astype(jnp.float32)), axis=(0, 2, 4)),
+        ],
+        axis=1,
+    )
     sums = sums + lax.ppermute(sums, ALL, moves(lambda tt, x, z, h: (tt ^ 1, x, z, h)))
     sums = sums + lax.ppermute(sums, ALL, moves(lambda tt, x, z, h: (tt ^ 2, x, z, h)))
+    copies = later(jnp.broadcast_to(errors[None], (shards, rows, COLS)), moved, own, own_panel, sums)
+    errors_all = lax.all_to_all(copies, "tp", split_axis=0, concat_axis=0)
     inv_norm = lax.rsqrt(sums / feat_total + EPS)[:, :, None]
     quarter_feats = feat_total // groups
     gain_rows = lax.dynamic_slice_in_dim(norm_gain, t * quarter_feats, quarter_feats, 0)
     gain_own = lax.dynamic_slice_in_dim(norm_gain, p * feats, feats, 0)
-    gram = mean_outer(quarter, own, inv_norm, gain_rows, gain_own)
+    table = jnp.stack(
+        [((x + d) % 4) ^ t for d in RING]
+        + [((z + d) % 4) * 2 + (h ^ c) for d in RING for c in range(2)]
+    ).astype(jnp.int32)
+    gram = mean_outer(part_a, part_d, own, inv_norm, gain_rows, gain_own, table)
 
     return (gram, corrected(moved, errors_all, own_panel))
 

time: 351 us -> 311 us (0.89)
  waiting for transfers between devices: 225 us -> 171 us
  starting transfers between devices: 49.1 us -> 71.8 us
  between operations: 14 us -> 1.23 us
  local copies, waits for them, and re-layouts: 17.9 us -> 9.35 us
  Pallas kernels: 36.3 us -> 44.7 us
    all_gather x3 -> x0, waiting for transfers between devices: 101 us -> none  [the longest x1 76 us: on_device(): errors_all = lax.all_gather(errors, 'tp', axis=0, tiled=True)]
    ppermute x4, waiting for transfers between devices: 104 us -> 5.41 us  [own_columns(): lax.ppermute(panels, ALL, moves(target(k)))]
    ppermute x1, waiting for transfers between devices: 0.01 us -> 73.6 us  [on_device(): lax.ppermute(sums, ALL, moves(lambda tt, x, z, h: (tt ^ 2, x, z, h)))]
    ppermute x10 -> x26, waiting for transfers between devices: 13.3 us -> 54.4 us  [the longest x12 22.9 us: ring(): others = [lax.ppermute(block, ALL, shift(-d, along_x)) for d in RING[1:]]]
    all_to_all x1 -> x2, waiting for transfers between devices: 0.01 us -> 35.6 us  [the longest x1 35.6 us: on_device(): errors_all = lax.all_to_all(copies, 'tp', split_axis=0, concat_axis=0)]
    ppermute x10 -> x26, starting transfers between devices: 7.31 us -> 35.3 us  [the longest x12 21 us: ring(): others = [lax.ppermute(block, ALL, shift(-d, along_x)) for d in RING[1:]]]
    ppermute x1, starting transfers between devices: 10.3 us -> 0.43 us  [on_device(): lax.ppermute(sums, ALL, moves(lambda tt, x, z, h: (tt ^ 2, x, z, h)))]
    pallas_call x2 -> x3, Pallas kernels: 22.8 us -> 31.8 us  [the longest x1 11.6 us: pack(): pl.pallas_call(pack_kernel, grid=(shards // 2,), out_shape=jax.ShapeDtype...]
  transfers between devices with their start and end apart: 21 -> 35, of which waited for: 8 -> 13; matrix products, arithmetic and copies ran while one was open for 5% -> 4% of each run, Pallas kernels for 8% -> 11%
where the time goes in v2:
time: 311 us; the launch traced here: 308 us
  waiting for transfers between devices  171 us (55%)
  starting transfers between devices  71.8 us (23%)
  Pallas kernels  44.7 us (14%)
  local copies, waits for them, and re-layouts  9.35 us (3%)
  other arithmetic  9.31 us (3%)
    ppermute x1, waiting for transfers between devices, on_device(): lax.ppermute(sums, ALL, moves(lambda tt, x, z, h: (tt ^ 2, x, z, h)))  73.6 us
    all_to_all x1, waiting for transfers between devices, on_device(): errors_all = lax.all_to_all(copies, 'tp', split_axis=0, concat_axis=0)  35.6 us
    ppermute x12, waiting for transfers between devices, ring(): others = [lax.ppermute(block, ALL, shift(-d, along_x)) for d in RING[1:]]  22.9 us
    ppermute x12, starting transfers between devices, ring(): others = [lax.ppermute(block, ALL, shift(-d, along_x)) for d in RING[1:]]  21 us
    pallas_call x1, Pallas kernels, block_errors(): pl.pallas_call(errors_kernel, grid=(1,), out_shape=jax.ShapeDtypeStruct((...  12.8 us
    all_to_all x1, starting transfers between devices, on_device(): errors_all = lax.all_to_all(copies, 'tp', split_axis=0, concat_axis=0)  12.3 us
    pallas_call x1, Pallas kernels, pack(): pl.pallas_call(pack_kernel, grid=(shards // 2,), out_shape=jax.ShapeDtype...  11.6 us
    ppermute x3, waiting for transfers between devices, exchange(): lax.ppermute(block, ALL, moves(lambda t, x, z, h, k=k: (t ^ k, x, z, h)))  11.6 us
  transfers between devices with their start and end apart: 35, of which 13 were waited for; matrix products, arithmetic and copies ran while one was open for 4% of the time, Pallas kernels for 11%

profile of v2, /device:TPU:1, one launch (start us, length us, event | category | flops | bytes accessed | tf_op | source)
XLA Modules:
  0.0 307.6 jit_solution(13471129319210080260)
XLA Ops:
  2.2 4.5 %collective-permute-start = (bf16[256,512]{1,0:T(8,128)(2,1)}, bf16[256,512]{1,0:T(8,128)(2,1)S(1)}, u32[]{:S(2)}, u32[]{:S(2)}) collective-permute-start(bf16[256,512]{1,0:T(8,128)(2,1)} %param.6), channel_id=1, source_target_pairs={{0,0},{1,1},{2,2},{3,3},{4,4},{5,5},{6,6},{7,7},{8,32},{9,33},{10,... | collective-permute-start | bytes 786440 | tf_op jit(solution)/shard_map/ppermute | solution.py:316
  6.7 2.7 collective-permute-start.1
  11.0 8.4 %collective-permute-done.1 = bf16[256,512]{1,0:T(8,128)(2,1)S(1)} collective-permute-done((bf16[256,512]{1,0:T(8,128)(2,1)}, bf16[256,512]{1,0:T(8,128)(2,1)S(1)}, u32[]{:S(2)}, u32[]{:S(2)}) %collective-permute-start.1) | collective-permute-done | bytes 262176 | tf_op jit(solution)/shard_map/ppermute | solution.py:317
  21.5 5.5 %collective-permute-start.8 = (bf16[2,128,512]{2,1,0:T(8,128)(2,1)S(1)}, bf16[2,128,512]{2,1,0:T(8,128)(2,1)S(1)}, u32[]{:S(2)}, u32[]{:S(2)}) collective-permute-start(bf16[2,128,512]{2,1,0:T(8,128)(2,1)S(1)} %get-tuple-element.50), channel_id=1, source_target_pairs={{0,16},{1,17},{2,18},{3,19},{4,20},{5,21},{6,22},{7,23},{8,24},{9,... | collective-permute-start | bytes 786440 | tf_op jit(solution)/shard_map/ppermute | solution.py:249
  29.2 2.7 collective-permute-start.6
  31.8 3.6 %collective-permute-start.5 = (bf16[2,128,512]{2,1,0:T(8,128)(2,1)S(1)}, bf16[2,128,512]{2,1,0:T(8,128)(2,1)S(1)}, u32[]{:S(2)}, u32[]{:S(2)}) collective-permute-start(bf16[2,128,512]{2,1,0:T(8,128)(2,1)S(1)} %get-tuple-element.51), channel_id=1, source_target_pairs={{0,4},{1,5},{2,6},{3,7},{4,0},{5,1},{6,2},{7,3},{8,12},{9,13},{10,... | collective-permute-start | bytes 786440 | tf_op jit(solution)/shard_map/ppermute | solution.py:249
  36.2 1.9 collective-permute-start.3
  41.0 2.5 collective-permute-done.4
  43.6 11.5 %collective-permute-done.15 = bf16[256,256]{1,0:T(8,128)(2,1)S(1)} collective-permute-done((bf16[256,256]{1,0:T(8,128)(2,1)S(1)}, bf16[256,256]{1,0:T(8,128)(2,1)S(1)}, u32[]{:S(2)}, u32[]{:S(2)}) %collective-permute-start.15) | collective-permute-done | bytes 131104 | tf_op jit(solution)/shard_map/ppermute | solution.py:285
  56.0 2.3 collective-permute-start.18
  60.0 1.6 collective-permute-start.22
  61.6 19.7 %collective-permute-done.20 = bf16[8,128,512]{2,1,0:T(8,128)(2,1)S(1)} collective-permute-done((bf16[8,128,512]{2,1,0:T(8,128)(2,1)S(1)}, bf16[8,128,512]{2,1,0:T(8,128)(2,1)S(1)}, u32[]{:S(2)}, u32[]{:S(2)}) %collective-permute-start.20) | collective-permute-done | bytes 1048608 | tf_op jit(solution)/shard_map/ppermute | solution.py:249
  82.3 11.6 %pack.1 = bf16[32,240,512]{2,1,0:T(8,128)(2,1)} custom-call(bf16[240,16384]{1,0:T(8,128)(2,1)} %w_ref), custom_call_target="tpu_custom_call" | custom-call | bytes 15728640 | tf_op jit(solution)/shard_map/pack/pallas_call | solution.py:231
  93.9 12.8 %errors.1 = bf16[240,256]{1,0:T(8,128)(2,1)S(1)} custom-call(bf16[240,256]{1,0:T(8,128)(2,1)S(1)} %slice.11.w_ref, f32[2,256]{1,0:T(2,128)S(1)} %pad.7.codes_ref, f32[2,256]{1,0:T(2,128)S(1)} %pad.8.zeros_ref, bf16[256,256]{1,0:T(8,128)(2,1)S(1)} %add_add_fusion.p_ref), custom_call_target="tpu_custom_call" | custom-call | flops 10000000 | bytes 1000000 | tf_op jit(solution)/shard_map/errors/pallas_call | solution.py:120
  107.5 4.9 %all-to-all-start = ((bf16[32,240,512]{2,1,0:T(8,128)(2,1)}), bf16[32,240,512]{2,1,0:T(8,128)(2,1)}, u32[]{:S(2)}, u32[]{:S(2)}) async-start(bf16[32,240,512]{2,1,0:T(8,128)(2,1)} %pack.1), calls=%async_computation | async-start | bytes 15728640 | tf_op jit(solution)/shard_map/all_to_all | solution.py:341
  112.5 6.8 %multiply_reduce_fusion = (f32[4,128]{1,0:T(4,128)S(1)}, bf16[4,4,2,128,512]{4,3,2,1,0:T(8,128)(2,1)}, f32[4,128]{1,0:T(4,128)S(1)}, bf16[4,4,2,128,512]{4,3,2,1,0:T(8,128)(2,1)}) fusion(bf16[1,4,2,128,512]{4,3,2,1,0:T(8,128)(2,1)} %bitcast.23, bf16[1,4,2,128,512]{4,3,2,1,0:T(8,128)(2,1)} %bitcast.22, bf16[1,4,2,128,512]{4,3,2,1,0:T(8,128)(2,1)} %bitcast.21, ...), kind=kLoop, calls=%fused_computation | loop fusion | flops 25164800 | bytes 16781312 | tf_op jit(solution)/shard_map/reduce_sum | solution.py:351
  119.3 3.8 %collective-permute-start.27 = (f32[4,256]{1,0:T(4,128)S(1)}, f32[4,256]{1,0:T(4,128)S(1)}, u32[]{:S(2)}, u32[]{:S(2)}) collective-permute-start(f32[4,256]{1,0:T(4,128)S(1)} %pad_maximum_fusion.9), channel_id=1, source_target_pairs={{0,32},{1,33},{2,34},{3,35},{4,36},{5,37},{6,38},{7,39},{8,40},{9,... | collective-permute-start | bytes 12296 | tf_op jit(solution)/shard_map/ppermute | solution.py:355
  124.3 4.0 %collective-permute-start.32 = (bf16[256,128]{1,0:T(8,128)(2,1)S(1)}, bf16[256,128]{1,0:T(8,128)(2,1)S(1)}, u32[]{:S(2)}, u32[]{:S(2)}) collective-permute-start(bf16[256,128]{1,0:T(8,128)(2,1)S(1)} %copy-done.2), channel_id=1, source_target_pairs={{0,96},{1,64},{2,32},{3,0},{4,97},{5,65},{6,33},{7,1},{8,98},{9,66... | collective-permute-start | bytes 196616 | tf_op jit(solution)/shard_map/ppermute | solution.py:298
  128.4 2.5 collective-permute-start.31
  131.3 3.7 %collective-permute-start.29 = (bf16[256,128]{1,0:T(8,128)(2,1)S(1)}, bf16[256,128]{1,0:T(8,128)(2,1)S(1)}, u32[]{:S(2)}, u32[]{:S(2)}) collective-permute-start(bf16[256,128]{1,0:T(8,128)(2,1)S(1)} %copy-done.2), channel_id=1, source_target_pairs={{0,0},{1,32},{2,64},{3,96},{4,1},{5,33},{6,65},{7,97},{8,2},{9,34}... | collective-permute-start | bytes 196616 | tf_op jit(solution)/shard_map/ppermute | solution.py:298
  135.0 73.6 %collective-permute-done.28 = f32[4,256]{1,0:T(4,128)S(1)} collective-permute-done((f32[4,256]{1,0:T(4,128)S(1)}, f32[4,256]{1,0:T(4,128)S(1)}, u32[]{:S(2)}, u32[]{:S(2)}) %collective-permute-start.28) | collective-permute-done | bytes 4128 | tf_op jit(solution)/shard_map/ppermute | solution.py:356
  208.6 3.7 %collective-permute-start.26 = (bf16[256,512]{1,0:T(8,128)(2,1)}, bf16[256,512]{1,0:T(8,128)(2,1)S(1)}, u32[]{:S(2)}, u32[]{:S(2)}) collective-permute-start(bf16[256,512]{1,0:T(8,128)(2,1)} %param.6), channel_id=1, source_target_pairs={{0,96},{1,97},{2,98},{3,99},{4,100},{5,101},{6,102},{7,103},{8,104... | collective-permute-start | bytes 786440 | tf_op jit(solution)/shard_map/ppermute | solution.py:254
  212.8 4.8 %collective-permute-done.31 = bf16[256,128]{1,0:T(8,128)(2,1)S(1)} collective-permute-done((bf16[256,128]{1,0:T(8,128)(2,1)S(1)}, bf16[256,128]{1,0:T(8,128)(2,1)S(1)}, u32[]{:S(2)}, u32[]{:S(2)}) %collective-permute-start.31) | collective-permute-done | bytes 65568 | tf_op jit(solution)/shard_map/ppermute | solution.py:298
  218.3 5.2 %collective-permute-done.26 = bf16[256,512]{1,0:T(8,128)(2,1)S(1)} collective-permute-done((bf16[256,512]{1,0:T(8,128)(2,1)}, bf16[256,512]{1,0:T(8,128)(2,1)S(1)}, u32[]{:S(2)}, u32[]{:S(2)}) %collective-permute-start.26) | collective-permute-done | bytes 262176 | tf_op jit(solution)/shard_map/ppermute | solution.py:254
  223.6 6.4 %collective-permute-done.25 = bf16[256,512]{1,0:T(8,128)(2,1)S(1)} collective-permute-done((bf16[256,512]{1,0:T(8,128)(2,1)}, bf16[256,512]{1,0:T(8,128)(2,1)S(1)}, u32[]{:S(2)}, u32[]{:S(2)}) %collective-permute-start.25) | collective-permute-done | bytes 262176 | tf_op jit(solution)/shard_map/ppermute | solution.py:254
  231.1 2.2 broadcast_in_dim.14
  233.2 12.3 %all-to-all-start.1 = ((bf16[32,240,256]{2,1,0:T(8,128)(2,1)}), bf16[32,240,256]{2,1,0:T(8,128)(2,1)}, u32[]{:S(2)}, u32[]{:S(2)}) async-start(bf16[32,240,256]{2,1,0:T(8,128)(2,1)} %broadcast_in_dim.14), calls=%async_computation.1 | async-start | bytes 7864320 | tf_op jit(solution)/shard_map/all_to_all | solution.py:358
  247.5 2.2 copy-done
  249.7 2.2 copy-done.1
  251.9 9.6 %mean_outer.1 = f32[4096,512]{1,0:T(8,128)} custom-call(s32[12]{0:T(128)S(1)} %stack.120.table, bf16[4,4,2,128,512]{4,3,2,1,0:T(8,128)(2,1)S(1)} %copy-done.1, bf16[4,4,2,128,512]{4,3,2,1,0:T(8,128)(2,1)S(1)} %copy-done, bf16[4,256,512]{2,1,0:T(8,128)(2,1)S(1)} %pad_maximum_fusion.4.own_ref, f32[4,256,1]{2,1,0:T(8,128)S(1)} %copy.8.inv_ref, ...), custom_call_target="tpu_custom_call" | custom-call | flops 4294967296 | bytes 20971520 | tf_op jit(solution)/shard_map/mean_outer/pallas_call | solution.py:180
  261.5 35.6 %all-to-all-done.1.e_ref = bf16[32,240,256]{2,1,0:T(8,128)(2,1)} async-done(((bf16[32,240,256]{2,1,0:T(8,128)(2,1)}), bf16[32,240,256]{2,1,0:T(8,128)(2,1)}, u32[]{:S(2)}, u32[]{:S(2)}) %all-to-all-start.1) | async-done | bytes 3932192 | tf_op jit(solution)/shard_map/all_to_all | solution.py:358
  297.1 10.6 %corrected.1 = bf16[7680,512]{1,0:T(8,128)(2,1)} custom-call(bf16[32,240,512]{2,1,0:T(8,128)(2,1)} %all-to-all-done.w_ref, bf16[32,240,256]{2,1,0:T(8,128)(2,1)} %all-to-all-done.1.e_ref, bf16[256,512]{1,0:T(8,128)(2,1)S(1)} %pad_maximum_fusion.7.p_ref), custom_call_target="tpu_custom_call" | custom-call | flops 2013265920 | bytes 20971520 | tf_op jit(solution)/shard_map/corrected/pallas_call | solution.py:204
  (80 shorter events, 21.0 us)
Async XLA Ops:
  1.5 7.9 %collective-permute-start.2 = (bf16[256,256]{1,0:T(8,128)(2,1)S(1)}, bf16[256,256]{1,0:T(8,128)(2,1)S(1)}, u32[]{:S(2)}, u32[]{:S(2)}) collective-permute-start(bf16[256,256]{1,0:T(8,128)(2,1)S(1)} %pad_maximum_fusion.8), channel_id=1, source_target_pairs={{0,1},{1,0}} | collective-permute-start | bytes 393224 | tf_op jit(solution)/shard_map/ppermute | solution.py:285
  2.2 8.8 %collective-permute-start = (bf16[256,512]{1,0:T(8,128)(2,1)}, bf16[256,512]{1,0:T(8,128)(2,1)S(1)}, u32[]{:S(2)}, u32[]{:S(2)}) collective-permute-start(bf16[256,512]{1,0:T(8,128)(2,1)} %param.6), channel_id=1, source_target_pairs={{0,0},{1,1},{2,2},{3,3},{4,4},{5,5},{6,6},{7,7},{8,32},{9,33},{10,... | collective-permute-start | bytes 786440 | tf_op jit(solution)/shard_map/ppermute | solution.py:316
  6.7 12.6 %collective-permute-start.1 = (bf16[256,512]{1,0:T(8,128)(2,1)}, bf16[256,512]{1,0:T(8,128)(2,1)S(1)}, u32[]{:S(2)}, u32[]{:S(2)}) collective-permute-start(bf16[256,512]{1,0:T(8,128)(2,1)} %param.6), channel_id=1, source_target_pairs={{0,1},{1,0},{2,3},{3,2},{4,5},{5,4},{6,7},{7,6},{8,33},{9,32},{10,... | collective-permute-start | bytes 786440 | tf_op jit(solution)/shard_map/ppermute | solution.py:317
  19.4 7.6 %collective-permute-start.11 = (bf16[256,256]{1,0:T(8,128)(2,1)S(1)}, bf16[256,256]{1,0:T(8,128)(2,1)S(1)}, u32[]{:S(2)}, u32[]{:S(2)}) collective-permute-start(bf16[256,256]{1,0:T(8,128)(2,1)S(1)} %fusion.1), channel_id=1, source_target_pairs={{0,24},{1,25}} | collective-permute-start | bytes 393224 | tf_op jit(solution)/shard_map/ppermute | solution.py:285
  20.1 6.9 %collective-permute-start.10 = (bf16[256,256]{1,0:T(8,128)(2,1)S(1)}, bf16[256,256]{1,0:T(8,128)(2,1)S(1)}, u32[]{:S(2)}, u32[]{:S(2)}) collective-permute-start(bf16[256,256]{1,0:T(8,128)(2,1)S(1)} %fusion.1), channel_id=1, source_target_pairs={{0,16},{1,17}} | collective-permute-start | bytes 393224 | tf_op jit(solution)/shard_map/ppermute | solution.py:285
  20.8 6.2 %collective-permute-start.9 = (bf16[256,256]{1,0:T(8,128)(2,1)S(1)}, bf16[256,256]{1,0:T(8,128)(2,1)S(1)}, u32[]{:S(2)}, u32[]{:S(2)}) collective-permute-start(bf16[256,256]{1,0:T(8,128)(2,1)S(1)} %fusion.1), channel_id=1, source_target_pairs={{0,8},{1,9}} | collective-permute-start | bytes 393224 | tf_op jit(solution)/shard_map/ppermute | solution.py:285
  21.5 14.7 %collective-permute-start.8 = (bf16[2,128,512]{2,1,0:T(8,128)(2,1)S(1)}, bf16[2,128,512]{2,1,0:T(8,128)(2,1)S(1)}, u32[]{:S(2)}, u32[]{:S(2)}) collective-permute-start(bf16[2,128,512]{2,1,0:T(8,128)(2,1)S(1)} %get-tuple-element.50), channel_id=1, source_target_pairs={{0,16},{1,17},{2,18},{3,19},{4,20},{5,21},{6,22},{7,23},{8,24},{9,... | collective-permute-start | bytes 786440 | tf_op jit(solution)/shard_map/ppermute | solution.py:249
  28.4 7.0 %collective-permute-start.12 = (bf16[256,256]{1,0:T(8,128)(2,1)S(1)}, bf16[256,256]{1,0:T(8,128)(2,1)S(1)}, u32[]{:S(2)}, u32[]{:S(2)}) collective-permute-start(bf16[256,256]{1,0:T(8,128)(2,1)S(1)} %add_add_fusion.2), channel_id=1, source_target_pairs={{0,2},{1,3},{8,10},{9,11},{16,18},{17,19},{24,26},{25,27}} | collective-permute-start | bytes 393224 | tf_op jit(solution)/shard_map/ppermute | solution.py:285
  29.1 9.1 %collective-permute-start.7 = (bf16[2,128,512]{2,1,0:T(8,128)(2,1)S(1)}, bf16[2,128,512]{2,1,0:T(8,128)(2,1)S(1)}, u32[]{:S(2)}, u32[]{:S(2)}) collective-permute-start(bf16[2,128,512]{2,1,0:T(8,128)(2,1)S(1)} %get-tuple-element.50), channel_id=1, source_target_pairs={{0,8},{1,9},{2,10},{3,11},{4,12},{5,13},{6,14},{7,15},{8,16},{9,17... | collective-permute-start | bytes 786440 | tf_op jit(solution)/shard_map/ppermute | solution.py:249
  29.2 9.7 %collective-permute-start.6 = (bf16[2,128,512]{2,1,0:T(8,128)(2,1)S(1)}, bf16[2,128,512]{2,1,0:T(8,128)(2,1)S(1)}, u32[]{:S(2)}, u32[]{:S(2)}) collective-permute-start(bf16[2,128,512]{2,1,0:T(8,128)(2,1)S(1)} %get-tuple-element.50), channel_id=1, source_target_pairs={{0,24},{1,25},{2,26},{3,27},{4,28},{5,29},{6,30},{7,31},{8,0},{9,1... | collective-permute-start | bytes 786440 | tf_op jit(solution)/shard_map/ppermute | solution.py:249
  31.8 7.8 %collective-permute-start.5 = (bf16[2,128,512]{2,1,0:T(8,128)(2,1)S(1)}, bf16[2,128,512]{2,1,0:T(8,128)(2,1)S(1)}, u32[]{:S(2)}, u32[]{:S(2)}) collective-permute-start(bf16[2,128,512]{2,1,0:T(8,128)(2,1)S(1)} %get-tuple-element.51), channel_id=1, source_target_pairs={{0,4},{1,5},{2,6},{3,7},{4,0},{5,1},{6,2},{7,3},{8,12},{9,13},{10,... | collective-permute-start | bytes 786440 | tf_op jit(solution)/shard_map/ppermute | solution.py:249
  35.4 8.0 %collective-permute-start.4 = (bf16[2,128,512]{2,1,0:T(8,128)(2,1)S(1)}, bf16[2,128,512]{2,1,0:T(8,128)(2,1)S(1)}, u32[]{:S(2)}, u32[]{:S(2)}) collective-permute-start(bf16[2,128,512]{2,1,0:T(8,128)(2,1)S(1)} %get-tuple-element.51), channel_id=1, source_target_pairs={{0,2},{1,3},{2,4},{3,5},{4,6},{5,7},{6,0},{7,1},{8,10},{9,11},{10,... | collective-permute-start | bytes 786440 | tf_op jit(solution)/shard_map/ppermute | solution.py:249
  36.2 7.3 %collective-permute-start.3 = (bf16[2,128,512]{2,1,0:T(8,128)(2,1)S(1)}, bf16[2,128,512]{2,1,0:T(8,128)(2,1)S(1)}, u32[]{:S(2)}, u32[]{:S(2)}) collective-permute-start(bf16[2,128,512]{2,1,0:T(8,128)(2,1)S(1)} %get-tuple-element.51), channel_id=1, source_target_pairs={{0,6},{1,7},{2,0},{3,1},{4,2},{5,3},{6,4},{7,5},{8,14},{9,15},{10,... | collective-permute-start | bytes 786440 | tf_op jit(solution)/shard_map/ppermute | solution.py:249
  38.2 5.4 %collective-permute-start.17 = (bf16[256,256]{1,0:T(8,128)(2,1)S(1)}, bf16[256,256]{1,0:T(8,128)(2,1)S(1)}, u32[]{:S(2)}, u32[]{:S(2)}) collective-permute-start(bf16[256,256]{1,0:T(8,128)(2,1)S(1)} %add_add_fusion.1), channel_id=1, source_target_pairs={{0,96},{1,97},{2,98},{3,99},{4,100},{5,101},{6,102},{7,103},{8,104... | collective-permute-start | bytes 393224 | tf_op jit(solution)/shard_map/ppermute | solution.py:285
  38.8 4.8 %collective-permute-start.16 = (bf16[256,256]{1,0:T(8,128)(2,1)S(1)}, bf16[256,256]{1,0:T(8,128)(2,1)S(1)}, u32[]{:S(2)}, u32[]{:S(2)}) collective-permute-start(bf16[256,256]{1,0:T(8,128)(2,1)S(1)} %add_add_fusion.1), channel_id=1, source_target_pairs={{0,64},{1,65},{2,66},{3,67},{4,68},{5,69},{6,70},{7,71},{8,72},{9,... | collective-permute-start | bytes 393224 | tf_op jit(solution)/shard_map/ppermute | solution.py:285
  39.7 15.4 %collective-permute-start.15 = (bf16[256,256]{1,0:T(8,128)(2,1)S(1)}, bf16[256,256]{1,0:T(8,128)(2,1)S(1)}, u32[]{:S(2)}, u32[]{:S(2)}) collective-permute-start(bf16[256,256]{1,0:T(8,128)(2,1)S(1)} %add_add_fusion.1), channel_id=1, source_target_pairs={{0,32},{1,33},{2,34},{3,35},{4,36},{5,37},{6,38},{7,39},{8,40},{9,... | collective-permute-start | bytes 393224 | tf_op jit(solution)/shard_map/ppermute | solution.py:285
  55.1 26.2 %collective-permute-start.20 = (bf16[8,128,512]{2,1,0:T(8,128)(2,1)S(1)}, bf16[8,128,512]{2,1,0:T(8,128)(2,1)S(1)}, u32[]{:S(2)}, u32[]{:S(2)}) collective-permute-start(bf16[8,128,512]{2,1,0:T(8,128)(2,1)S(1)} %pad_maximum_fusion.2), channel_id=1, source_target_pairs={{0,16},{1,17},{2,18},{3,19},{4,20},{5,21},{6,22},{7,23},{8,24},{9,... | collective-permute-start | bytes 3145736 | tf_op jit(solution)/shard_map/ppermute | solution.py:249
  55.2 51.6 %collective-permute-start.19 = (bf16[8,128,512]{2,1,0:T(8,128)(2,1)S(1)}, bf16[8,128,512]{2,1,0:T(8,128)(2,1)}, u32[]{:S(2)}, u32[]{:S(2)}) collective-permute-start(bf16[8,128,512]{2,1,0:T(8,128)(2,1)S(1)} %pad_maximum_fusion.2), channel_id=1, source_target_pairs={{0,8},{1,9},{2,10},{3,11},{4,12},{5,13},{6,14},{7,15},{8,16},{9,17... | collective-permute-start | bytes 3145736 | tf_op jit(solution)/shard_map/ppermute | solution.py:249
  56.0 50.8 %collective-permute-start.18 = (bf16[8,128,512]{2,1,0:T(8,128)(2,1)S(1)}, bf16[8,128,512]{2,1,0:T(8,128)(2,1)}, u32[]{:S(2)}, u32[]{:S(2)}) collective-permute-start(bf16[8,128,512]{2,1,0:T(8,128)(2,1)S(1)} %pad_maximum_fusion.2), channel_id=1, source_target_pairs={{0,24},{1,25},{2,26},{3,27},{4,28},{5,29},{6,30},{7,31},{8,0},{9,1... | collective-permute-start | bytes 3145736 | tf_op jit(solution)/shard_map/ppermute | solution.py:249
  58.3 48.5 %collective-permute-start.23 = (bf16[8,128,512]{2,1,0:T(8,128)(2,1)S(1)}, bf16[8,128,512]{2,1,0:T(8,128)(2,1)}, u32[]{:S(2)}, u32[]{:S(2)}) collective-permute-start(bf16[8,128,512]{2,1,0:T(8,128)(2,1)S(1)} %pad_maximum_fusion.3), channel_id=1, source_target_pairs={{0,4},{1,5},{2,6},{3,7},{4,0},{5,1},{6,2},{7,3},{8,12},{9,13},{10,... | collective-permute-start | bytes 3145736 | tf_op jit(solution)/shard_map/ppermute | solution.py:249
  60.0 47.5 %collective-permute-start.22 = (bf16[8,128,512]{2,1,0:T(8,128)(2,1)S(1)}, bf16[8,128,512]{2,1,0:T(8,128)(2,1)}, u32[]{:S(2)}, u32[]{:S(2)}) collective-permute-start(bf16[8,128,512]{2,1,0:T(8,128)(2,1)S(1)} %pad_maximum_fusion.3), channel_id=1, source_target_pairs={{0,2},{1,3},{2,4},{3,5},{4,6},{5,7},{6,0},{7,1},{8,10},{9,11},{10,... | collective-permute-start | bytes 3145736 | tf_op jit(solution)/shard_map/ppermute | solution.py:249
  81.3 26.2 %collective-permute-start.21 = (bf16[8,128,512]{2,1,0:T(8,128)(2,1)S(1)}, bf16[8,128,512]{2,1,0:T(8,128)(2,1)}, u32[]{:S(2)}, u32[]{:S(2)}) collective-permute-start(bf16[8,128,512]{2,1,0:T(8,128)(2,1)S(1)} %pad_maximum_fusion.3), channel_id=1, source_target_pairs={{0,6},{1,7},{2,0},{3,1},{4,2},{5,3},{6,4},{7,5},{8,14},{9,15},{10,... | collective-permute-start | bytes 3145736 | tf_op jit(solution)/shard_map/ppermute | solution.py:249
  107.5 123.5 %all-to-all-start = ((bf16[32,240,512]{2,1,0:T(8,128)(2,1)}), bf16[32,240,512]{2,1,0:T(8,128)(2,1)}, u32[]{:S(2)}, u32[]{:S(2)}) async-start(bf16[32,240,512]{2,1,0:T(8,128)(2,1)} %pack.1), calls=%async_computation | async-start | bytes 15728640 | tf_op jit(solution)/shard_map/all_to_all | solution.py:341
  123.9 84.7 %collective-permute-start.28 = (f32[4,256]{1,0:T(4,128)S(1)}, f32[4,256]{1,0:T(4,128)S(1)}, u32[]{:S(2)}, u32[]{:S(2)}) collective-permute-start(f32[4,256]{1,0:T(4,128)S(1)} %fusion), channel_id=1, source_target_pairs={{0,64},{1,65},{2,66},{3,67},{4,68},{5,69},{6,70},{7,71},{8,72},{9,... | collective-permute-start | bytes 12296 | tf_op jit(solution)/shard_map/ppermute | solution.py:356
  124.3 88.0 %collective-permute-start.32 = (bf16[256,128]{1,0:T(8,128)(2,1)S(1)}, bf16[256,128]{1,0:T(8,128)(2,1)S(1)}, u32[]{:S(2)}, u32[]{:S(2)}) collective-permute-start(bf16[256,128]{1,0:T(8,128)(2,1)S(1)} %copy-done.2), channel_id=1, source_target_pairs={{0,96},{1,64},{2,32},{3,0},{4,97},{5,65},{6,33},{7,1},{8,98},{9,66... | collective-permute-start | bytes 196616 | tf_op jit(solution)/shard_map/ppermute | solution.py:298
  128.4 89.2 %collective-permute-start.31 = (bf16[256,128]{1,0:T(8,128)(2,1)S(1)}, bf16[256,128]{1,0:T(8,128)(2,1)S(1)}, u32[]{:S(2)}, u32[]{:S(2)}) collective-permute-start(bf16[256,128]{1,0:T(8,128)(2,1)S(1)} %copy-done.2), channel_id=1, source_target_pairs={{0,64},{1,96},{2,0},{3,32},{4,65},{5,97},{6,1},{7,33},{8,66},{9,98... | collective-permute-start | bytes 196616 | tf_op jit(solution)/shard_map/ppermute | solution.py:298
  130.9 86.7 %collective-permute-start.30 = (bf16[256,128]{1,0:T(8,128)(2,1)S(1)}, bf16[256,128]{1,0:T(8,128)(2,1)S(1)}, u32[]{:S(2)}, u32[]{:S(2)}) collective-permute-start(bf16[256,128]{1,0:T(8,128)(2,1)S(1)} %copy-done.2), channel_id=1, source_target_pairs={{0,32},{1,0},{2,96},{3,64},{4,33},{5,1},{6,97},{7,65},{8,34},{9,2}... | collective-permute-start | bytes 196616 | tf_op jit(solution)/shard_map/ppermute | solution.py:298
  131.3 86.9 %collective-permute-start.29 = (bf16[256,128]{1,0:T(8,128)(2,1)S(1)}, bf16[256,128]{1,0:T(8,128)(2,1)S(1)}, u32[]{:S(2)}, u32[]{:S(2)}) collective-permute-start(bf16[256,128]{1,0:T(8,128)(2,1)S(1)} %copy-done.2), channel_id=1, source_target_pairs={{0,0},{1,32},{2,64},{3,96},{4,1},{5,33},{6,65},{7,97},{8,2},{9,34}... | collective-permute-start | bytes 196616 | tf_op jit(solution)/shard_map/ppermute | solution.py:298
  208.6 15.0 %collective-permute-start.26 = (bf16[256,512]{1,0:T(8,128)(2,1)}, bf16[256,512]{1,0:T(8,128)(2,1)S(1)}, u32[]{:S(2)}, u32[]{:S(2)}) collective-permute-start(bf16[256,512]{1,0:T(8,128)(2,1)} %param.6), channel_id=1, source_target_pairs={{0,96},{1,97},{2,98},{3,99},{4,100},{5,101},{6,102},{7,103},{8,104... | collective-permute-start | bytes 786440 | tf_op jit(solution)/shard_map/ppermute | solution.py:254
  212.3 17.7 %collective-permute-start.25 = (bf16[256,512]{1,0:T(8,128)(2,1)}, bf16[256,512]{1,0:T(8,128)(2,1)S(1)}, u32[]{:S(2)}, u32[]{:S(2)}) collective-permute-start(bf16[256,512]{1,0:T(8,128)(2,1)} %param.6), channel_id=1, source_target_pairs={{0,64},{1,65},{2,66},{3,67},{4,68},{5,69},{6,70},{7,71},{8,72},{9,... | collective-permute-start | bytes 786440 | tf_op jit(solution)/shard_map/ppermute | solution.py:254
  217.6 12.4 %collective-permute-start.24 = (bf16[256,512]{1,0:T(8,128)(2,1)}, bf16[256,512]{1,0:T(8,128)(2,1)S(1)}, u32[]{:S(2)}, u32[]{:S(2)}) collective-permute-start(bf16[256,512]{1,0:T(8,128)(2,1)} %param.6), channel_id=1, source_target_pairs={{0,32},{1,33},{2,34},{3,35},{4,36},{5,37},{6,38},{7,39},{8,40},{9,... | collective-permute-start | bytes 786440 | tf_op jit(solution)/shard_map/ppermute | solution.py:254
  233.2 63.8 %all-to-all-start.1 = ((bf16[32,240,256]{2,1,0:T(8,128)(2,1)}), bf16[32,240,256]{2,1,0:T(8,128)(2,1)}, u32[]{:S(2)}, u32[]{:S(2)}) async-start(bf16[32,240,256]{2,1,0:T(8,128)(2,1)} %broadcast_in_dim.14), calls=%async_computation.1 | async-start | bytes 7864320 | tf_op jit(solution)/shard_map/all_to_all | solution.py:358
  (8 other events, 170.8 us)

commit v3 on v2

--- a/solution.py
+++ b/solution.py
@@ -250,9 +250,12 @@
     return [block] + others
 
 
-def exchange(block):
-    others = [lax.ppermute(block, ALL, moves(lambda t, x, z, h, k=k: (t ^ k, x, z, h))) for k in (1, 2, 3)]
-    return jnp.stack([block] + others)
+def beside(block):
+    return jnp.stack([block, lax.ppermute(block, ALL, moves(lambda t, x, z, h: (t ^ 1, x, z, h)))])
+
+
+def beyond(pair):
+    return jnp.concatenate([pair, lax.ppermute(pair, ALL, moves(lambda t, x, z, h: (t ^ 2, x, z, h)))])
 
 
 def later(value, *others):
@@ -287,19 +290,6 @@
     return held
 
 
-def own_columns(panels, t):
-    def target(k):
-        def to(tt, x, z, h):
-            i = (z % 2) * 2 + h
-            return (i ^ k, tt, x, z // 2)
-
-        return to
-
-    got = jnp.stack([lax.ppermute(panels, ALL, moves(target(k))) for k in range(4)])
-    order = [lax.dynamic_index_in_dim(got, t ^ i, 0, keepdims=False) for i in range(4)]
-    return jnp.concatenate(order, axis=1)
-
-
 def on_device(residual, norm_gain, weight, scale_codes, zero_points, panels):
     toks, feats = residual.shape
     rows, feat_total = weight.shape
@@ -317,14 +307,15 @@
             lax.ppermute(residual, ALL, moves(lambda tt, x, z, h: (x, tt, z, 1 - h))),
         ]
     )
-    both, held = lax.optimization_barrier((both, held))
+    shard = lax.ppermute(panels, ALL, moves(lambda tt, x, z, h: (z % 2 * 2 + h, tt, x, z // 2)))
+    both, held, shard = lax.optimization_barrier((both, held, shard))
     held = spread(held, steps[1])
     left = toks - FIRST_PART
     part_a = jnp.concatenate(ring(both[:, :FIRST_PART], False))
     part_d = jnp.concatenate(ring(both[:, FIRST_PART:], True))
     held = spread(spread(held, steps[2]), steps[3])
-    part_a, part_d, first_panel, panels, residual, weight = lax.optimization_barrier(
-        (part_a, part_d, held, panels, residual, weight)
+    part_a, part_d, first_panel, shard, residual, weight = lax.optimization_barrier(
+        (part_a, part_d, held, shard, residual, weight)
     )
     part_a = ring(part_a, True)
     part_d = ring(part_d, False)
@@ -334,14 +325,18 @@
     zeros = jnp.pad(zero_points.astype(jnp.float32).T, ((0, 0), (0, pad)))
     errors = block_errors(weight[:, :COLS], codes, zeros, first_panel)
     packed = pack(weight, feats)
-    part_a, part_d, errors, packed, panels, residual = lax.optimization_barrier(
-        (part_a, part_d, errors, packed, panels, residual)
+    part_a, part_d, errors, packed, shard, residual = lax.optimization_barrier(
+        (part_a, part_d, errors, packed, shard, residual)
     )
 
     moved = lax.all_to_all(packed, "tp", split_axis=0, concat_axis=0)
 
-    own = exchange(residual)
-    own_panel = own_columns(panels, t)
+    pair = beside(jnp.concatenate([residual, shard], axis=1))
+    met = beyond(pair)
+    own = met[:, :, :feats]
+    own_panel = jnp.concatenate(
+        [lax.dynamic_index_in_dim(met, t ^ i, 0, keepdims=False)[:, feats:] for i in range(groups)], axis=1
+    )
     part_a = jnp.stack(part_a).reshape(4, 4, 2, FIRST_PART, feats)
     part_d = jnp.stack(part_d).reshape(4, 4, 2, left, feats)
 
@@ -354,7 +349,7 @@
     )
     sums = sums + lax.ppermute(sums, ALL, moves(lambda tt, x, z, h: (tt ^ 1, x, z, h)))
     sums = sums + lax.ppermute(sums, ALL, moves(lambda tt, x, z, h: (tt ^ 2, x, z, h)))
-    copies = later(jnp.broadcast_to(errors[None], (shards, rows, COLS)), moved, own, own_panel, sums)
+    copies = later(jnp.broadcast_to(errors[None], (shards, rows, COLS)), moved, met, sums)
     errors_all = lax.all_to_all(copies, "tp", split_axis=0, concat_axis=0)
     inv_norm = lax.rsqrt(sums / feat_total + EPS)[:, :, None]
     quarter_feats = feat_total // groups

time: 311 us -> 307 us (0.987)
  starting transfers between devices: 71.8 us -> 56.7 us
  waiting for transfers between devices: 171 us -> 182 us
    ppermute x1, waiting for transfers between devices: 73.6 us -> 93.3 us  [on_device(): lax.ppermute(sums, ALL, moves(lambda tt, x, z, h: (tt ^ 2, x, z, h)))]
    ppermute x7 -> x3, waiting for transfers between devices: 17 us -> 8.58 us  [the longest x1 7.32 us: on_device(): lax.ppermute(panels, ALL, moves(lambda tt, x, z, h: (z % 2 * 2 + h, tt, x...]
    ppermute x7 -> x3, starting transfers between devices: 14.9 us -> 7.23 us  [the longest x1 3.63 us: on_device(): lax.ppermute(panels, ALL, moves(lambda tt, x, z, h: (z % 2 * 2 + h, tt, x...]
    all_to_all x1, waiting for transfers between devices: 0.01 us -> 5.65 us  [on_device(): moved = lax.all_to_all(packed, 'tp', split_axis=0, concat_axis=0)]
    all_to_all x1, starting transfers between devices: 12.3 us -> 8.29 us  [on_device(): errors_all = lax.all_to_all(copies, 'tp', split_axis=0, concat_axis=0)]
  transfers between devices with their start and end apart: 35 -> 31, of which waited for: 13 -> 12; matrix products, arithmetic and copies ran while one was open for 4% -> 4% of each run, Pallas kernels for 11% -> 11%
where the time goes in v3:
time: 307 us; the launch traced here: 303 us
  waiting for transfers between devices  182 us (59%)
  starting transfers between devices  56.7 us (18%)
  Pallas kernels  44.7 us (15%)
  local copies, waits for them, and re-layouts  10.1 us (3%)
  other arithmetic  8.39 us (3%)
    ppermute x1, waiting for transfers between devices, on_device(): lax.ppermute(sums, ALL, moves(lambda tt, x, z, h: (tt ^ 2, x, z, h)))  93.3 us
    all_to_all x1, waiting for transfers between devices, on_device(): errors_all = lax.all_to_all(copies, 'tp', split_axis=0, concat_axis=0)  34.2 us
    ppermute x12, waiting for transfers between devices, ring(): others = [lax.ppermute(block, ALL, shift(-d, along_x)) for d in RING[1:]]  20.5 us
    ppermute x12, starting transfers between devices, ring(): others = [lax.ppermute(block, ALL, shift(-d, along_x)) for d in RING[1:]]  19 us
    pallas_call x1, Pallas kernels, block_errors(): pl.pallas_call(errors_kernel, grid=(1,), out_shape=jax.ShapeDtypeStruct((...  12.8 us
    ppermute x10, waiting for transfers between devices, spread(): lax.ppermute(held, ALL, perm)  12.6 us
    pallas_call x1, Pallas kernels, pack(): pl.pallas_call(pack_kernel, grid=(shards // 2,), out_shape=jax.ShapeDtype...  11.6 us
    pallas_call x1, Pallas kernels, corrected(): pl.pallas_call(corrected_kernel, grid=(shards // step,), out_shape=jax.Sh...  10.6 us
  transfers between devices with their start and end apart: 31, of which 12 were waited for; matrix products, arithmetic and copies ran while one was open for 4% of the time, Pallas kernels for 11%

profile of v3, /device:TPU:1, one launch (start us, length us, event | category | flops | bytes accessed | tf_op | source)
XLA Modules:
  0.0 303.0 jit_solution(12722905834812943529)
XLA Ops:
  2.2 4.5 %collective-permute-start = (bf16[256,512]{1,0:T(8,128)(2,1)}, bf16[256,512]{1,0:T(8,128)(2,1)S(1)}, u32[]{:S(2)}, u32[]{:S(2)}) collective-permute-start(bf16[256,512]{1,0:T(8,128)(2,1)} %param.6), channel_id=1, source_target_pairs={{0,0},{1,1},{2,2},{3,3},{4,4},{5,5},{6,6},{7,7},{8,32},{9,33},{10,... | collective-permute-start | bytes 786440 | tf_op jit(solution)/shard_map/ppermute | solution.py:306
  6.7 2.7 collective-permute-start.1
  9.4 3.6 %collective-permute-start.3 = (bf16[256,128]{1,0:T(8,128)(2,1)}, bf16[256,128]{1,0:T(8,128)(2,1)S(1)}, u32[]{:S(2)}, u32[]{:S(2)}) collective-permute-start(bf16[256,128]{1,0:T(8,128)(2,1)} %param.11), channel_id=1, source_target_pairs={{0,0},{1,32},{2,64},{3,96},{4,1},{5,33},{6,65},{7,97},{8,2},{9,34}... | collective-permute-start | bytes 196616 | tf_op jit(solution)/shard_map/ppermute | solution.py:310
  13.2 6.2 %collective-permute-done.1 = bf16[256,512]{1,0:T(8,128)(2,1)S(1)} collective-permute-done((bf16[256,512]{1,0:T(8,128)(2,1)}, bf16[256,512]{1,0:T(8,128)(2,1)S(1)}, u32[]{:S(2)}, u32[]{:S(2)}) %collective-permute-start.1) | collective-permute-done | bytes 262176 | tf_op jit(solution)/shard_map/ppermute | solution.py:307
  19.4 7.3 %collective-permute-done.3 = bf16[256,128]{1,0:T(8,128)(2,1)S(1)} collective-permute-done((bf16[256,128]{1,0:T(8,128)(2,1)}, bf16[256,128]{1,0:T(8,128)(2,1)S(1)}, u32[]{:S(2)}, u32[]{:S(2)}) %collective-permute-start.3) | collective-permute-done | bytes 65568 | tf_op jit(solution)/shard_map/ppermute | solution.py:310
  31.0 1.5 collective-permute-start.8
  32.5 1.3 collective-permute-start.7
  33.7 3.5 %collective-permute-start.6 = (bf16[2,128,512]{2,1,0:T(8,128)(2,1)S(1)}, bf16[2,128,512]{2,1,0:T(8,128)(2,1)S(1)}, u32[]{:S(2)}, u32[]{:S(2)}) collective-permute-start(bf16[2,128,512]{2,1,0:T(8,128)(2,1)S(1)} %get-tuple-element.57), channel_id=1, source_target_pairs={{0,4},{1,5},{2,6},{3,7},{4,0},{5,1},{6,2},{7,3},{8,12},{9,13},{10,... | collective-permute-start | bytes 786440 | tf_op jit(solution)/shard_map/ppermute | solution.py:249
  37.3 2.7 collective-permute-start.4
  41.6 1.3 collective-permute-start.16
  42.9 1.4 collective-permute-done.5
  44.8 12.6 %collective-permute-done.16 = bf16[256,256]{1,0:T(8,128)(2,1)S(1)} collective-permute-done((bf16[256,256]{1,0:T(8,128)(2,1)S(1)}, bf16[256,256]{1,0:T(8,128)(2,1)S(1)}, u32[]{:S(2)}, u32[]{:S(2)}) %collective-permute-start.16) | collective-permute-done | bytes 131104 | tf_op jit(solution)/shard_map/ppermute | solution.py:288
  58.4 2.2 collective-permute-start.20
  61.1 1.1 collective-permute-start.24
  62.2 1.6 collective-permute-start.23
  63.8 18.7 %collective-permute-done.21 = bf16[8,128,512]{2,1,0:T(8,128)(2,1)S(1)} collective-permute-done((bf16[8,128,512]{2,1,0:T(8,128)(2,1)S(1)}, bf16[8,128,512]{2,1,0:T(8,128)(2,1)S(1)}, u32[]{:S(2)}, u32[]{:S(2)}) %collective-permute-start.21) | collective-permute-done | bytes 1048608 | tf_op jit(solution)/shard_map/ppermute | solution.py:249
  82.5 3.6 %collective-permute-start.22 = (bf16[8,128,512]{2,1,0:T(8,128)(2,1)S(1)}, bf16[8,128,512]{2,1,0:T(8,128)(2,1)}, u32[]{:S(2)}, u32[]{:S(2)}) collective-permute-start(bf16[8,128,512]{2,1,0:T(8,128)(2,1)S(1)} %pad_maximum_fusion.4), channel_id=1, source_target_pairs={{0,6},{1,7},{2,0},{3,1},{4,2},{5,3},{6,4},{7,5},{8,14},{9,15},{10,... | collective-permute-start | bytes 3145736 | tf_op jit(solution)/shard_map/ppermute | solution.py:249
  87.1 11.6 %pack.1 = bf16[32,240,512]{2,1,0:T(8,128)(2,1)} custom-call(bf16[240,16384]{1,0:T(8,128)(2,1)} %w_ref), custom_call_target="tpu_custom_call" | custom-call | bytes 15728640 | tf_op jit(solution)/shard_map/pack/pallas_call | solution.py:231
  98.7 12.8 %errors.1 = bf16[240,256]{1,0:T(8,128)(2,1)S(1)} custom-call(bf16[240,256]{1,0:T(8,128)(2,1)S(1)} %slice.26.w_ref, f32[2,256]{1,0:T(2,128)S(1)} %pad.7.codes_ref, f32[2,256]{1,0:T(2,128)S(1)} %pad.8.zeros_ref, bf16[256,256]{1,0:T(8,128)(2,1)S(1)} %add_add_fusion.p_ref), custom_call_target="tpu_custom_call" | custom-call | flops 10000000 | bytes 1000000 | tf_op jit(solution)/shard_map/errors/pallas_call | solution.py:120
  111.6 5.9 %all-to-all-start = ((bf16[32,240,512]{2,1,0:T(8,128)(2,1)}), bf16[32,240,512]{2,1,0:T(8,128)(2,1)}, u32[]{:S(2)}, u32[]{:S(2)}) async-start(bf16[32,240,512]{2,1,0:T(8,128)(2,1)} %pack.1), calls=%async_computation | async-start | bytes 15728640 | tf_op jit(solution)/shard_map/all_to_all | solution.py:332
  118.4 3.0 %collective-permute-start.25 = (bf16[256,640]{1,0:T(8,128)(2,1)S(1)}, bf16[256,640]{1,0:T(8,128)(2,1)S(1)}, u32[]{:S(2)}, u32[]{:S(2)}) collective-permute-start(bf16[256,640]{1,0:T(8,128)(2,1)S(1)} %constant_dynamic-update-slice_fusion), channel_id=1, source_target_pairs={{0,32},{1,33},{2,34},{3,35},{4,36},{5,37},{6,38},{7,39},{8,40},{9,... | collective-permute-start | bytes 983048 | tf_op jit(solution)/shard_map/ppermute | solution.py:254
  121.4 1.3 collective-permute-done.25
  123.3 6.8 %multiply_reduce_fusion = (f32[4,128]{1,0:T(4,128)S(1)}, bf16[4,4,2,128,512]{4,3,2,1,0:T(8,128)(2,1)}, f32[4,128]{1,0:T(4,128)S(1)}, bf16[4,4,2,128,512]{4,3,2,1,0:T(8,128)(2,1)}) fusion(bf16[1,4,2,128,512]{4,3,2,1,0:T(8,128)(2,1)} %bitcast.23, bf16[1,4,2,128,512]{4,3,2,1,0:T(8,128)(2,1)} %bitcast.22, bf16[1,4,2,128,512]{4,3,2,1,0:T(8,128)(2,1)} %bitcast.21, ...), kind=kLoop, calls=%fused_computation | loop fusion | flops 25164800 | bytes 16781312 | tf_op jit(solution)/shard_map/reduce_sum | solution.py:346
  132.7 93.3 %collective-permute-done.28 = f32[4,256]{1,0:T(4,128)S(1)} collective-permute-done((f32[4,256]{1,0:T(4,128)S(1)}, f32[4,256]{1,0:T(4,128)S(1)}, u32[]{:S(2)}, u32[]{:S(2)}) %collective-permute-start.28) | collective-permute-done | bytes 4128 | tf_op jit(solution)/shard_map/ppermute | solution.py:351
  226.2 5.7 %all-to-all-done.w_ref = bf16[32,240,512]{2,1,0:T(8,128)(2,1)} async-done(((bf16[32,240,512]{2,1,0:T(8,128)(2,1)}), bf16[32,240,512]{2,1,0:T(8,128)(2,1)}, u32[]{:S(2)}, u32[]{:S(2)}) %all-to-all-start) | async-done | bytes 7864352 | tf_op jit(solution)/shard_map/all_to_all | solution.py:332
  231.8 2.2 broadcast_in_dim.14
  234.0 8.3 %all-to-all-start.1 = ((bf16[32,240,256]{2,1,0:T(8,128)(2,1)}), bf16[32,240,256]{2,1,0:T(8,128)(2,1)}, u32[]{:S(2)}, u32[]{:S(2)}) async-start(bf16[32,240,256]{2,1,0:T(8,128)(2,1)} %broadcast_in_dim.14), calls=%async_computation.1 | async-start | bytes 7864320 | tf_op jit(solution)/shard_map/all_to_all | solution.py:353
  244.6 1.9 copy-done
  246.5 2.2 copy-done.1
  248.7 9.6 %mean_outer.1 = f32[4096,512]{1,0:T(8,128)} custom-call(s32[12]{0:T(128)S(1)} %stack.99.table, bf16[4,4,2,128,512]{4,3,2,1,0:T(8,128)(2,1)S(1)} %copy-done.1, bf16[4,4,2,128,512]{4,3,2,1,0:T(8,128)(2,1)S(1)} %copy-done, bf16[4,256,512]{2,1,0:T(8,128)(2,1)S(1)} %slice.32.own_ref, f32[4,256,1]{2,1,0:T(8,128)S(1)} %copy.8.inv_ref, f32[8,1,512]{2,1,0:T(1,128)S(1)} %bitcast.40, ...), custom_call_target="tpu_custom_call" | custom-call | flops 4294967296 | bytes 20971520 | tf_op jit(solution)/shard_map/mean_outer/pallas_call | solution.py:180
  258.3 34.2 %all-to-all-done.1.e_ref = bf16[32,240,256]{2,1,0:T(8,128)(2,1)} async-done(((bf16[32,240,256]{2,1,0:T(8,128)(2,1)}), bf16[32,240,256]{2,1,0:T(8,128)(2,1)}, u32[]{:S(2)}, u32[]{:S(2)}) %all-to-all-start.1) | async-done | bytes 3932192 | tf_op jit(solution)/shard_map/all_to_all | solution.py:353
  292.5 10.6 %corrected.1 = bf16[7680,512]{1,0:T(8,128)(2,1)} custom-call(bf16[32,240,512]{2,1,0:T(8,128)(2,1)} %all-to-all-done.w_ref, bf16[32,240,256]{2,1,0:T(8,128)(2,1)} %all-to-all-done.1.e_ref, bf16[256,512]{1,0:T(8,128)(2,1)S(1)} %pad_maximum_fusion.7.p_ref), custom_call_target="tpu_custom_call" | custom-call | flops 2013265920 | bytes 20971520 | tf_op jit(solution)/shard_map/corrected/pallas_call | solution.py:204
  (81 shorter events, 16.7 us)
Async XLA Ops:
  1.5 11.6 %collective-permute-start.2 = (bf16[256,256]{1,0:T(8,128)(2,1)S(1)}, bf16[256,256]{1,0:T(8,128)(2,1)S(1)}, u32[]{:S(2)}, u32[]{:S(2)}) collective-permute-start(bf16[256,256]{1,0:T(8,128)(2,1)S(1)} %pad_maximum_fusion.8), channel_id=1, source_target_pairs={{0,1},{1,0}} | collective-permute-start | bytes 393224 | tf_op jit(solution)/shard_map/ppermute | solution.py:288
  2.2 11.0 %collective-permute-start = (bf16[256,512]{1,0:T(8,128)(2,1)}, bf16[256,512]{1,0:T(8,128)(2,1)S(1)}, u32[]{:S(2)}, u32[]{:S(2)}) collective-permute-start(bf16[256,512]{1,0:T(8,128)(2,1)} %param.6), channel_id=1, source_target_pairs={{0,0},{1,1},{2,2},{3,3},{4,4},{5,5},{6,6},{7,7},{8,32},{9,33},{10,... | collective-permute-start | bytes 786440 | tf_op jit(solution)/shard_map/ppermute | solution.py:306
  6.7 12.6 %collective-permute-start.1 = (bf16[256,512]{1,0:T(8,128)(2,1)}, bf16[256,512]{1,0:T(8,128)(2,1)S(1)}, u32[]{:S(2)}, u32[]{:S(2)}) collective-permute-start(bf16[256,512]{1,0:T(8,128)(2,1)} %param.6), channel_id=1, source_target_pairs={{0,1},{1,0},{2,3},{3,2},{4,5},{5,4},{6,7},{7,6},{8,33},{9,32},{10,... | collective-permute-start | bytes 786440 | tf_op jit(solution)/shard_map/ppermute | solution.py:307
  9.4 17.3 %collective-permute-start.3 = (bf16[256,128]{1,0:T(8,128)(2,1)}, bf16[256,128]{1,0:T(8,128)(2,1)S(1)}, u32[]{:S(2)}, u32[]{:S(2)}) collective-permute-start(bf16[256,128]{1,0:T(8,128)(2,1)} %param.11), channel_id=1, source_target_pairs={{0,0},{1,32},{2,64},{3,96},{4,1},{5,33},{6,65},{7,97},{8,2},{9,34}... | collective-permute-start | bytes 196616 | tf_op jit(solution)/shard_map/ppermute | solution.py:310
  13.2 73.0 %copy-start.5 = (s32[240,2]{0,1:T(2,128)S(1)}, s32[240,2]{0,1:T(2,128)}, u32[]{:S(2)}) copy-start(s32[240,2]{0,1:T(2,128)} %param.10) | copy-start | bytes 5764
  26.7 2.2 collective-permute-start.12
  27.4 1.5 collective-permute-start.11
  28.1 0.8 collective-permute-start.10
  28.8 8.5 %collective-permute-start.9 = (bf16[2,128,512]{2,1,0:T(8,128)(2,1)S(1)}, bf16[2,128,512]{2,1,0:T(8,128)(2,1)S(1)}, u32[]{:S(2)}, u32[]{:S(2)}) collective-permute-start(bf16[2,128,512]{2,1,0:T(8,128)(2,1)S(1)} %get-tuple-element.56), channel_id=1, source_target_pairs={{0,16},{1,17},{2,18},{3,19},{4,20},{5,21},{6,22},{7,23},{8,24},{9,... | collective-permute-start | bytes 786440 | tf_op jit(solution)/shard_map/ppermute | solution.py:249
  29.0 3.5 %collective-permute-start.15 = (bf16[256,256]{1,0:T(8,128)(2,1)S(1)}, bf16[256,256]{1,0:T(8,128)(2,1)S(1)}, u32[]{:S(2)}, u32[]{:S(2)}) collective-permute-start(bf16[256,256]{1,0:T(8,128)(2,1)S(1)} %add_add_fusion.2), channel_id=1, source_target_pairs={{0,6},{1,7},{8,14},{9,15},{16,22},{17,23},{24,30},{25,31}} | collective-permute-start | bytes 393224 | tf_op jit(solution)/shard_map/ppermute | solution.py:288
  29.6 4.1 %collective-permute-start.14 = (bf16[256,256]{1,0:T(8,128)(2,1)S(1)}, bf16[256,256]{1,0:T(8,128)(2,1)S(1)}, u32[]{:S(2)}, u32[]{:S(2)}) collective-permute-start(bf16[256,256]{1,0:T(8,128)(2,1)S(1)} %add_add_fusion.2), channel_id=1, source_target_pairs={{0,4},{1,5},{8,12},{9,13},{16,20},{17,21},{24,28},{25,29}} | collective-permute-start | bytes 393224 | tf_op jit(solution)/shard_map/ppermute | solution.py:288
  30.3 7.0 %collective-permute-start.13 = (bf16[256,256]{1,0:T(8,128)(2,1)S(1)}, bf16[256,256]{1,0:T(8,128)(2,1)S(1)}, u32[]{:S(2)}, u32[]{:S(2)}) collective-permute-start(bf16[256,256]{1,0:T(8,128)(2,1)S(1)} %add_add_fusion.2), channel_id=1, source_target_pairs={{0,2},{1,3},{8,10},{9,11},{16,18},{17,19},{24,26},{25,27}} | collective-permute-start | bytes 393224 | tf_op jit(solution)/shard_map/ppermute | solution.py:288
  31.0 9.1 %collective-permute-start.8 = (bf16[2,128,512]{2,1,0:T(8,128)(2,1)S(1)}, bf16[2,128,512]{2,1,0:T(8,128)(2,1)S(1)}, u32[]{:S(2)}, u32[]{:S(2)}) collective-permute-start(bf16[2,128,512]{2,1,0:T(8,128)(2,1)S(1)} %get-tuple-element.56), channel_id=1, source_target_pairs={{0,8},{1,9},{2,10},{3,11},{4,12},{5,13},{6,14},{7,15},{8,16},{9,17... | collective-permute-start | bytes 786440 | tf_op jit(solution)/shard_map/ppermute | solution.py:249
  32.5 8.3 %collective-permute-start.7 = (bf16[2,128,512]{2,1,0:T(8,128)(2,1)S(1)}, bf16[2,128,512]{2,1,0:T(8,128)(2,1)S(1)}, u32[]{:S(2)}, u32[]{:S(2)}) collective-permute-start(bf16[2,128,512]{2,1,0:T(8,128)(2,1)S(1)} %get-tuple-element.56), channel_id=1, source_target_pairs={{0,24},{1,25},{2,26},{3,27},{4,28},{5,29},{6,30},{7,31},{8,0},{9,1... | collective-permute-start | bytes 786440 | tf_op jit(solution)/shard_map/ppermute | solution.py:249
  33.7 7.8 %collective-permute-start.6 = (bf16[2,128,512]{2,1,0:T(8,128)(2,1)S(1)}, bf16[2,128,512]{2,1,0:T(8,128)(2,1)S(1)}, u32[]{:S(2)}, u32[]{:S(2)}) collective-permute-start(bf16[2,128,512]{2,1,0:T(8,128)(2,1)S(1)} %get-tuple-element.57), channel_id=1, source_target_pairs={{0,4},{1,5},{2,6},{3,7},{4,0},{5,1},{6,2},{7,3},{8,12},{9,13},{10,... | collective-permute-start | bytes 786440 | tf_op jit(solution)/shard_map/ppermute | solution.py:249
  37.3 7.0 %collective-permute-start.5 = (bf16[2,128,512]{2,1,0:T(8,128)(2,1)S(1)}, bf16[2,128,512]{2,1,0:T(8,128)(2,1)S(1)}, u32[]{:S(2)}, u32[]{:S(2)}) collective-permute-start(bf16[2,128,512]{2,1,0:T(8,128)(2,1)S(1)} %get-tuple-element.57), channel_id=1, source_target_pairs={{0,2},{1,3},{2,4},{3,5},{4,6},{5,7},{6,0},{7,1},{8,10},{9,11},{10,... | collective-permute-start | bytes 786440 | tf_op jit(solution)/shard_map/ppermute | solution.py:249
  37.3 7.4 %collective-permute-start.4 = (bf16[2,128,512]{2,1,0:T(8,128)(2,1)S(1)}, bf16[2,128,512]{2,1,0:T(8,128)(2,1)S(1)}, u32[]{:S(2)}, u32[]{:S(2)}) collective-permute-start(bf16[2,128,512]{2,1,0:T(8,128)(2,1)S(1)} %get-tuple-element.57), channel_id=1, source_target_pairs={{0,6},{1,7},{2,0},{3,1},{4,2},{5,3},{6,4},{7,5},{8,14},{9,15},{10,... | collective-permute-start | bytes 786440 | tf_op jit(solution)/shard_map/ppermute | solution.py:249
  40.1 4.7 %collective-permute-start.18 = (bf16[256,256]{1,0:T(8,128)(2,1)S(1)}, bf16[256,256]{1,0:T(8,128)(2,1)S(1)}, u32[]{:S(2)}, u32[]{:S(2)}) collective-permute-start(bf16[256,256]{1,0:T(8,128)(2,1)S(1)} %add_add_fusion.1), channel_id=1, source_target_pairs={{0,96},{1,97},{2,98},{3,99},{4,100},{5,101},{6,102},{7,103},{8,104... | collective-permute-start | bytes 393224 | tf_op jit(solution)/shard_map/ppermute | solution.py:288
  40.8 4.1 %collective-permute-start.17 = (bf16[256,256]{1,0:T(8,128)(2,1)S(1)}, bf16[256,256]{1,0:T(8,128)(2,1)S(1)}, u32[]{:S(2)}, u32[]{:S(2)}) collective-permute-start(bf16[256,256]{1,0:T(8,128)(2,1)S(1)} %add_add_fusion.1), channel_id=1, source_target_pairs={{0,64},{1,65},{2,66},{3,67},{4,68},{5,69},{6,70},{7,71},{8,72},{9,... | collective-permute-start | bytes 393224 | tf_op jit(solution)/shard_map/ppermute | solution.py:288
  41.6 15.8 %collective-permute-start.16 = (bf16[256,256]{1,0:T(8,128)(2,1)S(1)}, bf16[256,256]{1,0:T(8,128)(2,1)S(1)}, u32[]{:S(2)}, u32[]{:S(2)}) collective-permute-start(bf16[256,256]{1,0:T(8,128)(2,1)S(1)} %add_add_fusion.1), channel_id=1, source_target_pairs={{0,32},{1,33},{2,34},{3,35},{4,36},{5,37},{6,38},{7,39},{8,40},{9,... | collective-permute-start | bytes 393224 | tf_op jit(solution)/shard_map/ppermute | solution.py:288
  57.5 25.0 %collective-permute-start.21 = (bf16[8,128,512]{2,1,0:T(8,128)(2,1)S(1)}, bf16[8,128,512]{2,1,0:T(8,128)(2,1)S(1)}, u32[]{:S(2)}, u32[]{:S(2)}) collective-permute-start(bf16[8,128,512]{2,1,0:T(8,128)(2,1)S(1)} %pad_maximum_fusion.3), channel_id=1, source_target_pairs={{0,16},{1,17},{2,18},{3,19},{4,20},{5,21},{6,22},{7,23},{8,24},{9,... | collective-permute-start | bytes 3145736 | tf_op jit(solution)/shard_map/ppermute | solution.py:249
  58.4 53.1 %collective-permute-start.20 = (bf16[8,128,512]{2,1,0:T(8,128)(2,1)S(1)}, bf16[8,128,512]{2,1,0:T(8,128)(2,1)}, u32[]{:S(2)}, u32[]{:S(2)}) collective-permute-start(bf16[8,128,512]{2,1,0:T(8,128)(2,1)S(1)} %pad_maximum_fusion.3), channel_id=1, source_target_pairs={{0,8},{1,9},{2,10},{3,11},{4,12},{5,13},{6,14},{7,15},{8,16},{9,17... | collective-permute-start | bytes 3145736 | tf_op jit(solution)/shard_map/ppermute | solution.py:249
  60.6 51.0 %collective-permute-start.19 = (bf16[8,128,512]{2,1,0:T(8,128)(2,1)S(1)}, bf16[8,128,512]{2,1,0:T(8,128)(2,1)}, u32[]{:S(2)}, u32[]{:S(2)}) collective-permute-start(bf16[8,128,512]{2,1,0:T(8,128)(2,1)S(1)} %pad_maximum_fusion.3), channel_id=1, source_target_pairs={{0,24},{1,25},{2,26},{3,27},{4,28},{5,29},{6,30},{7,31},{8,0},{9,1... | collective-permute-start | bytes 3145736 | tf_op jit(solution)/shard_map/ppermute | solution.py:249
  61.1 50.5 %collective-permute-start.24 = (bf16[8,128,512]{2,1,0:T(8,128)(2,1)S(1)}, bf16[8,128,512]{2,1,0:T(8,128)(2,1)}, u32[]{:S(2)}, u32[]{:S(2)}) collective-permute-start(bf16[8,128,512]{2,1,0:T(8,128)(2,1)S(1)} %pad_maximum_fusion.4), channel_id=1, source_target_pairs={{0,4},{1,5},{2,6},{3,7},{4,0},{5,1},{6,2},{7,3},{8,12},{9,13},{10,... | collective-permute-start | bytes 3145736 | tf_op jit(solution)/shard_map/ppermute | solution.py:249
  62.2 49.4 %collective-permute-start.23 = (bf16[8,128,512]{2,1,0:T(8,128)(2,1)S(1)}, bf16[8,128,512]{2,1,0:T(8,128)(2,1)}, u32[]{:S(2)}, u32[]{:S(2)}) collective-permute-start(bf16[8,128,512]{2,1,0:T(8,128)(2,1)S(1)} %pad_maximum_fusion.4), channel_id=1, source_target_pairs={{0,2},{1,3},{2,4},{3,5},{4,6},{5,7},{6,0},{7,1},{8,10},{9,11},{10,... | collective-permute-start | bytes 3145736 | tf_op jit(solution)/shard_map/ppermute | solution.py:249
  82.5 29.1 %collective-permute-start.22 = (bf16[8,128,512]{2,1,0:T(8,128)(2,1)S(1)}, bf16[8,128,512]{2,1,0:T(8,128)(2,1)}, u32[]{:S(2)}, u32[]{:S(2)}) collective-permute-start(bf16[8,128,512]{2,1,0:T(8,128)(2,1)S(1)} %pad_maximum_fusion.4), channel_id=1, source_target_pairs={{0,6},{1,7},{2,0},{3,1},{4,2},{5,3},{6,4},{7,5},{8,14},{9,15},{10,... | collective-permute-start | bytes 3145736 | tf_op jit(solution)/shard_map/ppermute | solution.py:249
  111.6 120.2 %all-to-all-start = ((bf16[32,240,512]{2,1,0:T(8,128)(2,1)}), bf16[32,240,512]{2,1,0:T(8,128)(2,1)}, u32[]{:S(2)}, u32[]{:S(2)}) async-start(bf16[32,240,512]{2,1,0:T(8,128)(2,1)} %pack.1), calls=%async_computation | async-start | bytes 15728640 | tf_op jit(solution)/shard_map/all_to_all | solution.py:332
  118.4 4.3 %collective-permute-start.25 = (bf16[256,640]{1,0:T(8,128)(2,1)S(1)}, bf16[256,640]{1,0:T(8,128)(2,1)S(1)}, u32[]{:S(2)}, u32[]{:S(2)}) collective-permute-start(bf16[256,640]{1,0:T(8,128)(2,1)S(1)} %constant_dynamic-update-slice_fusion), channel_id=1, source_target_pairs={{0,32},{1,33},{2,34},{3,35},{4,36},{5,37},{6,38},{7,39},{8,40},{9,... | collective-permute-start | bytes 983048 | tf_op jit(solution)/shard_map/ppermute | solution.py:254
  122.8 103.2 %collective-permute-start.26 = (bf16[2,256,640]{2,1,0:T(8,128)(2,1)S(1)}, bf16[2,256,640]{2,1,0:T(8,128)(2,1)S(1)}, u32[]{:S(2)}, u32[]{:S(2)}) collective-permute-start(bf16[2,256,640]{2,1,0:T(8,128)(2,1)S(1)} %pad_maximum_fusion.5), channel_id=1, source_target_pairs={{0,64},{1,65},{2,66},{3,67},{4,68},{5,69},{6,70},{7,71},{8,72},{9,... | collective-permute-start | bytes 1966088 | tf_op jit(solution)/shard_map/ppermute | solution.py:258
  130.1 1.6 collective-permute-start.27
  131.7 94.3 %collective-permute-start.28 = (f32[4,256]{1,0:T(4,128)S(1)}, f32[4,256]{1,0:T(4,128)S(1)}, u32[]{:S(2)}, u32[]{:S(2)}) collective-permute-start(f32[4,256]{1,0:T(4,128)S(1)} %fusion), channel_id=1, source_target_pairs={{0,64},{1,65},{2,66},{3,67},{4,68},{5,69},{6,70},{7,71},{8,72},{9,... | collective-permute-start | bytes 12296 | tf_op jit(solution)/shard_map/ppermute | solution.py:351
  234.0 58.5 %all-to-all-start.1 = ((bf16[32,240,256]{2,1,0:T(8,128)(2,1)}), bf16[32,240,256]{2,1,0:T(8,128)(2,1)}, u32[]{:S(2)}, u32[]{:S(2)}) async-start(bf16[32,240,256]{2,1,0:T(8,128)(2,1)} %broadcast_in_dim.14), calls=%async_computation.1 | async-start | bytes 7864320 | tf_op jit(solution)/shard_map/all_to_all | solution.py:353
  (5 other events, 97.3 us)

commit v4 on v3

--- a/solution.py
+++ b/solution.py
@@ -191,23 +191,24 @@
     )(table, part_a, part_d, own, inv_norm, gain_rows.reshape(pieces, 1, feats), gain_own.reshape(1, feats))
 
 
-def corrected_kernel(w_ref, e_ref, p_ref, out_ref):
-    rows, feats = out_ref.shape
-    correction = jnp.dot(e_ref[...].reshape(rows, COLS), p_ref[...], preferred_element_type=jnp.float32)
-    value = w_ref[...].reshape(rows, feats).astype(jnp.float32) - correction
+def corrected_kernel(feats, both_ref, p_ref, out_ref):
+    rows = out_ref.shape[0]
+    errors = both_ref[:, :, feats:].reshape(rows, COLS)
+    correction = jnp.dot(errors, p_ref[...], preferred_element_type=jnp.float32)
+    value = both_ref[:, :, :feats].reshape(rows, feats).astype(jnp.float32) - correction
     out_ref[...] = value.astype(jnp.bfloat16)
 
 
-def corrected(moved, errors, panel):
-    shards, rows, feats = moved.shape
+def corrected(arrived, panel):
+    shards, rows, width = arrived.shape
+    feats = width - COLS
     step = 4
     return pl.pallas_call(
-        corrected_kernel,
+        functools.partial(corrected_kernel, feats),
         grid=(shards // step,),
         out_shape=jax.ShapeDtypeStruct((shards * rows, feats), jnp.bfloat16),
         in_specs=[
-            pl.BlockSpec((step, rows, feats), lambda i: (i, 0, 0)),
-            pl.BlockSpec((step, rows, COLS), lambda i: (i, 0, 0)),
+            pl.BlockSpec((step, rows, width), lambda i: (i, 0, 0)),
             pl.BlockSpec((COLS, feats), lambda i: (0, 0)),
         ],
         out_specs=pl.BlockSpec((step * rows, feats), lambda i: (i, 0)),
@@ -216,27 +217,32 @@
             flops=2 * shards * rows * feats * COLS, bytes_accessed=20 * 2**20, transcendentals=0
         ),
         name="corrected",
-    )(moved, errors, panel)
-
-
-def pack_kernel(w_ref, out_ref):
-    feats = out_ref.shape[2]
+    )(arrived, panel)
+
+
+def pack_kernel(feats, w_ref, e_ref, out_ref):
     for i in range(out_ref.shape[0]):
-        out_ref[i] = w_ref[:, i * feats : (i + 1) * feats]
-
-
-def pack(weight, feats):
+        out_ref[i, :, :feats] = w_ref[:, i * feats : (i + 1) * feats]
+        out_ref[i, :, feats:] = e_ref[...]
+
+
+def pack(weight, errors, feats):
     rows, total = weight.shape
     shards = total // feats
+    step = 2
     return pl.pallas_call(
-        pack_kernel,
-        grid=(shards // 2,),
-        out_shape=jax.ShapeDtypeStruct((shards, rows, feats), weight.dtype),
-        in_specs=[pl.BlockSpec((rows, 2 * feats), lambda i: (0, i))],
-        out_specs=pl.BlockSpec((2, rows, feats), lambda i: (i, 0, 0)),
-        cost_estimate=pl.CostEstimate(flops=0, bytes_accessed=4 * rows * total, transcendentals=0),
+        functools.partial(pack_kernel, feats),
+        grid=(shards // step,),
+        out_shape=jax.ShapeDtypeStruct((shards, rows, feats + COLS), weight.dtype),
+        in_specs=[
+            pl.BlockSpec((rows, step * feats), lambda i: (0, i)),
+            pl.BlockSpec((rows, COLS), lambda i: (0, 0)),
+        ],
+        out_specs=pl.BlockSpec((step, rows, feats + COLS), lambda i: (i, 0, 0)),
+        compiler_params=pltpu.CompilerParams(vmem_limit_bytes=16 * 2**20),
+        cost_estimate=pl.CostEstimate(flops=0, bytes_accessed=5 * rows * total, transcendentals=0),
         name="pack",
-    )(weight)
+    )(weight, errors)
 
 
 def shift(d, along_x):
@@ -324,12 +330,12 @@
     codes = jnp.pad(scale_codes.astype(jnp.float32).T, ((0, 0), (0, pad)))
     zeros = jnp.pad(zero_points.astype(jnp.float32).T, ((0, 0), (0, pad)))
     errors = block_errors(weight[:, :COLS], codes, zeros, first_panel)
-    packed = pack(weight, feats)
-    part_a, part_d, errors, packed, shard, residual = lax.optimization_barrier(
-        (part_a, part_d, errors, packed, shard, residual)
-    )
-
-    moved = lax.all_to_all(packed, "tp", split_axis=0, concat_axis=0)
+    packed = pack(weight, errors, feats)
+    part_a, part_d, packed, shard, residual = lax.optimization_barrier(
+        (part_a, part_d, packed, shard, residual)
+    )
+
+    arrived = lax.all_to_all(packed, "tp", split_axis=0, concat_axis=0)
 
     pair = beside(jnp.concatenate([residual, shard], axis=1))
     met = beyond(pair)
@@ -349,8 +355,6 @@
     )
     sums = sums + lax.ppermute(sums, ALL, moves(lambda tt, x, z, h: (tt ^ 1, x, z, h)))
     sums = sums + lax.ppermute(sums, ALL, moves(lambda tt, x, z, h: (tt ^ 2, x, z, h)))
-    copies = later(jnp.broadcast_to(errors[None], (shards, rows, COLS)), moved, met, sums)
-    errors_all = lax.all_to_all(copies, "tp", split_axis=0, concat_axis=0)
     inv_norm = lax.rsqrt(sums / feat_total + EPS)[:, :, None]
     quarter_feats = feat_total // groups
     gain_rows = lax.dynamic_slice_in_dim(norm_gain, t * quarter_feats, quarter_feats, 0)
@@ -361,7 +365,7 @@
     ).astype(jnp.int32)
     gram = mean_outer(part_a, part_d, own, inv_norm, gain_rows, gain_own, table)
 
-    return (gram, corrected(moved, errors_all, own_panel))
+    return (gram, corrected(arrived, own_panel))
 
 
 def solution(mesh):

time: 307 us -> 326 us (1.062)
  the two profiles are of different devices: /device:TPU:1 before, /device:TPU:64 now
where the time goes in v4:
time: 326 us; the launch traced here: 325 us
  waiting for transfers between devices  220 us (67%)
  starting transfers between devices  47.9 us (15%)
  Pallas kernels  34.9 us (11%)
  local copies, waits for them, and re-layouts  11.5 us (4%)
  other arithmetic  9.5 us (3%)
    ppermute x1, waiting for transfers between devices, on_device(): lax.ppermute(sums, ALL, moves(lambda tt, x, z, h: (tt ^ 2, x, z, h)))  135 us
    all_to_all x1, waiting for transfers between devices, on_device(): arrived = lax.all_to_all(packed, 'tp', split_axis=0, concat_axis=0)  34.7 us
    ppermute x12, waiting for transfers between devices, ring(): others = [lax.ppermute(block, ALL, shift(-d, along_x)) for d in RING[1:]]  27 us
    ppermute x12, starting transfers between devices, ring(): others = [lax.ppermute(block, ALL, shift(-d, along_x)) for d in RING[1:]]  16.8 us
    pallas_call x1, Pallas kernels, block_errors(): pl.pallas_call(errors_kernel, grid=(1,), out_shape=jax.ShapeDtypeStruct((...  12.8 us
    ppermute x10, waiting for transfers between devices, spread(): lax.ppermute(held, ALL, perm)  11.3 us
    pallas_call x1, Pallas kernels, corrected(): pl.pallas_call(functools.partial(corrected_kernel, feats), grid=(shards /...  10.8 us
    pallas_call x1, Pallas kernels, mean_outer(): pl.pallas_call(functools.partial(gram_kernel, groups * toks), grid_spec=s...  9.63 us
  transfers between devices with their start and end apart: 30, of which 13 were waited for; matrix products, arithmetic and copies ran while one was open for 3% of the time, Pallas kernels for 7%

profile of v4, /device:TPU:64, one launch (start us, length us, event | category | flops | bytes accessed | tf_op | source)
XLA Modules:
  0.0 325.1 jit_solution(13071536314046362958)
XLA Ops:
  2.2 1.6 collective-permute-start
  3.8 3.2 collective-permute-start.1
  7.0 5.8 %collective-permute-start.3 = (bf16[256,128]{1,0:T(8,128)(2,1)}, bf16[256,128]{1,0:T(8,128)(2,1)S(1)}, u32[]{:S(2)}, u32[]{:S(2)}) collective-permute-start(bf16[256,128]{1,0:T(8,128)(2,1)} %param.11), channel_id=1, source_target_pairs={{0,0},{1,32},{2,64},{3,96},{4,1},{5,33},{6,65},{7,97},{8,2},{9,34}... | collective-permute-start | bytes 196616 | tf_op jit(solution)/shard_map/ppermute | solution.py:316
  12.9 8.2 %collective-permute-done.1 = bf16[256,512]{1,0:T(8,128)(2,1)S(1)} collective-permute-done((bf16[256,512]{1,0:T(8,128)(2,1)}, bf16[256,512]{1,0:T(8,128)(2,1)S(1)}, u32[]{:S(2)}, u32[]{:S(2)}) %collective-permute-start.1) | collective-permute-done | bytes 262176 | tf_op jit(solution)/shard_map/ppermute | solution.py:313
  21.1 1.4 collective-permute-done.3
  24.5 2.0 collective-permute-start.9
  27.2 1.3 collective-permute-start.14
  29.2 2.9 collective-permute-start.8
  32.5 11.3 %collective-permute-done.14 = bf16[256,256]{1,0:T(8,128)(2,1)S(1)} collective-permute-done((bf16[256,256]{1,0:T(8,128)(2,1)S(1)}, bf16[256,256]{1,0:T(8,128)(2,1)S(1)}, u32[]{:S(2)}, u32[]{:S(2)}) %collective-permute-start.14) | collective-permute-done | bytes 131104 | tf_op jit(solution)/shard_map/ppermute | solution.py:294
  43.9 1.3 collective-permute-start.6
  45.2 1.6 collective-permute-start.5
  46.8 1.5 collective-permute-start.4
  48.3 1.3 collective-permute-start.18
  49.6 1.3 collective-permute-start.17
  51.8 1.3 collective-permute-start.16
  53.1 1.4 collective-permute-done.5
  54.8 3.0 collective-permute-start.20
  58.1 2.5 collective-permute-start.24
  61.2 21.2 %collective-permute-done.21 = bf16[8,128,512]{2,1,0:T(8,128)(2,1)S(1)} collective-permute-done((bf16[8,128,512]{2,1,0:T(8,128)(2,1)S(1)}, bf16[8,128,512]{2,1,0:T(8,128)(2,1)S(1)}, u32[]{:S(2)}, u32[]{:S(2)}) %collective-permute-start.21) | collective-permute-done | bytes 1048608 | tf_op jit(solution)/shard_map/ppermute | solution.py:255
  84.3 12.8 %errors.1.e_ref = bf16[240,256]{1,0:T(8,128)(2,1)S(1)} custom-call(bf16[240,256]{1,0:T(8,128)(2,1)S(1)} %slice.26.w_ref, f32[2,256]{1,0:T(2,128)S(1)} %pad.7.codes_ref, f32[2,256]{1,0:T(2,128)S(1)} %pad.8.zeros_ref, bf16[256,256]{1,0:T(8,128)(2,1)S(1)} %add_add_fusion.p_ref), custom_call_target="tpu_custom_call" | custom-call | flops 10000000 | bytes 1000000 | tf_op jit(solution)/shard_map/errors/pallas_call | solution.py:120
  97.1 1.6 pack.1
  98.8 4.3 %copy-done = bf16[32,240,768]{2,1,0:T(8,128)(2,1)} copy-done((bf16[32,240,768]{2,1,0:T(8,128)(2,1)}, bf16[32,240,768]{2,1,0:T(8,128)(2,1)S(1)}, u32[]{:S(2)}) %copy-start) | copy-done | bytes 11796504
  103.8 2.9 collective-permute-done.23
  107.7 9.0 %all-to-all-start = ((bf16[32,240,768]{2,1,0:T(8,128)(2,1)}), bf16[32,240,768]{2,1,0:T(8,128)(2,1)}, u32[]{:S(2)}, u32[]{:S(2)}) async-start(bf16[32,240,768]{2,1,0:T(8,128)(2,1)} %copy-done), calls=%async_computation | async-start | bytes 23592960 | tf_op jit(solution)/shard_map/all_to_all | solution.py:338
  116.9 1.6 collective-permute-done.25
  119.4 7.0 %multiply_reduce_fusion = (f32[4,128]{1,0:T(4,128)S(1)}, bf16[4,4,2,128,512]{4,3,2,1,0:T(8,128)(2,1)}, f32[4,128]{1,0:T(4,128)S(1)}, bf16[4,4,2,128,512]{4,3,2,1,0:T(8,128)(2,1)}) fusion(bf16[1,4,2,128,512]{4,3,2,1,0:T(8,128)(2,1)} %bitcast.51, bf16[1,4,2,128,512]{4,3,2,1,0:T(8,128)(2,1)} %bitcast.52, bf16[1,4,2,128,512]{4,3,2,1,0:T(8,128)(2,1)} %bitcast.21, ...), kind=kLoop, calls=%fused_computation | loop fusion | flops 25164800 | bytes 16781312 | tf_op jit(solution)/shard_map/reduce_sum | solution.py:352
  127.7 2.0 collective-permute-start.28
  131.3 135.1 %collective-permute-done.28 = f32[4,256]{1,0:T(4,128)S(1)} collective-permute-done((f32[4,256]{1,0:T(4,128)S(1)}, f32[4,256]{1,0:T(4,128)S(1)}, u32[]{:S(2)}, u32[]{:S(2)}) %collective-permute-start.28) | collective-permute-done | bytes 4128 | tf_op jit(solution)/shard_map/ppermute | solution.py:357
  267.1 1.7 copy-done.1
  270.1 9.6 %mean_outer.1 = f32[4096,512]{1,0:T(8,128)} custom-call(s32[12]{0:T(128)S(1)} %stack.99.table, bf16[4,4,2,128,512]{4,3,2,1,0:T(8,128)(2,1)S(1)} %copy-done.2, bf16[4,4,2,128,512]{4,3,2,1,0:T(8,128)(2,1)S(1)} %copy-done.1, bf16[4,256,512]{2,1,0:T(8,128)(2,1)S(1)} %slice.32.own_ref, f32[4,256,1]{2,1,0:T(8,128)S(1)} %copy.8.inv_ref, f32[8,1,512]{2,1,0:T(1,128)S(1)} %bitcast.40, ...), custom_call_target="tpu_custom_call" | custom-call | flops 4294967296 | bytes 20971520 | tf_op jit(solution)/shard_map/mean_outer/pallas_call | solution.py:180
  279.7 34.7 %all-to-all-done.both_ref = bf16[32,240,768]{2,1,0:T(8,128)(2,1)} async-done(((bf16[32,240,768]{2,1,0:T(8,128)(2,1)}), bf16[32,240,768]{2,1,0:T(8,128)(2,1)}, u32[]{:S(2)}, u32[]{:S(2)}) %all-to-all-start) | async-done | bytes 11796512 | tf_op jit(solution)/shard_map/all_to_all | solution.py:338
  314.4 10.8 %corrected.1 = bf16[7680,512]{1,0:T(8,128)(2,1)} custom-call(bf16[32,240,768]{2,1,0:T(8,128)(2,1)} %all-to-all-done.both_ref, bf16[256,512]{1,0:T(8,128)(2,1)S(1)} %pad_maximum_fusion.7.p_ref), custom_call_target="tpu_custom_call" | custom-call | flops 2013265920 | bytes 20971520 | tf_op jit(solution)/shard_map/corrected/pallas_call | solution.py:206
  (90 shorter events, 16.8 us)
Async XLA Ops:
  1.5 11.3 %collective-permute-start.2 = (bf16[256,256]{1,0:T(8,128)(2,1)S(1)}, bf16[256,256]{1,0:T(8,128)(2,1)S(1)}, u32[]{:S(2)}, u32[]{:S(2)}) collective-permute-start(bf16[256,256]{1,0:T(8,128)(2,1)S(1)} %pad_maximum_fusion.8), channel_id=1, source_target_pairs={{0,1},{1,0}} | collective-permute-start | bytes 393224 | tf_op jit(solution)/shard_map/ppermute | solution.py:294
  2.2 10.7 %collective-permute-start = (bf16[256,512]{1,0:T(8,128)(2,1)}, bf16[256,512]{1,0:T(8,128)(2,1)S(1)}, u32[]{:S(2)}, u32[]{:S(2)}) collective-permute-start(bf16[256,512]{1,0:T(8,128)(2,1)} %param.6), channel_id=1, source_target_pairs={{0,0},{1,1},{2,2},{3,3},{4,4},{5,5},{6,6},{7,7},{8,32},{9,33},{10,... | collective-permute-start | bytes 786440 | tf_op jit(solution)/shard_map/ppermute | solution.py:312
  3.8 17.2 %collective-permute-start.1 = (bf16[256,512]{1,0:T(8,128)(2,1)}, bf16[256,512]{1,0:T(8,128)(2,1)S(1)}, u32[]{:S(2)}, u32[]{:S(2)}) collective-permute-start(bf16[256,512]{1,0:T(8,128)(2,1)} %param.6), channel_id=1, source_target_pairs={{0,1},{1,0},{2,3},{3,2},{4,5},{5,4},{6,7},{7,6},{8,33},{9,32},{10,... | collective-permute-start | bytes 786440 | tf_op jit(solution)/shard_map/ppermute | solution.py:313
  7.0 15.5 %collective-permute-start.3 = (bf16[256,128]{1,0:T(8,128)(2,1)}, bf16[256,128]{1,0:T(8,128)(2,1)S(1)}, u32[]{:S(2)}, u32[]{:S(2)}) collective-permute-start(bf16[256,128]{1,0:T(8,128)(2,1)} %param.11), channel_id=1, source_target_pairs={{0,0},{1,32},{2,64},{3,96},{4,1},{5,33},{6,65},{7,97},{8,2},{9,34}... | collective-permute-start | bytes 196616 | tf_op jit(solution)/shard_map/ppermute | solution.py:316
  12.8 71.4 %copy-start.11 = (s32[240,2]{0,1:T(2,128)S(1)}, s32[240,2]{0,1:T(2,128)}, u32[]{:S(2)}) copy-start(s32[240,2]{0,1:T(2,128)} %param.10) | copy-start | bytes 5764
  12.9 71.4 %copy-start.3 = (bf16[240,16384]{1,0:T(8,128)(2,1)S(1)}, bf16[240,16384]{1,0:T(8,128)(2,1)}, u32[]{:S(2)}) copy-start(bf16[240,16384]{1,0:T(8,128)(2,1)} %w_ref) | copy-start | bytes 23592964
  22.5 4.0 %collective-permute-start.12 = (bf16[256,256]{1,0:T(8,128)(2,1)S(1)}, bf16[256,256]{1,0:T(8,128)(2,1)S(1)}, u32[]{:S(2)}, u32[]{:S(2)}) collective-permute-start(bf16[256,256]{1,0:T(8,128)(2,1)S(1)} %fusion.1), channel_id=1, source_target_pairs={{0,24},{1,25}} | collective-permute-start | bytes 393224 | tf_op jit(solution)/shard_map/ppermute | solution.py:294
  23.2 3.4 %collective-permute-start.11 = (bf16[256,256]{1,0:T(8,128)(2,1)S(1)}, bf16[256,256]{1,0:T(8,128)(2,1)S(1)}, u32[]{:S(2)}, u32[]{:S(2)}) collective-permute-start(bf16[256,256]{1,0:T(8,128)(2,1)S(1)} %fusion.1), channel_id=1, source_target_pairs={{0,16},{1,17}} | collective-permute-start | bytes 393224 | tf_op jit(solution)/shard_map/ppermute | solution.py:294
  23.8 2.7 collective-permute-start.10
  24.5 22.2 %collective-permute-start.9 = (bf16[2,128,512]{2,1,0:T(8,128)(2,1)S(1)}, bf16[2,128,512]{2,1,0:T(8,128)(2,1)S(1)}, u32[]{:S(2)}, u32[]{:S(2)}) collective-permute-start(bf16[2,128,512]{2,1,0:T(8,128)(2,1)S(1)} %get-tuple-element.50), channel_id=1, source_target_pairs={{0,16},{1,17},{2,18},{3,19},{4,20},{5,21},{6,22},{7,23},{8,24},{9,... | collective-permute-start | bytes 786440 | tf_op jit(solution)/shard_map/ppermute | solution.py:255
  26.6 5.6 %collective-permute-start.15 = (bf16[256,256]{1,0:T(8,128)(2,1)S(1)}, bf16[256,256]{1,0:T(8,128)(2,1)S(1)}, u32[]{:S(2)}, u32[]{:S(2)}) collective-permute-start(bf16[256,256]{1,0:T(8,128)(2,1)S(1)} %add_add_fusion.2), channel_id=1, source_target_pairs={{0,6},{1,7},{8,14},{9,15},{16,22},{17,23},{24,30},{25,31}} | collective-permute-start | bytes 393224 | tf_op jit(solution)/shard_map/ppermute | solution.py:294
  27.2 16.6 %collective-permute-start.14 = (bf16[256,256]{1,0:T(8,128)(2,1)S(1)}, bf16[256,256]{1,0:T(8,128)(2,1)S(1)}, u32[]{:S(2)}, u32[]{:S(2)}) collective-permute-start(bf16[256,256]{1,0:T(8,128)(2,1)S(1)} %add_add_fusion.2), channel_id=1, source_target_pairs={{0,4},{1,5},{8,12},{9,13},{16,20},{17,21},{24,28},{25,29}} | collective-permute-start | bytes 393224 | tf_op jit(solution)/shard_map/ppermute | solution.py:294
  28.5 16.6 %collective-permute-start.13 = (bf16[256,256]{1,0:T(8,128)(2,1)S(1)}, bf16[256,256]{1,0:T(8,128)(2,1)S(1)}, u32[]{:S(2)}, u32[]{:S(2)}) collective-permute-start(bf16[256,256]{1,0:T(8,128)(2,1)S(1)} %add_add_fusion.2), channel_id=1, source_target_pairs={{0,2},{1,3},{8,10},{9,11},{16,18},{17,19},{24,26},{25,27}} | collective-permute-start | bytes 393224 | tf_op jit(solution)/shard_map/ppermute | solution.py:294
  29.2 19.0 %collective-permute-start.8 = (bf16[2,128,512]{2,1,0:T(8,128)(2,1)S(1)}, bf16[2,128,512]{2,1,0:T(8,128)(2,1)S(1)}, u32[]{:S(2)}, u32[]{:S(2)}) collective-permute-start(bf16[2,128,512]{2,1,0:T(8,128)(2,1)S(1)} %get-tuple-element.50), channel_id=1, source_target_pairs={{0,8},{1,9},{2,10},{3,11},{4,12},{5,13},{6,14},{7,15},{8,16},{9,17... | collective-permute-start | bytes 786440 | tf_op jit(solution)/shard_map/ppermute | solution.py:255
  32.2 17.4 %collective-permute-start.7 = (bf16[2,128,512]{2,1,0:T(8,128)(2,1)S(1)}, bf16[2,128,512]{2,1,0:T(8,128)(2,1)S(1)}, u32[]{:S(2)}, u32[]{:S(2)}) collective-permute-start(bf16[2,128,512]{2,1,0:T(8,128)(2,1)S(1)} %get-tuple-element.50), channel_id=1, source_target_pairs={{0,24},{1,25},{2,26},{3,27},{4,28},{5,29},{6,30},{7,31},{8,0},{9,1... | collective-permute-start | bytes 786440 | tf_op jit(solution)/shard_map/ppermute | solution.py:255
  43.9 8.0 %collective-permute-start.6 = (bf16[2,128,512]{2,1,0:T(8,128)(2,1)S(1)}, bf16[2,128,512]{2,1,0:T(8,128)(2,1)S(1)}, u32[]{:S(2)}, u32[]{:S(2)}) collective-permute-start(bf16[2,128,512]{2,1,0:T(8,128)(2,1)S(1)} %get-tuple-element.51), channel_id=1, source_target_pairs={{0,4},{1,5},{2,6},{3,7},{4,0},{5,1},{6,2},{7,3},{8,12},{9,13},{10,... | collective-permute-start | bytes 786440 | tf_op jit(solution)/shard_map/ppermute | solution.py:255
  45.2 9.4 %collective-permute-start.5 = (bf16[2,128,512]{2,1,0:T(8,128)(2,1)S(1)}, bf16[2,128,512]{2,1,0:T(8,128)(2,1)S(1)}, u32[]{:S(2)}, u32[]{:S(2)}) collective-permute-start(bf16[2,128,512]{2,1,0:T(8,128)(2,1)S(1)} %get-tuple-element.51), channel_id=1, source_target_pairs={{0,2},{1,3},{2,4},{3,5},{4,6},{5,7},{6,0},{7,1},{8,10},{9,11},{10,... | collective-permute-start | bytes 786440 | tf_op jit(solution)/shard_map/ppermute | solution.py:255
  46.8 7.8 %collective-permute-start.4 = (bf16[2,128,512]{2,1,0:T(8,128)(2,1)S(1)}, bf16[2,128,512]{2,1,0:T(8,128)(2,1)S(1)}, u32[]{:S(2)}, u32[]{:S(2)}) collective-permute-start(bf16[2,128,512]{2,1,0:T(8,128)(2,1)S(1)} %get-tuple-element.51), channel_id=1, source_target_pairs={{0,6},{1,7},{2,0},{3,1},{4,2},{5,3},{6,4},{7,5},{8,14},{9,15},{10,... | collective-permute-start | bytes 786440 | tf_op jit(solution)/shard_map/ppermute | solution.py:255
  48.3 6.4 %collective-permute-start.18 = (bf16[256,256]{1,0:T(8,128)(2,1)S(1)}, bf16[256,256]{1,0:T(8,128)(2,1)S(1)}, u32[]{:S(2)}, u32[]{:S(2)}) collective-permute-start(bf16[256,256]{1,0:T(8,128)(2,1)S(1)} %add_add_fusion.1), channel_id=1, source_target_pairs={{0,96},{1,97},{2,98},{3,99},{4,100},{5,101},{6,102},{7,103},{8,104... | collective-permute-start | bytes 393224 | tf_op jit(solution)/shard_map/ppermute | solution.py:294
  49.6 5.1 %collective-permute-start.17 = (bf16[256,256]{1,0:T(8,128)(2,1)S(1)}, bf16[256,256]{1,0:T(8,128)(2,1)S(1)}, u32[]{:S(2)}, u32[]{:S(2)}) collective-permute-start(bf16[256,256]{1,0:T(8,128)(2,1)S(1)} %add_add_fusion.1), channel_id=1, source_target_pairs={{0,64},{1,65},{2,66},{3,67},{4,68},{5,69},{6,70},{7,71},{8,72},{9,... | collective-permute-start | bytes 393224 | tf_op jit(solution)/shard_map/ppermute | solution.py:294
  51.8 2.9 collective-permute-start.16
  54.7 27.7 %collective-permute-start.21 = (bf16[8,128,512]{2,1,0:T(8,128)(2,1)S(1)}, bf16[8,128,512]{2,1,0:T(8,128)(2,1)S(1)}, u32[]{:S(2)}, u32[]{:S(2)}) collective-permute-start(bf16[8,128,512]{2,1,0:T(8,128)(2,1)S(1)} %pad_maximum_fusion.3), channel_id=1, source_target_pairs={{0,16},{1,17},{2,18},{3,19},{4,20},{5,21},{6,22},{7,23},{8,24},{9,... | collective-permute-start | bytes 3145736 | tf_op jit(solution)/shard_map/ppermute | solution.py:255
  54.8 48.6 %collective-permute-start.20 = (bf16[8,128,512]{2,1,0:T(8,128)(2,1)S(1)}, bf16[8,128,512]{2,1,0:T(8,128)(2,1)S(1)}, u32[]{:S(2)}, u32[]{:S(2)}) collective-permute-start(bf16[8,128,512]{2,1,0:T(8,128)(2,1)S(1)} %pad_maximum_fusion.3), channel_id=1, source_target_pairs={{0,8},{1,9},{2,10},{3,11},{4,12},{5,13},{6,14},{7,15},{8,16},{9,17... | collective-permute-start | bytes 3145736 | tf_op jit(solution)/shard_map/ppermute | solution.py:255
  57.8 45.9 %collective-permute-start.19 = (bf16[8,128,512]{2,1,0:T(8,128)(2,1)S(1)}, bf16[8,128,512]{2,1,0:T(8,128)(2,1)S(1)}, u32[]{:S(2)}, u32[]{:S(2)}) collective-permute-start(bf16[8,128,512]{2,1,0:T(8,128)(2,1)S(1)} %pad_maximum_fusion.3), channel_id=1, source_target_pairs={{0,24},{1,25},{2,26},{3,27},{4,28},{5,29},{6,30},{7,31},{8,0},{9,1... | collective-permute-start | bytes 3145736 | tf_op jit(solution)/shard_map/ppermute | solution.py:255
  58.1 45.6 %collective-permute-start.24 = (bf16[8,128,512]{2,1,0:T(8,128)(2,1)S(1)}, bf16[8,128,512]{2,1,0:T(8,128)(2,1)S(1)}, u32[]{:S(2)}, u32[]{:S(2)}) collective-permute-start(bf16[8,128,512]{2,1,0:T(8,128)(2,1)S(1)} %pad_maximum_fusion.4), channel_id=1, source_target_pairs={{0,4},{1,5},{2,6},{3,7},{4,0},{5,1},{6,2},{7,3},{8,12},{9,13},{10,... | collective-permute-start | bytes 3145736 | tf_op jit(solution)/shard_map/ppermute | solution.py:255
  60.6 46.0 %collective-permute-start.23 = (bf16[8,128,512]{2,1,0:T(8,128)(2,1)S(1)}, bf16[8,128,512]{2,1,0:T(8,128)(2,1)S(1)}, u32[]{:S(2)}, u32[]{:S(2)}) collective-permute-start(bf16[8,128,512]{2,1,0:T(8,128)(2,1)S(1)} %pad_maximum_fusion.4), channel_id=1, source_target_pairs={{0,2},{1,3},{2,4},{3,5},{4,6},{5,7},{6,0},{7,1},{8,10},{9,11},{10,... | collective-permute-start | bytes 3145736 | tf_op jit(solution)/shard_map/ppermute | solution.py:255
  83.5 24.2 %collective-permute-start.22 = (bf16[8,128,512]{2,1,0:T(8,128)(2,1)S(1)}, bf16[8,128,512]{2,1,0:T(8,128)(2,1)}, u32[]{:S(2)}, u32[]{:S(2)}) collective-permute-start(bf16[8,128,512]{2,1,0:T(8,128)(2,1)S(1)} %pad_maximum_fusion.4), channel_id=1, source_target_pairs={{0,6},{1,7},{2,0},{3,1},{4,2},{5,3},{6,4},{7,5},{8,14},{9,15},{10,... | collective-permute-start | bytes 3145736 | tf_op jit(solution)/shard_map/ppermute | solution.py:255
  107.7 206.7 %all-to-all-start = ((bf16[32,240,768]{2,1,0:T(8,128)(2,1)}), bf16[32,240,768]{2,1,0:T(8,128)(2,1)}, u32[]{:S(2)}, u32[]{:S(2)}) async-start(bf16[32,240,768]{2,1,0:T(8,128)(2,1)} %copy-done), calls=%async_computation | async-start | bytes 23592960 | tf_op jit(solution)/shard_map/all_to_all | solution.py:338
  116.8 1.7 collective-permute-start.25
  119.4 147.2 %collective-permute-start.26 = (bf16[2,256,640]{2,1,0:T(8,128)(2,1)}, bf16[2,256,640]{2,1,0:T(8,128)(2,1)S(1)}, u32[]{:S(2)}, u32[]{:S(2)}) collective-permute-start(bf16[2,256,640]{2,1,0:T(8,128)(2,1)} %pad_maximum_fusion.5), channel_id=1, source_target_pairs={{0,64},{1,65},{2,66},{3,67},{4,68},{5,69},{6,70},{7,71},{8,72},{9,... | collective-permute-start | bytes 1966088 | tf_op jit(solution)/shard_map/ppermute | solution.py:264
  126.4 1.2 collective-permute-start.27
  127.7 138.6 %collective-permute-start.28 = (f32[4,256]{1,0:T(4,128)S(1)}, f32[4,256]{1,0:T(4,128)S(1)}, u32[]{:S(2)}, u32[]{:S(2)}) collective-permute-start(f32[4,256]{1,0:T(4,128)S(1)} %fusion), channel_id=1, source_target_pairs={{0,64},{1,65},{2,66},{3,67},{4,68},{5,69},{6,70},{7,71},{8,72},{9,... | collective-permute-start | bytes 12296 | tf_op jit(solution)/shard_map/ppermute | solution.py:357
  (10 other events, 106.2 us)

commit v5 on v3

--- a/solution.py
+++ b/solution.py
@@ -320,16 +320,14 @@
     part_a = ring(part_a, True)
     part_d = ring(part_d, False)
 
+    packed, part_a, part_d, first_panel, shard, residual = lax.optimization_barrier(
+        (pack(weight, feats), part_a, part_d, first_panel, shard, residual)
+    )
+    moved = lax.all_to_all(packed, "tp", split_axis=0, concat_axis=0)
     pad = -(-rows // 128) * 128 - rows
     codes = jnp.pad(scale_codes.astype(jnp.float32).T, ((0, 0), (0, pad)))
     zeros = jnp.pad(zero_points.astype(jnp.float32).T, ((0, 0), (0, pad)))
     errors = block_errors(weight[:, :COLS], codes, zeros, first_panel)
-    packed = pack(weight, feats)
-    part_a, part_d, errors, packed, shard, residual = lax.optimization_barrier(
-        (part_a, part_d, errors, packed, shard, residual)
-    )
-
-    moved = lax.all_to_all(packed, "tp", split_axis=0, concat_axis=0)
 
     pair = beside(jnp.concatenate([residual, shard], axis=1))
     met = beyond(pair)

time: 307 us -> 311 us (1.013)
  waiting for transfers between devices: 182 us -> 189 us
  starting transfers between devices: 56.7 us -> 51.5 us
    ppermute x12, waiting for transfers between devices: 20.5 us -> 33.1 us  [ring(): others = [lax.ppermute(block, ALL, shift(-d, along_x)) for d in RING[1:]]]
    ppermute x1, waiting for transfers between devices: 93.3 us -> 83.6 us  [on_device(): lax.ppermute(sums, ALL, moves(lambda tt, x, z, h: (tt ^ 2, x, z, h)))]
    all_to_all x1, waiting for transfers between devices: 5.65 us -> 11.6 us  [on_device(): moved = lax.all_to_all(packed, 'tp', split_axis=0, concat_axis=0)]
    all_to_all x1, starting transfers between devices: 8.29 us -> 4.83 us  [on_device(): errors_all = lax.all_to_all(copies, 'tp', split_axis=0, concat_axis=0)]
  transfers between devices with their start and end apart: 31 -> 31, of which waited for: 12 -> 13; matrix products, arithmetic and copies ran while one was open for 4% -> 4% of each run, Pallas kernels for 11% -> 11%
where the time goes in v5:
time: 311 us; the launch traced here: 305 us
  waiting for transfers between devices  189 us (61%)
  starting transfers between devices  51.5 us (17%)
  Pallas kernels  44.7 us (14%)
  local copies, waits for them, and re-layouts  10.1 us (3%)
  other arithmetic  8.4 us (3%)
    ppermute x1, waiting for transfers between devices, on_device(): lax.ppermute(sums, ALL, moves(lambda tt, x, z, h: (tt ^ 2, x, z, h)))  83.6 us
    all_to_all x1, waiting for transfers between devices, on_device(): errors_all = lax.all_to_all(copies, 'tp', split_axis=0, concat_axis=0)  33.9 us
    ppermute x12, waiting for transfers between devices, ring(): others = [lax.ppermute(block, ALL, shift(-d, along_x)) for d in RING[1:]]  33.1 us
    ppermute x12, starting transfers between devices, ring(): others = [lax.ppermute(block, ALL, shift(-d, along_x)) for d in RING[1:]]  19 us
    pallas_call x1, Pallas kernels, block_errors(): pl.pallas_call(errors_kernel, grid=(1,), out_shape=jax.ShapeDtypeStruct((...  12.8 us
    ppermute x10, waiting for transfers between devices, spread(): lax.ppermute(held, ALL, perm)  12.6 us
    pallas_call x1, Pallas kernels, pack(): pl.pallas_call(pack_kernel, grid=(shards // 2,), out_shape=jax.ShapeDtype...  11.6 us
    all_to_all x1, waiting for transfers between devices, on_device(): moved = lax.all_to_all(packed, 'tp', split_axis=0, concat_axis=0)  11.6 us
  transfers between devices with their start and end apart: 31, of which 13 were waited for; matrix products, arithmetic and copies ran while one was open for 4% of the time, Pallas kernels for 11%

profile of v5, /device:TPU:1, one launch (start us, length us, event | category | flops | bytes accessed | tf_op | source)
XLA Modules:
  0.0 305.2 jit_solution(13134416714268571162)
XLA Ops:
  2.2 4.5 %collective-permute-start = (bf16[256,512]{1,0:T(8,128)(2,1)}, bf16[256,512]{1,0:T(8,128)(2,1)S(1)}, u32[]{:S(2)}, u32[]{:S(2)}) collective-permute-start(bf16[256,512]{1,0:T(8,128)(2,1)} %param.6), channel_id=1, source_target_pairs={{0,0},{1,1},{2,2},{3,3},{4,4},{5,5},{6,6},{7,7},{8,32},{9,33},{10,... | collective-permute-start | bytes 786440 | tf_op jit(solution)/shard_map/ppermute | solution.py:306
  6.7 2.7 collective-permute-start.1
  9.4 3.6 %collective-permute-start.3 = (bf16[256,128]{1,0:T(8,128)(2,1)}, bf16[256,128]{1,0:T(8,128)(2,1)S(1)}, u32[]{:S(2)}, u32[]{:S(2)}) collective-permute-start(bf16[256,128]{1,0:T(8,128)(2,1)} %param.11), channel_id=1, source_target_pairs={{0,0},{1,32},{2,64},{3,96},{4,1},{5,33},{6,65},{7,97},{8,2},{9,34}... | collective-permute-start | bytes 196616 | tf_op jit(solution)/shard_map/ppermute | solution.py:310
  13.2 6.2 %collective-permute-done.1 = bf16[256,512]{1,0:T(8,128)(2,1)S(1)} collective-permute-done((bf16[256,512]{1,0:T(8,128)(2,1)}, bf16[256,512]{1,0:T(8,128)(2,1)S(1)}, u32[]{:S(2)}, u32[]{:S(2)}) %collective-permute-start.1) | collective-permute-done | bytes 262176 | tf_op jit(solution)/shard_map/ppermute | solution.py:307
  19.4 7.3 %collective-permute-done.3 = bf16[256,128]{1,0:T(8,128)(2,1)S(1)} collective-permute-done((bf16[256,128]{1,0:T(8,128)(2,1)}, bf16[256,128]{1,0:T(8,128)(2,1)S(1)}, u32[]{:S(2)}, u32[]{:S(2)}) %collective-permute-start.3) | collective-permute-done | bytes 65568 | tf_op jit(solution)/shard_map/ppermute | solution.py:310
  31.0 1.5 collective-permute-start.8
  32.5 1.3 collective-permute-start.7
  33.7 3.5 %collective-permute-start.6 = (bf16[2,128,512]{2,1,0:T(8,128)(2,1)S(1)}, bf16[2,128,512]{2,1,0:T(8,128)(2,1)S(1)}, u32[]{:S(2)}, u32[]{:S(2)}) collective-permute-start(bf16[2,128,512]{2,1,0:T(8,128)(2,1)S(1)} %get-tuple-element.57), channel_id=1, source_target_pairs={{0,4},{1,5},{2,6},{3,7},{4,0},{5,1},{6,2},{7,3},{8,12},{9,13},{10,... | collective-permute-start | bytes 786440 | tf_op jit(solution)/shard_map/ppermute | solution.py:249
  37.3 2.7 collective-permute-start.4
  41.6 1.3 collective-permute-start.16
  42.9 1.4 collective-permute-done.5
  44.8 12.6 %collective-permute-done.16 = bf16[256,256]{1,0:T(8,128)(2,1)S(1)} collective-permute-done((bf16[256,256]{1,0:T(8,128)(2,1)S(1)}, bf16[256,256]{1,0:T(8,128)(2,1)S(1)}, u32[]{:S(2)}, u32[]{:S(2)}) %collective-permute-start.16) | collective-permute-done | bytes 131104 | tf_op jit(solution)/shard_map/ppermute | solution.py:288
  58.4 2.2 collective-permute-start.20
  62.2 1.6 collective-permute-start.23
  63.8 18.6 %collective-permute-done.21 = bf16[8,128,512]{2,1,0:T(8,128)(2,1)S(1)} collective-permute-done((bf16[8,128,512]{2,1,0:T(8,128)(2,1)S(1)}, bf16[8,128,512]{2,1,0:T(8,128)(2,1)S(1)}, u32[]{:S(2)}, u32[]{:S(2)}) %collective-permute-start.21) | collective-permute-done | bytes 1048608 | tf_op jit(solution)/shard_map/ppermute | solution.py:249
  82.5 3.6 %collective-permute-start.22 = (bf16[8,128,512]{2,1,0:T(8,128)(2,1)S(1)}, bf16[8,128,512]{2,1,0:T(8,128)(2,1)}, u32[]{:S(2)}, u32[]{:S(2)}) collective-permute-start(bf16[8,128,512]{2,1,0:T(8,128)(2,1)S(1)} %pad_maximum_fusion.4), channel_id=1, source_target_pairs={{0,6},{1,7},{2,0},{3,1},{4,2},{5,3},{6,4},{7,5},{8,14},{9,15},{10,... | collective-permute-start | bytes 3145736 | tf_op jit(solution)/shard_map/ppermute | solution.py:249
  86.1 11.6 %pack.1 = bf16[32,240,512]{2,1,0:T(8,128)(2,1)} custom-call(bf16[240,16384]{1,0:T(8,128)(2,1)} %w_ref), custom_call_target="tpu_custom_call" | custom-call | bytes 15728640 | tf_op jit(solution)/shard_map/pack/pallas_call | solution.py:231
  97.7 9.0 %collective-permute-done.20 = bf16[8,128,512]{2,1,0:T(8,128)(2,1)} collective-permute-done((bf16[8,128,512]{2,1,0:T(8,128)(2,1)S(1)}, bf16[8,128,512]{2,1,0:T(8,128)(2,1)}, u32[]{:S(2)}, u32[]{:S(2)}) %collective-permute-start.20) | collective-permute-done | bytes 1048608 | tf_op jit(solution)/shard_map/ppermute | solution.py:249
  106.7 3.6 %collective-permute-done.23 = bf16[8,128,512]{2,1,0:T(8,128)(2,1)} collective-permute-done((bf16[8,128,512]{2,1,0:T(8,128)(2,1)S(1)}, bf16[8,128,512]{2,1,0:T(8,128)(2,1)}, u32[]{:S(2)}, u32[]{:S(2)}) %collective-permute-start.23) | collective-permute-done | bytes 1048608 | tf_op jit(solution)/shard_map/ppermute | solution.py:249
  110.3 6.7 %all-to-all-start = ((bf16[32,240,512]{2,1,0:T(8,128)(2,1)}), bf16[32,240,512]{2,1,0:T(8,128)(2,1)}, u32[]{:S(2)}, u32[]{:S(2)}) async-start(bf16[32,240,512]{2,1,0:T(8,128)(2,1)} %pack.1), calls=%async_computation | async-start | bytes 15728640 | tf_op jit(solution)/shard_map/all_to_all | solution.py:326
  117.9 2.0 collective-permute-start.25
  119.9 6.8 %multiply_reduce_fusion = (f32[4,128]{1,0:T(4,128)S(1)}, bf16[4,4,2,128,512]{4,3,2,1,0:T(8,128)(2,1)}, f32[4,128]{1,0:T(4,128)S(1)}, bf16[4,4,2,128,512]{4,3,2,1,0:T(8,128)(2,1)}) fusion(bf16[1,4,2,128,512]{4,3,2,1,0:T(8,128)(2,1)} %bitcast.21, bf16[1,4,2,128,512]{4,3,2,1,0:T(8,128)(2,1)} %bitcast.20, bf16[1,4,2,128,512]{4,3,2,1,0:T(8,128)(2,1)} %bitcast.19, ...), kind=kLoop, calls=%fused_computation | loop fusion | flops 25164800 | bytes 16781312 | tf_op jit(solution)/shard_map/reduce_sum | solution.py:344
  129.5 12.8 %errors.1 = bf16[240,256]{1,0:T(8,128)(2,1)S(1)} custom-call(bf16[240,256]{1,0:T(8,128)(2,1)S(1)} %slice.27.w_ref, f32[2,256]{1,0:T(2,128)S(1)} %pad.7.codes_ref, f32[2,256]{1,0:T(2,128)S(1)} %pad.8.zeros_ref, bf16[256,256]{1,0:T(8,128)(2,1)S(1)} %add_add_fusion.p_ref), custom_call_target="tpu_custom_call" | custom-call | flops 10000000 | bytes 1000000 | tf_op jit(solution)/shard_map/errors/pallas_call | solution.py:120
  142.3 83.6 %collective-permute-done.28 = f32[4,256]{1,0:T(4,128)S(1)} collective-permute-done((f32[4,256]{1,0:T(4,128)S(1)}, f32[4,256]{1,0:T(4,128)S(1)}, u32[]{:S(2)}, u32[]{:S(2)}) %collective-permute-start.28) | collective-permute-done | bytes 4128 | tf_op jit(solution)/shard_map/ppermute | solution.py:349
  226.1 11.6 %all-to-all-done.w_ref = bf16[32,240,512]{2,1,0:T(8,128)(2,1)} async-done(((bf16[32,240,512]{2,1,0:T(8,128)(2,1)}), bf16[32,240,512]{2,1,0:T(8,128)(2,1)}, u32[]{:S(2)}, u32[]{:S(2)}) %all-to-all-start) | async-done | bytes 7864352 | tf_op jit(solution)/shard_map/all_to_all | solution.py:326
  237.7 2.2 broadcast_in_dim.14
  239.9 4.8 %all-to-all-start.1 = ((bf16[32,240,256]{2,1,0:T(8,128)(2,1)}), bf16[32,240,256]{2,1,0:T(8,128)(2,1)}, u32[]{:S(2)}, u32[]{:S(2)}) async-start(bf16[32,240,256]{2,1,0:T(8,128)(2,1)} %broadcast_in_dim.14), calls=%async_computation.1 | async-start | bytes 7864320 | tf_op jit(solution)/shard_map/all_to_all | solution.py:351
  247.1 1.9 copy-done
  248.9 2.2 copy-done.1
  251.1 9.6 %mean_outer.1 = f32[4096,512]{1,0:T(8,128)} custom-call(s32[12]{0:T(128)S(1)} %stack.99.table, bf16[4,4,2,128,512]{4,3,2,1,0:T(8,128)(2,1)S(1)} %copy-done.1, bf16[4,4,2,128,512]{4,3,2,1,0:T(8,128)(2,1)S(1)} %copy-done, bf16[4,256,512]{2,1,0:T(8,128)(2,1)S(1)} %slice.32.own_ref, f32[4,256,1]{2,1,0:T(8,128)S(1)} %copy.8.inv_ref, f32[8,1,512]{2,1,0:T(1,128)S(1)} %bitcast.40, ...), custom_call_target="tpu_custom_call" | custom-call | flops 4294967296 | bytes 20971520 | tf_op jit(solution)/shard_map/mean_outer/pallas_call | solution.py:180
  260.7 33.9 %all-to-all-done.1.e_ref = bf16[32,240,256]{2,1,0:T(8,128)(2,1)} async-done(((bf16[32,240,256]{2,1,0:T(8,128)(2,1)}), bf16[32,240,256]{2,1,0:T(8,128)(2,1)}, u32[]{:S(2)}, u32[]{:S(2)}) %all-to-all-start.1) | async-done | bytes 3932192 | tf_op jit(solution)/shard_map/all_to_all | solution.py:351
  294.7 10.6 %corrected.1 = bf16[7680,512]{1,0:T(8,128)(2,1)} custom-call(bf16[32,240,512]{2,1,0:T(8,128)(2,1)} %all-to-all-done.w_ref, bf16[32,240,256]{2,1,0:T(8,128)(2,1)} %all-to-all-done.1.e_ref, bf16[256,512]{1,0:T(8,128)(2,1)S(1)} %pad_maximum_fusion.7.p_ref), custom_call_target="tpu_custom_call" | custom-call | flops 2013265920 | bytes 20971520 | tf_op jit(solution)/shard_map/corrected/pallas_call | solution.py:204
  (81 shorter events, 16.4 us)
Async XLA Ops:
  1.5 11.6 %collective-permute-start.2 = (bf16[256,256]{1,0:T(8,128)(2,1)S(1)}, bf16[256,256]{1,0:T(8,128)(2,1)S(1)}, u32[]{:S(2)}, u32[]{:S(2)}) collective-permute-start(bf16[256,256]{1,0:T(8,128)(2,1)S(1)} %pad_maximum_fusion.8), channel_id=1, source_target_pairs={{0,1},{1,0}} | collective-permute-start | bytes 393224 | tf_op jit(solution)/shard_map/ppermute | solution.py:288
  2.2 10.9 %collective-permute-start = (bf16[256,512]{1,0:T(8,128)(2,1)}, bf16[256,512]{1,0:T(8,128)(2,1)S(1)}, u32[]{:S(2)}, u32[]{:S(2)}) collective-permute-start(bf16[256,512]{1,0:T(8,128)(2,1)} %param.6), channel_id=1, source_target_pairs={{0,0},{1,1},{2,2},{3,3},{4,4},{5,5},{6,6},{7,7},{8,32},{9,33},{10,... | collective-permute-start | bytes 786440 | tf_op jit(solution)/shard_map/ppermute | solution.py:306
  6.7 12.6 %collective-permute-start.1 = (bf16[256,512]{1,0:T(8,128)(2,1)}, bf16[256,512]{1,0:T(8,128)(2,1)S(1)}, u32[]{:S(2)}, u32[]{:S(2)}) collective-permute-start(bf16[256,512]{1,0:T(8,128)(2,1)} %param.6), channel_id=1, source_target_pairs={{0,1},{1,0},{2,3},{3,2},{4,5},{5,4},{6,7},{7,6},{8,33},{9,32},{10,... | collective-permute-start | bytes 786440 | tf_op jit(solution)/shard_map/ppermute | solution.py:307
  9.4 17.3 %collective-permute-start.3 = (bf16[256,128]{1,0:T(8,128)(2,1)}, bf16[256,128]{1,0:T(8,128)(2,1)S(1)}, u32[]{:S(2)}, u32[]{:S(2)}) collective-permute-start(bf16[256,128]{1,0:T(8,128)(2,1)} %param.11), channel_id=1, source_target_pairs={{0,0},{1,32},{2,64},{3,96},{4,1},{5,33},{6,65},{7,97},{8,2},{9,34}... | collective-permute-start | bytes 196616 | tf_op jit(solution)/shard_map/ppermute | solution.py:310
  26.7 2.2 collective-permute-start.12
  27.4 1.5 collective-permute-start.11
  28.1 0.8 collective-permute-start.10
  28.8 8.5 %collective-permute-start.9 = (bf16[2,128,512]{2,1,0:T(8,128)(2,1)S(1)}, bf16[2,128,512]{2,1,0:T(8,128)(2,1)S(1)}, u32[]{:S(2)}, u32[]{:S(2)}) collective-permute-start(bf16[2,128,512]{2,1,0:T(8,128)(2,1)S(1)} %get-tuple-element.56), channel_id=1, source_target_pairs={{0,16},{1,17},{2,18},{3,19},{4,20},{5,21},{6,22},{7,23},{8,24},{9,... | collective-permute-start | bytes 786440 | tf_op jit(solution)/shard_map/ppermute | solution.py:249
  29.0 3.5 %collective-permute-start.15 = (bf16[256,256]{1,0:T(8,128)(2,1)S(1)}, bf16[256,256]{1,0:T(8,128)(2,1)S(1)}, u32[]{:S(2)}, u32[]{:S(2)}) collective-permute-start(bf16[256,256]{1,0:T(8,128)(2,1)S(1)} %add_add_fusion.2), channel_id=1, source_target_pairs={{0,6},{1,7},{8,14},{9,15},{16,22},{17,23},{24,30},{25,31}} | collective-permute-start | bytes 393224 | tf_op jit(solution)/shard_map/ppermute | solution.py:288
  29.6 4.1 %collective-permute-start.14 = (bf16[256,256]{1,0:T(8,128)(2,1)S(1)}, bf16[256,256]{1,0:T(8,128)(2,1)S(1)}, u32[]{:S(2)}, u32[]{:S(2)}) collective-permute-start(bf16[256,256]{1,0:T(8,128)(2,1)S(1)} %add_add_fusion.2), channel_id=1, source_target_pairs={{0,4},{1,5},{8,12},{9,13},{16,20},{17,21},{24,28},{25,29}} | collective-permute-start | bytes 393224 | tf_op jit(solution)/shard_map/ppermute | solution.py:288
  30.3 7.0 %collective-permute-start.13 = (bf16[256,256]{1,0:T(8,128)(2,1)S(1)}, bf16[256,256]{1,0:T(8,128)(2,1)S(1)}, u32[]{:S(2)}, u32[]{:S(2)}) collective-permute-start(bf16[256,256]{1,0:T(8,128)(2,1)S(1)} %add_add_fusion.2), channel_id=1, source_target_pairs={{0,2},{1,3},{8,10},{9,11},{16,18},{17,19},{24,26},{25,27}} | collective-permute-start | bytes 393224 | tf_op jit(solution)/shard_map/ppermute | solution.py:288
  31.0 9.1 %collective-permute-start.8 = (bf16[2,128,512]{2,1,0:T(8,128)(2,1)S(1)}, bf16[2,128,512]{2,1,0:T(8,128)(2,1)S(1)}, u32[]{:S(2)}, u32[]{:S(2)}) collective-permute-start(bf16[2,128,512]{2,1,0:T(8,128)(2,1)S(1)} %get-tuple-element.56), channel_id=1, source_target_pairs={{0,8},{1,9},{2,10},{3,11},{4,12},{5,13},{6,14},{7,15},{8,16},{9,17... | collective-permute-start | bytes 786440 | tf_op jit(solution)/shard_map/ppermute | solution.py:249
  32.5 8.3 %collective-permute-start.7 = (bf16[2,128,512]{2,1,0:T(8,128)(2,1)S(1)}, bf16[2,128,512]{2,1,0:T(8,128)(2,1)S(1)}, u32[]{:S(2)}, u32[]{:S(2)}) collective-permute-start(bf16[2,128,512]{2,1,0:T(8,128)(2,1)S(1)} %get-tuple-element.56), channel_id=1, source_target_pairs={{0,24},{1,25},{2,26},{3,27},{4,28},{5,29},{6,30},{7,31},{8,0},{9,1... | collective-permute-start | bytes 786440 | tf_op jit(solution)/shard_map/ppermute | solution.py:249
  33.7 7.8 %collective-permute-start.6 = (bf16[2,128,512]{2,1,0:T(8,128)(2,1)S(1)}, bf16[2,128,512]{2,1,0:T(8,128)(2,1)S(1)}, u32[]{:S(2)}, u32[]{:S(2)}) collective-permute-start(bf16[2,128,512]{2,1,0:T(8,128)(2,1)S(1)} %get-tuple-element.57), channel_id=1, source_target_pairs={{0,4},{1,5},{2,6},{3,7},{4,0},{5,1},{6,2},{7,3},{8,12},{9,13},{10,... | collective-permute-start | bytes 786440 | tf_op jit(solution)/shard_map/ppermute | solution.py:249
  37.3 7.0 %collective-permute-start.5 = (bf16[2,128,512]{2,1,0:T(8,128)(2,1)S(1)}, bf16[2,128,512]{2,1,0:T(8,128)(2,1)S(1)}, u32[]{:S(2)}, u32[]{:S(2)}) collective-permute-start(bf16[2,128,512]{2,1,0:T(8,128)(2,1)S(1)} %get-tuple-element.57), channel_id=1, source_target_pairs={{0,2},{1,3},{2,4},{3,5},{4,6},{5,7},{6,0},{7,1},{8,10},{9,11},{10,... | collective-permute-start | bytes 786440 | tf_op jit(solution)/shard_map/ppermute | solution.py:249
  37.3 7.4 %collective-permute-start.4 = (bf16[2,128,512]{2,1,0:T(8,128)(2,1)S(1)}, bf16[2,128,512]{2,1,0:T(8,128)(2,1)S(1)}, u32[]{:S(2)}, u32[]{:S(2)}) collective-permute-start(bf16[2,128,512]{2,1,0:T(8,128)(2,1)S(1)} %get-tuple-element.57), channel_id=1, source_target_pairs={{0,6},{1,7},{2,0},{3,1},{4,2},{5,3},{6,4},{7,5},{8,14},{9,15},{10,... | collective-permute-start | bytes 786440 | tf_op jit(solution)/shard_map/ppermute | solution.py:249
  40.1 4.7 %collective-permute-start.18 = (bf16[256,256]{1,0:T(8,128)(2,1)S(1)}, bf16[256,256]{1,0:T(8,128)(2,1)S(1)}, u32[]{:S(2)}, u32[]{:S(2)}) collective-permute-start(bf16[256,256]{1,0:T(8,128)(2,1)S(1)} %add_add_fusion.1), channel_id=1, source_target_pairs={{0,96},{1,97},{2,98},{3,99},{4,100},{5,101},{6,102},{7,103},{8,104... | collective-permute-start | bytes 393224 | tf_op jit(solution)/shard_map/ppermute | solution.py:288
  40.8 4.1 %collective-permute-start.17 = (bf16[256,256]{1,0:T(8,128)(2,1)S(1)}, bf16[256,256]{1,0:T(8,128)(2,1)S(1)}, u32[]{:S(2)}, u32[]{:S(2)}) collective-permute-start(bf16[256,256]{1,0:T(8,128)(2,1)S(1)} %add_add_fusion.1), channel_id=1, source_target_pairs={{0,64},{1,65},{2,66},{3,67},{4,68},{5,69},{6,70},{7,71},{8,72},{9,... | collective-permute-start | bytes 393224 | tf_op jit(solution)/shard_map/ppermute | solution.py:288
  41.6 15.8 %collective-permute-start.16 = (bf16[256,256]{1,0:T(8,128)(2,1)S(1)}, bf16[256,256]{1,0:T(8,128)(2,1)S(1)}, u32[]{:S(2)}, u32[]{:S(2)}) collective-permute-start(bf16[256,256]{1,0:T(8,128)(2,1)S(1)} %add_add_fusion.1), channel_id=1, source_target_pairs={{0,32},{1,33},{2,34},{3,35},{4,36},{5,37},{6,38},{7,39},{8,40},{9,... | collective-permute-start | bytes 393224 | tf_op jit(solution)/shard_map/ppermute | solution.py:288
  57.5 25.0 %collective-permute-start.21 = (bf16[8,128,512]{2,1,0:T(8,128)(2,1)S(1)}, bf16[8,128,512]{2,1,0:T(8,128)(2,1)S(1)}, u32[]{:S(2)}, u32[]{:S(2)}) collective-permute-start(bf16[8,128,512]{2,1,0:T(8,128)(2,1)S(1)} %pad_maximum_fusion.3), channel_id=1, source_target_pairs={{0,16},{1,17},{2,18},{3,19},{4,20},{5,21},{6,22},{7,23},{8,24},{9,... | collective-permute-start | bytes 3145736 | tf_op jit(solution)/shard_map/ppermute | solution.py:249
  58.4 48.3 %collective-permute-start.20 = (bf16[8,128,512]{2,1,0:T(8,128)(2,1)S(1)}, bf16[8,128,512]{2,1,0:T(8,128)(2,1)}, u32[]{:S(2)}, u32[]{:S(2)}) collective-permute-start(bf16[8,128,512]{2,1,0:T(8,128)(2,1)S(1)} %pad_maximum_fusion.3), channel_id=1, source_target_pairs={{0,8},{1,9},{2,10},{3,11},{4,12},{5,13},{6,14},{7,15},{8,16},{9,17... | collective-permute-start | bytes 3145736 | tf_op jit(solution)/shard_map/ppermute | solution.py:249
  60.6 46.1 %collective-permute-start.19 = (bf16[8,128,512]{2,1,0:T(8,128)(2,1)S(1)}, bf16[8,128,512]{2,1,0:T(8,128)(2,1)}, u32[]{:S(2)}, u32[]{:S(2)}) collective-permute-start(bf16[8,128,512]{2,1,0:T(8,128)(2,1)S(1)} %pad_maximum_fusion.3), channel_id=1, source_target_pairs={{0,24},{1,25},{2,26},{3,27},{4,28},{5,29},{6,30},{7,31},{8,0},{9,1... | collective-permute-start | bytes 3145736 | tf_op jit(solution)/shard_map/ppermute | solution.py:249
  61.1 45.6 %collective-permute-start.24 = (bf16[8,128,512]{2,1,0:T(8,128)(2,1)S(1)}, bf16[8,128,512]{2,1,0:T(8,128)(2,1)}, u32[]{:S(2)}, u32[]{:S(2)}) collective-permute-start(bf16[8,128,512]{2,1,0:T(8,128)(2,1)S(1)} %pad_maximum_fusion.4), channel_id=1, source_target_pairs={{0,4},{1,5},{2,6},{3,7},{4,0},{5,1},{6,2},{7,3},{8,12},{9,13},{10,... | collective-permute-start | bytes 3145736 | tf_op jit(solution)/shard_map/ppermute | solution.py:249
  62.2 48.0 %collective-permute-start.23 = (bf16[8,128,512]{2,1,0:T(8,128)(2,1)S(1)}, bf16[8,128,512]{2,1,0:T(8,128)(2,1)}, u32[]{:S(2)}, u32[]{:S(2)}) collective-permute-start(bf16[8,128,512]{2,1,0:T(8,128)(2,1)S(1)} %pad_maximum_fusion.4), channel_id=1, source_target_pairs={{0,2},{1,3},{2,4},{3,5},{4,6},{5,7},{6,0},{7,1},{8,10},{9,11},{10,... | collective-permute-start | bytes 3145736 | tf_op jit(solution)/shard_map/ppermute | solution.py:249
  82.5 27.8 %collective-permute-start.22 = (bf16[8,128,512]{2,1,0:T(8,128)(2,1)S(1)}, bf16[8,128,512]{2,1,0:T(8,128)(2,1)}, u32[]{:S(2)}, u32[]{:S(2)}) collective-permute-start(bf16[8,128,512]{2,1,0:T(8,128)(2,1)S(1)} %pad_maximum_fusion.4), channel_id=1, source_target_pairs={{0,6},{1,7},{2,0},{3,1},{4,2},{5,3},{6,4},{7,5},{8,14},{9,15},{10,... | collective-permute-start | bytes 3145736 | tf_op jit(solution)/shard_map/ppermute | solution.py:249
  97.7 19.2 %copy-start.2 = (bf16[256,512]{1,0:T(8,128)(2,1)S(1)}, bf16[256,512]{1,0:T(8,128)(2,1)}, u32[]{:S(2)}) copy-start(bf16[256,512]{1,0:T(8,128)(2,1)} %param.6) | copy-start | bytes 786436
  110.3 127.5 %all-to-all-start = ((bf16[32,240,512]{2,1,0:T(8,128)(2,1)}), bf16[32,240,512]{2,1,0:T(8,128)(2,1)}, u32[]{:S(2)}, u32[]{:S(2)}) async-start(bf16[32,240,512]{2,1,0:T(8,128)(2,1)} %pack.1), calls=%async_computation | async-start | bytes 15728640 | tf_op jit(solution)/shard_map/all_to_all | solution.py:326
  117.9 8.9 %collective-permute-start.25 = (bf16[256,640]{1,0:T(8,128)(2,1)S(1)}, bf16[256,640]{1,0:T(8,128)(2,1)S(1)}, u32[]{:S(2)}, u32[]{:S(2)}) collective-permute-start(bf16[256,640]{1,0:T(8,128)(2,1)S(1)} %constant_dynamic-update-slice_fusion), channel_id=1, source_target_pairs={{0,32},{1,33},{2,34},{3,35},{4,36},{5,37},{6,38},{7,39},{8,40},{9,... | collective-permute-start | bytes 983048 | tf_op jit(solution)/shard_map/ppermute | solution.py:254
  126.7 1.2 collective-permute-start.27
  126.9 99.1 %collective-permute-start.26 = (bf16[2,256,640]{2,1,0:T(8,128)(2,1)S(1)}, bf16[2,256,640]{2,1,0:T(8,128)(2,1)S(1)}, u32[]{:S(2)}, u32[]{:S(2)}) collective-permute-start(bf16[2,256,640]{2,1,0:T(8,128)(2,1)S(1)} %pad_maximum_fusion.5), channel_id=1, source_target_pairs={{0,64},{1,65},{2,66},{3,67},{4,68},{5,69},{6,70},{7,71},{8,72},{9,... | collective-permute-start | bytes 1966088 | tf_op jit(solution)/shard_map/ppermute | solution.py:258
  127.9 98.0 %collective-permute-start.28 = (f32[4,256]{1,0:T(4,128)S(1)}, f32[4,256]{1,0:T(4,128)S(1)}, u32[]{:S(2)}, u32[]{:S(2)}) collective-permute-start(f32[4,256]{1,0:T(4,128)S(1)} %fusion), channel_id=1, source_target_pairs={{0,64},{1,65},{2,66},{3,67},{4,68},{5,69},{6,70},{7,71},{8,72},{9,... | collective-permute-start | bytes 12296 | tf_op jit(solution)/shard_map/ppermute | solution.py:349
  239.9 54.8 %all-to-all-start.1 = ((bf16[32,240,256]{2,1,0:T(8,128)(2,1)}), bf16[32,240,256]{2,1,0:T(8,128)(2,1)}, u32[]{:S(2)}, u32[]{:S(2)}) async-start(bf16[32,240,256]{2,1,0:T(8,128)(2,1)} %broadcast_in_dim.14), calls=%async_computation.1 | async-start | bytes 7864320 | tf_op jit(solution)/shard_map/all_to_all | solution.py:351
  (5 other events, 46.2 us)

commit v6 on v5

--- a/solution.py
+++ b/solution.py
@@ -111,30 +111,32 @@
             for part in split3(errs[first : first + BLOCK, :]):
                 spill = spill + contract_rows(p_rows, part.astype(jnp.bfloat16))
             work[first + BLOCK :, :] -= spill
-    e_ref[...] = errs[...].T[:rows].astype(jnp.bfloat16)
-
-
-def block_errors(weight, codes, zeros, first_panel):
+    found = errs[...].T[:rows].astype(jnp.bfloat16)
+    for i in range(e_ref.shape[0]):
+        e_ref[i] = found
+
+
+def block_errors(weight, codes, zeros, first_panel, shards):
     rows = weight.shape[0]
     lanes = -(-rows // 128) * 128
     return pl.pallas_call(
         errors_kernel,
         grid=(1,),
-        out_shape=jax.ShapeDtypeStruct((rows, COLS), jnp.bfloat16),
+        out_shape=jax.ShapeDtypeStruct((shards, rows, COLS), jnp.bfloat16),
         in_specs=[
             pl.BlockSpec((rows, COLS), lambda i: (0, 0)),
             pl.BlockSpec((BLOCKS, lanes), lambda i: (0, 0)),
             pl.BlockSpec((BLOCKS, lanes), lambda i: (0, 0)),
             pl.BlockSpec((COLS, COLS), lambda i: (0, 0)),
         ],
-        out_specs=pl.BlockSpec((rows, COLS), lambda i: (0, 0)),
+        out_specs=pl.BlockSpec((shards, rows, COLS), lambda i: (0, 0, 0)),
         scratch_shapes=[
             pltpu.VMEM((COLS, lanes), jnp.float32),
             pltpu.VMEM((COLS, 128), jnp.float32),
             pltpu.VMEM((COLS, COLS), jnp.float32),
             pltpu.VMEM((COLS, lanes), jnp.float32),
         ],
-        compiler_params=pltpu.CompilerParams(vmem_limit_bytes=16 * 2**20),
+        compiler_params=pltpu.CompilerParams(vmem_limit_bytes=24 * 2**20),
         cost_estimate=pl.CostEstimate(flops=10**7, bytes_accessed=10**6, transcendentals=0),
         name="errors",
     )(weight, codes, zeros, first_panel)
@@ -327,7 +329,7 @@
     pad = -(-rows // 128) * 128 - rows
     codes = jnp.pad(scale_codes.astype(jnp.float32).T, ((0, 0), (0, pad)))
     zeros = jnp.pad(zero_points.astype(jnp.float32).T, ((0, 0), (0, pad)))
-    errors = block_errors(weight[:, :COLS], codes, zeros, first_panel)
+    errors = block_errors(weight[:, :COLS], codes, zeros, first_panel, shards)
 
     pair = beside(jnp.concatenate([residual, shard], axis=1))
     met = beyond(pair)
@@ -347,7 +349,7 @@
     )
     sums = sums + lax.ppermute(sums, ALL, moves(lambda tt, x, z, h: (tt ^ 1, x, z, h)))
     sums = sums + lax.ppermute(sums, ALL, moves(lambda tt, x, z, h: (tt ^ 2, x, z, h)))
-    copies = later(jnp.broadcast_to(errors[None], (shards, rows, COLS)), moved, met, sums)
+    copies = later(errors, moved, met, sums)
     errors_all = lax.all_to_all(copies, "tp", split_axis=0, concat_axis=0)
     inv_norm = lax.rsqrt(sums / feat_total + EPS)[:, :, None]
     quarter_feats = feat_total // groups

time: 311 us -> 309 us (level)
  no operation moved by 1% of the time
where the time goes in v6:
time: 309 us; the launch traced here: 303 us
  waiting for transfers between devices  187 us (61%)
  starting transfers between devices  51.5 us (17%)
  Pallas kernels  44.9 us (15%)
  local copies, waits for them, and re-layouts  9.8 us (3%)
  other arithmetic  8.41 us (3%)
    ppermute x1, waiting for transfers between devices, on_device(): lax.ppermute(sums, ALL, moves(lambda tt, x, z, h: (tt ^ 2, x, z, h)))  81.5 us
    all_to_all x1, waiting for transfers between devices, on_device(): errors_all = lax.all_to_all(copies, 'tp', split_axis=0, concat_axis=0)  33.9 us
    ppermute x12, waiting for transfers between devices, ring(): others = [lax.ppermute(block, ALL, shift(-d, along_x)) for d in RING[1:]]  33.1 us
    ppermute x12, starting transfers between devices, ring(): others = [lax.ppermute(block, ALL, shift(-d, along_x)) for d in RING[1:]]  19 us
    pallas_call x1, Pallas kernels, block_errors(): pl.pallas_call(errors_kernel, grid=(1,), out_shape=jax.ShapeDtypeStruct((...  13.1 us
    ppermute x10, waiting for transfers between devices, spread(): lax.ppermute(held, ALL, perm)  12.6 us
    pallas_call x1, Pallas kernels, pack(): pl.pallas_call(pack_kernel, grid=(shards // 2,), out_shape=jax.ShapeDtype...  11.6 us
    all_to_all x1, waiting for transfers between devices, on_device(): moved = lax.all_to_all(packed, 'tp', split_axis=0, concat_axis=0)  11.6 us
  transfers between devices with their start and end apart: 31, of which 13 were waited for; matrix products, arithmetic and copies ran while one was open for 4% of the time, Pallas kernels for 11%

profile of v6, /device:TPU:1, one launch (start us, length us, event | category | flops | bytes accessed | tf_op | source)
XLA Modules:
  0.0 303.1 jit_solution(968989441712220587)
XLA Ops:
  2.2 4.5 %collective-permute-start = (bf16[256,512]{1,0:T(8,128)(2,1)}, bf16[256,512]{1,0:T(8,128)(2,1)S(1)}, u32[]{:S(2)}, u32[]{:S(2)}) collective-permute-start(bf16[256,512]{1,0:T(8,128)(2,1)} %param.6), channel_id=1, source_target_pairs={{0,0},{1,1},{2,2},{3,3},{4,4},{5,5},{6,6},{7,7},{8,32},{9,33},{10,... | collective-permute-start | bytes 786440 | tf_op jit(solution)/shard_map/ppermute | solution.py:308
  6.7 2.7 collective-permute-start.1
  9.4 3.6 %collective-permute-start.3 = (bf16[256,128]{1,0:T(8,128)(2,1)}, bf16[256,128]{1,0:T(8,128)(2,1)S(1)}, u32[]{:S(2)}, u32[]{:S(2)}) collective-permute-start(bf16[256,128]{1,0:T(8,128)(2,1)} %param.11), channel_id=1, source_target_pairs={{0,0},{1,32},{2,64},{3,96},{4,1},{5,33},{6,65},{7,97},{8,2},{9,34}... | collective-permute-start | bytes 196616 | tf_op jit(solution)/shard_map/ppermute | solution.py:312
  13.2 6.2 %collective-permute-done.1 = bf16[256,512]{1,0:T(8,128)(2,1)S(1)} collective-permute-done((bf16[256,512]{1,0:T(8,128)(2,1)}, bf16[256,512]{1,0:T(8,128)(2,1)S(1)}, u32[]{:S(2)}, u32[]{:S(2)}) %collective-permute-start.1) | collective-permute-done | bytes 262176 | tf_op jit(solution)/shard_map/ppermute | solution.py:309
  19.4 7.3 %collective-permute-done.3 = bf16[256,128]{1,0:T(8,128)(2,1)S(1)} collective-permute-done((bf16[256,128]{1,0:T(8,128)(2,1)}, bf16[256,128]{1,0:T(8,128)(2,1)S(1)}, u32[]{:S(2)}, u32[]{:S(2)}) %collective-permute-start.3) | collective-permute-done | bytes 65568 | tf_op jit(solution)/shard_map/ppermute | solution.py:312
  31.0 1.5 collective-permute-start.8
  32.5 1.3 collective-permute-start.7
  33.7 3.5 %collective-permute-start.6 = (bf16[2,128,512]{2,1,0:T(8,128)(2,1)S(1)}, bf16[2,128,512]{2,1,0:T(8,128)(2,1)S(1)}, u32[]{:S(2)}, u32[]{:S(2)}) collective-permute-start(bf16[2,128,512]{2,1,0:T(8,128)(2,1)S(1)} %get-tuple-element.57), channel_id=1, source_target_pairs={{0,4},{1,5},{2,6},{3,7},{4,0},{5,1},{6,2},{7,3},{8,12},{9,13},{10,... | collective-permute-start | bytes 786440 | tf_op jit(solution)/shard_map/ppermute | solution.py:251
  37.3 2.7 collective-permute-start.4
  41.6 1.3 collective-permute-start.16
  42.9 1.4 collective-permute-done.5
  44.8 12.6 %collective-permute-done.16 = bf16[256,256]{1,0:T(8,128)(2,1)S(1)} collective-permute-done((bf16[256,256]{1,0:T(8,128)(2,1)S(1)}, bf16[256,256]{1,0:T(8,128)(2,1)S(1)}, u32[]{:S(2)}, u32[]{:S(2)}) %collective-permute-start.16) | collective-permute-done | bytes 131104 | tf_op jit(solution)/shard_map/ppermute | solution.py:290
  58.4 2.2 collective-permute-start.20
  62.2 1.6 collective-permute-start.23
  63.8 18.6 %collective-permute-done.21 = bf16[8,128,512]{2,1,0:T(8,128)(2,1)S(1)} collective-permute-done((bf16[8,128,512]{2,1,0:T(8,128)(2,1)S(1)}, bf16[8,128,512]{2,1,0:T(8,128)(2,1)S(1)}, u32[]{:S(2)}, u32[]{:S(2)}) %collective-permute-start.21) | collective-permute-done | bytes 1048608 | tf_op jit(solution)/shard_map/ppermute | solution.py:251
  82.5 3.6 %collective-permute-start.22 = (bf16[8,128,512]{2,1,0:T(8,128)(2,1)S(1)}, bf16[8,128,512]{2,1,0:T(8,128)(2,1)}, u32[]{:S(2)}, u32[]{:S(2)}) collective-permute-start(bf16[8,128,512]{2,1,0:T(8,128)(2,1)S(1)} %pad_maximum_fusion.4), channel_id=1, source_target_pairs={{0,6},{1,7},{2,0},{3,1},{4,2},{5,3},{6,4},{7,5},{8,14},{9,15},{10,... | collective-permute-start | bytes 3145736 | tf_op jit(solution)/shard_map/ppermute | solution.py:251
  86.1 11.6 %pack.1 = bf16[32,240,512]{2,1,0:T(8,128)(2,1)} custom-call(bf16[240,16384]{1,0:T(8,128)(2,1)} %w_ref), custom_call_target="tpu_custom_call" | custom-call | bytes 15728640 | tf_op jit(solution)/shard_map/pack/pallas_call | solution.py:233
  97.7 9.0 %collective-permute-done.20 = bf16[8,128,512]{2,1,0:T(8,128)(2,1)} collective-permute-done((bf16[8,128,512]{2,1,0:T(8,128)(2,1)S(1)}, bf16[8,128,512]{2,1,0:T(8,128)(2,1)}, u32[]{:S(2)}, u32[]{:S(2)}) %collective-permute-start.20) | collective-permute-done | bytes 1048608 | tf_op jit(solution)/shard_map/ppermute | solution.py:251
  106.7 3.6 %collective-permute-done.23 = bf16[8,128,512]{2,1,0:T(8,128)(2,1)} collective-permute-done((bf16[8,128,512]{2,1,0:T(8,128)(2,1)S(1)}, bf16[8,128,512]{2,1,0:T(8,128)(2,1)}, u32[]{:S(2)}, u32[]{:S(2)}) %collective-permute-start.23) | collective-permute-done | bytes 1048608 | tf_op jit(solution)/shard_map/ppermute | solution.py:251
  110.3 6.7 %all-to-all-start = ((bf16[32,240,512]{2,1,0:T(8,128)(2,1)}), bf16[32,240,512]{2,1,0:T(8,128)(2,1)}, u32[]{:S(2)}, u32[]{:S(2)}) async-start(bf16[32,240,512]{2,1,0:T(8,128)(2,1)} %pack.1), calls=%async_computation | async-start | bytes 15728640 | tf_op jit(solution)/shard_map/all_to_all | solution.py:328
  117.9 2.0 collective-permute-start.25
  119.9 6.8 %multiply_reduce_fusion = (f32[4,128]{1,0:T(4,128)S(1)}, bf16[4,4,2,128,512]{4,3,2,1,0:T(8,128)(2,1)}, f32[4,128]{1,0:T(4,128)S(1)}, bf16[4,4,2,128,512]{4,3,2,1,0:T(8,128)(2,1)}) fusion(bf16[1,4,2,128,512]{4,3,2,1,0:T(8,128)(2,1)} %bitcast.21, bf16[1,4,2,128,512]{4,3,2,1,0:T(8,128)(2,1)} %bitcast.20, bf16[1,4,2,128,512]{4,3,2,1,0:T(8,128)(2,1)} %bitcast.19, ...), kind=kLoop, calls=%fused_computation | loop fusion | flops 25164800 | bytes 16781312 | tf_op jit(solution)/shard_map/reduce_sum | solution.py:346
  129.5 13.1 %errors.1 = bf16[32,240,256]{2,1,0:T(8,128)(2,1)S(1)} custom-call(bf16[240,256]{1,0:T(8,128)(2,1)S(1)} %slice.27.w_ref, f32[2,256]{1,0:T(2,128)S(1)} %pad.7.codes_ref, f32[2,256]{1,0:T(2,128)S(1)} %pad.8.zeros_ref, bf16[256,256]{1,0:T(8,128)(2,1)S(1)} %add_add_fusion.p_ref), custom_call_target="tpu_custom_call" | custom-call | flops 10000000 | bytes 1000000 | tf_op jit(solution)/shard_map/errors/pallas_call | solution.py:122
  142.5 1.9 copy-done.2
  144.4 81.5 %collective-permute-done.28 = f32[4,256]{1,0:T(4,128)S(1)} collective-permute-done((f32[4,256]{1,0:T(4,128)S(1)}, f32[4,256]{1,0:T(4,128)S(1)}, u32[]{:S(2)}, u32[]{:S(2)}) %collective-permute-start.28) | collective-permute-done | bytes 4128 | tf_op jit(solution)/shard_map/ppermute | solution.py:351
  226.1 11.6 %all-to-all-done.w_ref = bf16[32,240,512]{2,1,0:T(8,128)(2,1)} async-done(((bf16[32,240,512]{2,1,0:T(8,128)(2,1)}), bf16[32,240,512]{2,1,0:T(8,128)(2,1)}, u32[]{:S(2)}, u32[]{:S(2)}) %all-to-all-start) | async-done | bytes 7864352 | tf_op jit(solution)/shard_map/all_to_all | solution.py:328
  237.7 4.8 %all-to-all-start.1 = ((bf16[32,240,256]{2,1,0:T(8,128)(2,1)}), bf16[32,240,256]{2,1,0:T(8,128)(2,1)}, u32[]{:S(2)}, u32[]{:S(2)}) async-start(bf16[32,240,256]{2,1,0:T(8,128)(2,1)} %copy-done.2), calls=%async_computation.1 | async-start | bytes 7864320 | tf_op jit(solution)/shard_map/all_to_all | solution.py:353
  244.9 1.9 copy-done
  246.8 2.2 copy-done.1
  248.9 9.6 %mean_outer.1 = f32[4096,512]{1,0:T(8,128)} custom-call(s32[12]{0:T(128)S(1)} %stack.99.table, bf16[4,4,2,128,512]{4,3,2,1,0:T(8,128)(2,1)S(1)} %copy-done.1, bf16[4,4,2,128,512]{4,3,2,1,0:T(8,128)(2,1)S(1)} %copy-done, bf16[4,256,512]{2,1,0:T(8,128)(2,1)S(1)} %slice.32.own_ref, f32[4,256,1]{2,1,0:T(8,128)S(1)} %copy.8.inv_ref, f32[8,1,512]{2,1,0:T(1,128)S(1)} %bitcast.40, ...), custom_call_target="tpu_custom_call" | custom-call | flops 4294967296 | bytes 20971520 | tf_op jit(solution)/shard_map/mean_outer/pallas_call | solution.py:182
  258.6 33.9 %all-to-all-done.1.e_ref = bf16[32,240,256]{2,1,0:T(8,128)(2,1)} async-done(((bf16[32,240,256]{2,1,0:T(8,128)(2,1)}), bf16[32,240,256]{2,1,0:T(8,128)(2,1)}, u32[]{:S(2)}, u32[]{:S(2)}) %all-to-all-start.1) | async-done | bytes 3932192 | tf_op jit(solution)/shard_map/all_to_all | solution.py:353
  292.5 10.6 %corrected.1 = bf16[7680,512]{1,0:T(8,128)(2,1)} custom-call(bf16[32,240,512]{2,1,0:T(8,128)(2,1)} %all-to-all-done.w_ref, bf16[32,240,256]{2,1,0:T(8,128)(2,1)} %all-to-all-done.1.e_ref, bf16[256,512]{1,0:T(8,128)(2,1)S(1)} %pad_maximum_fusion.7.p_ref), custom_call_target="tpu_custom_call" | custom-call | flops 2013265920 | bytes 20971520 | tf_op jit(solution)/shard_map/corrected/pallas_call | solution.py:206
  (82 shorter events, 16.4 us)
Async XLA Ops:
  1.5 11.6 %collective-permute-start.2 = (bf16[256,256]{1,0:T(8,128)(2,1)S(1)}, bf16[256,256]{1,0:T(8,128)(2,1)S(1)}, u32[]{:S(2)}, u32[]{:S(2)}) collective-permute-start(bf16[256,256]{1,0:T(8,128)(2,1)S(1)} %pad_maximum_fusion.8), channel_id=1, source_target_pairs={{0,1},{1,0}} | collective-permute-start | bytes 393224 | tf_op jit(solution)/shard_map/ppermute | solution.py:290
  2.2 10.9 %collective-permute-start = (bf16[256,512]{1,0:T(8,128)(2,1)}, bf16[256,512]{1,0:T(8,128)(2,1)S(1)}, u32[]{:S(2)}, u32[]{:S(2)}) collective-permute-start(bf16[256,512]{1,0:T(8,128)(2,1)} %param.6), channel_id=1, source_target_pairs={{0,0},{1,1},{2,2},{3,3},{4,4},{5,5},{6,6},{7,7},{8,32},{9,33},{10,... | collective-permute-start | bytes 786440 | tf_op jit(solution)/shard_map/ppermute | solution.py:308
  6.7 12.6 %collective-permute-start.1 = (bf16[256,512]{1,0:T(8,128)(2,1)}, bf16[256,512]{1,0:T(8,128)(2,1)S(1)}, u32[]{:S(2)}, u32[]{:S(2)}) collective-permute-start(bf16[256,512]{1,0:T(8,128)(2,1)} %param.6), channel_id=1, source_target_pairs={{0,1},{1,0},{2,3},{3,2},{4,5},{5,4},{6,7},{7,6},{8,33},{9,32},{10,... | collective-permute-start | bytes 786440 | tf_op jit(solution)/shard_map/ppermute | solution.py:309
  9.4 17.3 %collective-permute-start.3 = (bf16[256,128]{1,0:T(8,128)(2,1)}, bf16[256,128]{1,0:T(8,128)(2,1)S(1)}, u32[]{:S(2)}, u32[]{:S(2)}) collective-permute-start(bf16[256,128]{1,0:T(8,128)(2,1)} %param.11), channel_id=1, source_target_pairs={{0,0},{1,32},{2,64},{3,96},{4,1},{5,33},{6,65},{7,97},{8,2},{9,34}... | collective-permute-start | bytes 196616 | tf_op jit(solution)/shard_map/ppermute | solution.py:312
  26.7 2.2 collective-permute-start.12
  27.4 1.5 collective-permute-start.11
  28.1 0.8 collective-permute-start.10
  28.8 8.5 %collective-permute-start.9 = (bf16[2,128,512]{2,1,0:T(8,128)(2,1)S(1)}, bf16[2,128,512]{2,1,0:T(8,128)(2,1)S(1)}, u32[]{:S(2)}, u32[]{:S(2)}) collective-permute-start(bf16[2,128,512]{2,1,0:T(8,128)(2,1)S(1)} %get-tuple-element.56), channel_id=1, source_target_pairs={{0,16},{1,17},{2,18},{3,19},{4,20},{5,21},{6,22},{7,23},{8,24},{9,... | collective-permute-start | bytes 786440 | tf_op jit(solution)/shard_map/ppermute | solution.py:251
  29.0 3.5 %collective-permute-start.15 = (bf16[256,256]{1,0:T(8,128)(2,1)S(1)}, bf16[256,256]{1,0:T(8,128)(2,1)S(1)}, u32[]{:S(2)}, u32[]{:S(2)}) collective-permute-start(bf16[256,256]{1,0:T(8,128)(2,1)S(1)} %add_add_fusion.2), channel_id=1, source_target_pairs={{0,6},{1,7},{8,14},{9,15},{16,22},{17,23},{24,30},{25,31}} | collective-permute-start | bytes 393224 | tf_op jit(solution)/shard_map/ppermute | solution.py:290
  29.6 4.1 %collective-permute-start.14 = (bf16[256,256]{1,0:T(8,128)(2,1)S(1)}, bf16[256,256]{1,0:T(8,128)(2,1)S(1)}, u32[]{:S(2)}, u32[]{:S(2)}) collective-permute-start(bf16[256,256]{1,0:T(8,128)(2,1)S(1)} %add_add_fusion.2), channel_id=1, source_target_pairs={{0,4},{1,5},{8,12},{9,13},{16,20},{17,21},{24,28},{25,29}} | collective-permute-start | bytes 393224 | tf_op jit(solution)/shard_map/ppermute | solution.py:290
  30.3 7.0 %collective-permute-start.13 = (bf16[256,256]{1,0:T(8,128)(2,1)S(1)}, bf16[256,256]{1,0:T(8,128)(2,1)S(1)}, u32[]{:S(2)}, u32[]{:S(2)}) collective-permute-start(bf16[256,256]{1,0:T(8,128)(2,1)S(1)} %add_add_fusion.2), channel_id=1, source_target_pairs={{0,2},{1,3},{8,10},{9,11},{16,18},{17,19},{24,26},{25,27}} | collective-permute-start | bytes 393224 | tf_op jit(solution)/shard_map/ppermute | solution.py:290
  31.0 9.1 %collective-permute-start.8 = (bf16[2,128,512]{2,1,0:T(8,128)(2,1)S(1)}, bf16[2,128,512]{2,1,0:T(8,128)(2,1)S(1)}, u32[]{:S(2)}, u32[]{:S(2)}) collective-permute-start(bf16[2,128,512]{2,1,0:T(8,128)(2,1)S(1)} %get-tuple-element.56), channel_id=1, source_target_pairs={{0,8},{1,9},{2,10},{3,11},{4,12},{5,13},{6,14},{7,15},{8,16},{9,17... | collective-permute-start | bytes 786440 | tf_op jit(solution)/shard_map/ppermute | solution.py:251
  32.5 8.3 %collective-permute-start.7 = (bf16[2,128,512]{2,1,0:T(8,128)(2,1)S(1)}, bf16[2,128,512]{2,1,0:T(8,128)(2,1)S(1)}, u32[]{:S(2)}, u32[]{:S(2)}) collective-permute-start(bf16[2,128,512]{2,1,0:T(8,128)(2,1)S(1)} %get-tuple-element.56), channel_id=1, source_target_pairs={{0,24},{1,25},{2,26},{3,27},{4,28},{5,29},{6,30},{7,31},{8,0},{9,1... | collective-permute-start | bytes 786440 | tf_op jit(solution)/shard_map/ppermute | solution.py:251
  33.7 7.8 %collective-permute-start.6 = (bf16[2,128,512]{2,1,0:T(8,128)(2,1)S(1)}, bf16[2,128,512]{2,1,0:T(8,128)(2,1)S(1)}, u32[]{:S(2)}, u32[]{:S(2)}) collective-permute-start(bf16[2,128,512]{2,1,0:T(8,128)(2,1)S(1)} %get-tuple-element.57), channel_id=1, source_target_pairs={{0,4},{1,5},{2,6},{3,7},{4,0},{5,1},{6,2},{7,3},{8,12},{9,13},{10,... | collective-permute-start | bytes 786440 | tf_op jit(solution)/shard_map/ppermute | solution.py:251
  37.3 7.0 %collective-permute-start.5 = (bf16[2,128,512]{2,1,0:T(8,128)(2,1)S(1)}, bf16[2,128,512]{2,1,0:T(8,128)(2,1)S(1)}, u32[]{:S(2)}, u32[]{:S(2)}) collective-permute-start(bf16[2,128,512]{2,1,0:T(8,128)(2,1)S(1)} %get-tuple-element.57), channel_id=1, source_target_pairs={{0,2},{1,3},{2,4},{3,5},{4,6},{5,7},{6,0},{7,1},{8,10},{9,11},{10,... | collective-permute-start | bytes 786440 | tf_op jit(solution)/shard_map/ppermute | solution.py:251
  37.3 7.4 %collective-permute-start.4 = (bf16[2,128,512]{2,1,0:T(8,128)(2,1)S(1)}, bf16[2,128,512]{2,1,0:T(8,128)(2,1)S(1)}, u32[]{:S(2)}, u32[]{:S(2)}) collective-permute-start(bf16[2,128,512]{2,1,0:T(8,128)(2,1)S(1)} %get-tuple-element.57), channel_id=1, source_target_pairs={{0,6},{1,7},{2,0},{3,1},{4,2},{5,3},{6,4},{7,5},{8,14},{9,15},{10,... | collective-permute-start | bytes 786440 | tf_op jit(solution)/shard_map/ppermute | solution.py:251
  40.1 4.7 %collective-permute-start.18 = (bf16[256,256]{1,0:T(8,128)(2,1)S(1)}, bf16[256,256]{1,0:T(8,128)(2,1)S(1)}, u32[]{:S(2)}, u32[]{:S(2)}) collective-permute-start(bf16[256,256]{1,0:T(8,128)(2,1)S(1)} %add_add_fusion.1), channel_id=1, source_target_pairs={{0,96},{1,97},{2,98},{3,99},{4,100},{5,101},{6,102},{7,103},{8,104... | collective-permute-start | bytes 393224 | tf_op jit(solution)/shard_map/ppermute | solution.py:290
  40.8 4.1 %collective-permute-start.17 = (bf16[256,256]{1,0:T(8,128)(2,1)S(1)}, bf16[256,256]{1,0:T(8,128)(2,1)S(1)}, u32[]{:S(2)}, u32[]{:S(2)}) collective-permute-start(bf16[256,256]{1,0:T(8,128)(2,1)S(1)} %add_add_fusion.1), channel_id=1, source_target_pairs={{0,64},{1,65},{2,66},{3,67},{4,68},{5,69},{6,70},{7,71},{8,72},{9,... | collective-permute-start | bytes 393224 | tf_op jit(solution)/shard_map/ppermute | solution.py:290
  41.6 15.8 %collective-permute-start.16 = (bf16[256,256]{1,0:T(8,128)(2,1)S(1)}, bf16[256,256]{1,0:T(8,128)(2,1)S(1)}, u32[]{:S(2)}, u32[]{:S(2)}) collective-permute-start(bf16[256,256]{1,0:T(8,128)(2,1)S(1)} %add_add_fusion.1), channel_id=1, source_target_pairs={{0,32},{1,33},{2,34},{3,35},{4,36},{5,37},{6,38},{7,39},{8,40},{9,... | collective-permute-start | bytes 393224 | tf_op jit(solution)/shard_map/ppermute | solution.py:290
  57.5 25.0 %collective-permute-start.21 = (bf16[8,128,512]{2,1,0:T(8,128)(2,1)S(1)}, bf16[8,128,512]{2,1,0:T(8,128)(2,1)S(1)}, u32[]{:S(2)}, u32[]{:S(2)}) collective-permute-start(bf16[8,128,512]{2,1,0:T(8,128)(2,1)S(1)} %pad_maximum_fusion.3), channel_id=1, source_target_pairs={{0,16},{1,17},{2,18},{3,19},{4,20},{5,21},{6,22},{7,23},{8,24},{9,... | collective-permute-start | bytes 3145736 | tf_op jit(solution)/shard_map/ppermute | solution.py:251
  58.4 48.3 %collective-permute-start.20 = (bf16[8,128,512]{2,1,0:T(8,128)(2,1)S(1)}, bf16[8,128,512]{2,1,0:T(8,128)(2,1)}, u32[]{:S(2)}, u32[]{:S(2)}) collective-permute-start(bf16[8,128,512]{2,1,0:T(8,128)(2,1)S(1)} %pad_maximum_fusion.3), channel_id=1, source_target_pairs={{0,8},{1,9},{2,10},{3,11},{4,12},{5,13},{6,14},{7,15},{8,16},{9,17... | collective-permute-start | bytes 3145736 | tf_op jit(solution)/shard_map/ppermute | solution.py:251
  60.6 46.1 %collective-permute-start.19 = (bf16[8,128,512]{2,1,0:T(8,128)(2,1)S(1)}, bf16[8,128,512]{2,1,0:T(8,128)(2,1)}, u32[]{:S(2)}, u32[]{:S(2)}) collective-permute-start(bf16[8,128,512]{2,1,0:T(8,128)(2,1)S(1)} %pad_maximum_fusion.3), channel_id=1, source_target_pairs={{0,24},{1,25},{2,26},{3,27},{4,28},{5,29},{6,30},{7,31},{8,0},{9,1... | collective-permute-start | bytes 3145736 | tf_op jit(solution)/shard_map/ppermute | solution.py:251
  61.1 45.6 %collective-permute-start.24 = (bf16[8,128,512]{2,1,0:T(8,128)(2,1)S(1)}, bf16[8,128,512]{2,1,0:T(8,128)(2,1)}, u32[]{:S(2)}, u32[]{:S(2)}) collective-permute-start(bf16[8,128,512]{2,1,0:T(8,128)(2,1)S(1)} %pad_maximum_fusion.4), channel_id=1, source_target_pairs={{0,4},{1,5},{2,6},{3,7},{4,0},{5,1},{6,2},{7,3},{8,12},{9,13},{10,... | collective-permute-start | bytes 3145736 | tf_op jit(solution)/shard_map/ppermute | solution.py:251
  62.2 48.0 %collective-permute-start.23 = (bf16[8,128,512]{2,1,0:T(8,128)(2,1)S(1)}, bf16[8,128,512]{2,1,0:T(8,128)(2,1)}, u32[]{:S(2)}, u32[]{:S(2)}) collective-permute-start(bf16[8,128,512]{2,1,0:T(8,128)(2,1)S(1)} %pad_maximum_fusion.4), channel_id=1, source_target_pairs={{0,2},{1,3},{2,4},{3,5},{4,6},{5,7},{6,0},{7,1},{8,10},{9,11},{10,... | collective-permute-start | bytes 3145736 | tf_op jit(solution)/shard_map/ppermute | solution.py:251
  82.5 27.8 %collective-permute-start.22 = (bf16[8,128,512]{2,1,0:T(8,128)(2,1)S(1)}, bf16[8,128,512]{2,1,0:T(8,128)(2,1)}, u32[]{:S(2)}, u32[]{:S(2)}) collective-permute-start(bf16[8,128,512]{2,1,0:T(8,128)(2,1)S(1)} %pad_maximum_fusion.4), channel_id=1, source_target_pairs={{0,6},{1,7},{2,0},{3,1},{4,2},{5,3},{6,4},{7,5},{8,14},{9,15},{10,... | collective-permute-start | bytes 3145736 | tf_op jit(solution)/shard_map/ppermute | solution.py:251
  97.7 19.2 %copy-start.3 = (bf16[256,512]{1,0:T(8,128)(2,1)S(1)}, bf16[256,512]{1,0:T(8,128)(2,1)}, u32[]{:S(2)}) copy-start(bf16[256,512]{1,0:T(8,128)(2,1)} %param.6) | copy-start | bytes 786436
  110.3 127.5 %all-to-all-start = ((bf16[32,240,512]{2,1,0:T(8,128)(2,1)}), bf16[32,240,512]{2,1,0:T(8,128)(2,1)}, u32[]{:S(2)}, u32[]{:S(2)}) async-start(bf16[32,240,512]{2,1,0:T(8,128)(2,1)} %pack.1), calls=%async_computation | async-start | bytes 15728640 | tf_op jit(solution)/shard_map/all_to_all | solution.py:328
  117.9 8.9 %collective-permute-start.25 = (bf16[256,640]{1,0:T(8,128)(2,1)S(1)}, bf16[256,640]{1,0:T(8,128)(2,1)S(1)}, u32[]{:S(2)}, u32[]{:S(2)}) collective-permute-start(bf16[256,640]{1,0:T(8,128)(2,1)S(1)} %constant_dynamic-update-slice_fusion), channel_id=1, source_target_pairs={{0,32},{1,33},{2,34},{3,35},{4,36},{5,37},{6,38},{7,39},{8,40},{9,... | collective-permute-start | bytes 983048 | tf_op jit(solution)/shard_map/ppermute | solution.py:256
  126.7 1.2 collective-permute-start.27
  126.9 99.1 %collective-permute-start.26 = (bf16[2,256,640]{2,1,0:T(8,128)(2,1)S(1)}, bf16[2,256,640]{2,1,0:T(8,128)(2,1)S(1)}, u32[]{:S(2)}, u32[]{:S(2)}) collective-permute-start(bf16[2,256,640]{2,1,0:T(8,128)(2,1)S(1)} %pad_maximum_fusion.5), channel_id=1, source_target_pairs={{0,64},{1,65},{2,66},{3,67},{4,68},{5,69},{6,70},{7,71},{8,72},{9,... | collective-permute-start | bytes 1966088 | tf_op jit(solution)/shard_map/ppermute | solution.py:260
  127.9 98.0 %collective-permute-start.28 = (f32[4,256]{1,0:T(4,128)S(1)}, f32[4,256]{1,0:T(4,128)S(1)}, u32[]{:S(2)}, u32[]{:S(2)}) collective-permute-start(f32[4,256]{1,0:T(4,128)S(1)} %fusion), channel_id=1, source_target_pairs={{0,64},{1,65},{2,66},{3,67},{4,68},{5,69},{6,70},{7,71},{8,72},{9,... | collective-permute-start | bytes 12296 | tf_op jit(solution)/shard_map/ppermute | solution.py:351
  237.7 54.8 %all-to-all-start.1 = ((bf16[32,240,256]{2,1,0:T(8,128)(2,1)}), bf16[32,240,256]{2,1,0:T(8,128)(2,1)}, u32[]{:S(2)}, u32[]{:S(2)}) async-start(bf16[32,240,256]{2,1,0:T(8,128)(2,1)} %copy-done.2), calls=%async_computation.1 | async-start | bytes 7864320 | tf_op jit(solution)/shard_map/all_to_all | solution.py:353
  (6 other events, 48.1 us)
